TPU v7x, 32 devices: a whole 2x2x4 slice. The times are simulated.
32 devices in a mesh: dp: 8 (over z, y), blk: 4 (over x, core).
Axes of the slice: x: 2, y: 2, z: 4, core: 2. Of those that a mesh axis runs over, the one named last changes fastest.
Arguments:
- inputs: bfloat16 [32, 1024, 768], P('dp', 'blk'), may hold values from -6 to 6
- lengths: int32 [32], P('dp'), may hold values from 512 to 1024, as said below
- out_grad: bfloat16 [32, 1024, 768], P('dp', 'blk'), may hold values from -6 to 6
- ln1_gain: bfloat16 [768], replicated, may hold values from 0.5 to 1.5
- ln1_bias: bfloat16 [768], replicated, may hold values from -1 to 1
- w_query: bfloat16 [768, 768], replicated, may hold values from -0.3125 to 0.3125
- b_query: bfloat16 [768], replicated, may hold values from -1 to 1
- w_key: bfloat16 [768, 768], replicated, may hold values from -0.3125 to 0.3125
- w_value: bfloat16 [768, 768], replicated, may hold values from -0.21875 to 0.21875
- b_value: bfloat16 [768], replicated, may hold values from -1 to 1
- w_output: bfloat16 [768, 768], replicated, may hold values from -0.875 to 0.875
- b_output: bfloat16 [768], replicated, may hold values from -1 to 1
- ln2_gain: bfloat16 [768], replicated, may hold values from 0.5 to 1.5
- ln2_bias: bfloat16 [768], replicated, may hold values from -1 to 1
- w_in: bfloat16 [768, 3072], replicated, may hold values from -0.21875 to 0.21875
- b_in: bfloat16 [3072], replicated, may hold values from -1 to 1
- w_out: bfloat16 [3072, 768], replicated, may hold values from -0.109375 to 0.109375
- b_out: bfloat16 [768], replicated, may hold values from -1 to 1
Outputs:
- output: bfloat16 [32, 1024, 768], P('dp', 'blk')
- input_grad: bfloat16 [32, 1024, 768], P('dp', 'blk')
- ln1_gain_grad: float32 [768], P(('dp', 'blk'))
- ln1_bias_grad: float32 [768], P(('dp', 'blk'))
- w_query_grad: float32 [768, 768], P(('dp', 'blk'))
- b_query_grad: float32 [768], P(('dp', 'blk'))
- w_key_grad: float32 [768, 768], P(('dp', 'blk'))
- w_value_grad: float32 [768, 768], P(('dp', 'blk'))
- b_value_grad: float32 [768], P(('dp', 'blk'))
- w_output_grad: float32 [768, 768], P(('dp', 'blk'))
- b_output_grad: float32 [768], P(('dp', 'blk'))
- ln2_gain_grad: float32 [768], P(('dp', 'blk'))
- ln2_bias_grad: float32 [768], P(('dp', 'blk'))
- w_in_grad: float32 [768, 3072], P(('dp', 'blk'))
- b_in_grad: float32 [3072], P(('dp', 'blk'))
- w_out_grad: float32 [3072, 768], P(('dp', 'blk'))
- b_out_grad: float32 [768], P(('dp', 'blk'))
Inputs may be any that keep to these rules, and one draw needn't show every extreme that they name: `lengths`: every length is 512 or 1024; among the 4 sequences of one index of dp at least one has length 1024.
All inputs are finite; a program needn't handle non-finite values.
Results may differ from a plain program's by a relative error of at most 0.02.
Values may be sent and summed in bfloat16 or wider, within the bound.
A program may use at most 256 MiB of HBM per device.

v0:
```python
import math

import jax
import jax.numpy as jnp
from jax import lax
from jax.sharding import PartitionSpec as P

H = 12


epsilon = 1e-05


def layer_norm(values, gains, shifts):
    average = jnp.mean(values, axis=-1, keepdims=True)
    centred = values - average
    variance = jnp.mean(centred * centred, axis=-1, keepdims=True)
    return centred * lax.rsqrt(variance + epsilon) * gains + shifts


def smooth_gate(values):
    return jax.nn.gelu(values, approximate=False)


def contract_rows(left, right):
    return lax.dot_general(
        left, right, (((0,), (0,)), ((), ())), preferred_element_type=jnp.float32
    )


def times_transposed(left, right):
    return lax.dot_general(
        left, right, (((1,), (1,)), ((), ())), preferred_element_type=jnp.float32
    )


def column_sums(values):
    return jnp.sum(values, axis=0, dtype=jnp.float32)


def body(
    inputs,
    lengths,
    out_grad,
    ln1_gain,
    ln1_bias,
    w_query,
    b_query,
    w_key,
    w_value,
    b_value,
    w_output,
    b_output,
    ln2_gain,
    ln2_bias,
    w_in,
    b_in,
    w_out,
    b_out,
):
    seq_count, blk_tok, model_width = inputs.shape
    row_count = seq_count * blk_tok
    head_size = model_width // H
    score_scale = head_size ** (-0.5)
    full_len = blk_tok * lax.axis_size("blk")
    key_block = math.gcd(full_len, 512)
    block_count = full_len // key_block
    flat_inputs = inputs.astype(jnp.float32).reshape(row_count, model_width)
    normed_f, ln_one_back = jax.vjp(
        layer_norm, flat_inputs, ln1_gain.astype(jnp.float32), ln1_bias.astype(jnp.float32)
    )
    normed_one = normed_f.astype(jnp.bfloat16)
    queries = (
        jnp.dot(normed_one, w_query, preferred_element_type=jnp.float32)
        + b_query.astype(jnp.float32)
    ).astype(jnp.bfloat16)
    keys_local = (
        jnp.dot(normed_one, w_key, preferred_element_type=jnp.float32)
        .astype(jnp.bfloat16)
        .reshape(seq_count, blk_tok, model_width)
    )
    values_local = (
        (
            jnp.dot(normed_one, w_value, preferred_element_type=jnp.float32)
            + b_value.astype(jnp.float32)
        )
        .astype(jnp.bfloat16)
        .reshape(seq_count, blk_tok, model_width)
    )
    query_heads = queries.reshape(seq_count, blk_tok, H, head_size)

    def key_validity(offset, key_count):
        positions = offset + jnp.arange(key_count, dtype=jnp.int32)
        return (positions[None, :] < lengths[:, None])[:, None, None, :]

    absorb_row_max = jnp.full((seq_count, H, blk_tok), -1e30, jnp.float32)
    key_piece = lax.all_gather(keys_local, "blk", axis=1, tiled=True)
    value_piece = lax.all_gather(values_local, "blk", axis=1, tiled=True)
    key_count = key_piece.shape[1]
    key_heads = key_piece.reshape(seq_count, key_count, H, head_size)
    value_heads = value_piece.reshape(seq_count, key_count, H, head_size)
    scores = (
        jnp.einsum("sqhd,skhd->shqk", query_heads, key_heads, preferred_element_type=jnp.float32)
        * score_scale
    )
    key_mask = key_validity(jnp.int32(0), key_count)
    masked = jnp.where(key_mask, scores, -1e30)
    new_max = jnp.maximum(absorb_row_max, jnp.max(masked, axis=-1))
    weights = jnp.where(key_mask, jnp.exp(masked - new_max[..., None]), 0.0)
    absorb_row_total = jnp.sum(weights, axis=-1)
    summed = jnp.einsum(
        "shqk,skhd->sqhd",
        weights.astype(jnp.bfloat16),
        value_heads,
        preferred_element_type=jnp.float32,
    )
    row_max, row_total, summed = (new_max, absorb_row_total, summed)
    context_f = summed / jnp.transpose(row_total, (0, 2, 1))[..., None]
    context_b = context_f.astype(jnp.bfloat16).reshape(row_count, model_width)
    middle = (
        flat_inputs
        + jnp.dot(context_b, w_output, preferred_element_type=jnp.float32)
        + b_output.astype(jnp.float32)
    )
    normed_two_f, ln_two_back = jax.vjp(
        layer_norm, middle, ln2_gain.astype(jnp.float32), ln2_bias.astype(jnp.float32)
    )
    normed_two = normed_two_f.astype(jnp.bfloat16)
    pre_gate = jnp.dot(normed_two, w_in, preferred_element_type=jnp.float32) + b_in.astype(
        jnp.float32
    )
    activated_f, gate_back = jax.vjp(smooth_gate, pre_gate)
    activated = activated_f.astype(jnp.bfloat16)
    result = (
        middle
        + jnp.dot(activated, w_out, preferred_element_type=jnp.float32)
        + b_out.astype(jnp.float32)
    )
    output = result.astype(jnp.bfloat16).reshape(seq_count, blk_tok, model_width)
    grad_rows = out_grad.reshape(row_count, model_width)
    grad_float = grad_rows.astype(jnp.float32)
    b_out_grad = jnp.sum(grad_float, axis=0)
    w_out_grad = contract_rows(activated, grad_rows)
    (d_pre,) = gate_back(times_transposed(grad_rows, w_out))
    d_pre_b = d_pre.astype(jnp.bfloat16)
    b_in_grad = column_sums(d_pre_b)
    w_in_grad = contract_rows(normed_two, d_pre_b)
    d_middle_norm, ln2_gain_grad, ln2_bias_grad = ln_two_back(times_transposed(d_pre_b, w_in))
    d_middle = grad_float + d_middle_norm
    d_branch = d_middle.astype(jnp.bfloat16)
    b_output_grad = column_sums(d_branch)
    w_output_grad = contract_rows(context_b, d_branch)
    d_context = (
        times_transposed(d_branch, w_output)
        .astype(jnp.bfloat16)
        .reshape(seq_count, blk_tok, H, head_size)
    )
    row_delta = jnp.transpose(
        jnp.sum(d_context.astype(jnp.float32) * context_f, axis=-1), (0, 2, 1)
    )
    keys_back, values_back = (
        lax.all_gather(keys_local, "blk", axis=1, tiled=True),
        lax.all_gather(values_local, "blk", axis=1, tiled=True),
    )
    dq_start = jnp.zeros((seq_count, blk_tok, H, head_size), jnp.float32)

    def backward_block(dq_sum, step_index):
        offset = step_index * key_block
        key_heads = lax.dynamic_slice_in_dim(keys_back, offset, key_block, 1).reshape(
            seq_count, key_block, H, head_size
        )
        value_heads = lax.dynamic_slice_in_dim(values_back, offset, key_block, 1).reshape(
            seq_count, key_block, H, head_size
        )
        scores = (
            jnp.einsum(
                "sqhd,skhd->shqk", query_heads, key_heads, preferred_element_type=jnp.float32
            )
            * score_scale
        )
        key_mask = key_validity(offset, key_block)
        probabilities = jnp.where(
            key_mask, jnp.exp(scores - row_max[..., None]) / row_total[..., None], 0.0
        )
        d_values = jnp.einsum(
            "shqk,sqhd->kshd",
            probabilities.astype(jnp.bfloat16),
            d_context,
            preferred_element_type=jnp.float32,
        )
        d_probs = jnp.einsum(
            "sqhd,skhd->shqk", d_context, value_heads, preferred_element_type=jnp.float32
        )
        d_scores = (probabilities * (d_probs - row_delta[..., None])).astype(jnp.bfloat16)
        dq_sum = (
            dq_sum
            + jnp.einsum("shqk,skhd->sqhd", d_scores, key_heads, preferred_element_type=jnp.float32)
            * score_scale
        )
        d_keys = (
            jnp.einsum("shqk,sqhd->kshd", d_scores, query_heads, preferred_element_type=jnp.float32)
            * score_scale
        )
        joined = jnp.concatenate(
            [
                d_keys.reshape(key_block, seq_count, model_width),
                d_values.reshape(key_block, seq_count, model_width),
            ],
            axis=-1,
        )
        return (dq_sum, joined)

    dq_sum, key_terms = lax.scan(backward_block, dq_start, jnp.arange(block_count, dtype=jnp.int32))
    key_terms = key_terms.reshape(full_len, seq_count, 2 * model_width)
    own_terms = lax.psum_scatter(
        key_terms.astype(jnp.bfloat16), "blk", scatter_dimension=0, tiled=True
    ).astype(jnp.float32)
    own_terms = jnp.transpose(own_terms, (1, 0, 2)).reshape(row_count, 2 * model_width)
    d_key_b = own_terms[:, :model_width].astype(jnp.bfloat16)
    d_value_b = own_terms[:, model_width:].astype(jnp.bfloat16)
    d_query_b = dq_sum.reshape(row_count, model_width).astype(jnp.bfloat16)
    b_query_grad = column_sums(d_query_b)
    b_value_grad = column_sums(d_value_b)
    w_query_grad = contract_rows(normed_one, d_query_b)
    w_key_grad = contract_rows(normed_one, d_key_b)
    w_value_grad = contract_rows(normed_one, d_value_b)
    d_normed = (
        times_transposed(d_query_b, w_query)
        + times_transposed(d_key_b, w_key)
        + times_transposed(d_value_b, w_value)
    )
    d_input_norm, ln1_gain_grad, ln1_bias_grad = ln_one_back(d_normed)
    input_grad = (
        (d_middle + d_input_norm).astype(jnp.bfloat16).reshape(seq_count, blk_tok, model_width)
    )
    grad_list = (
        ln1_gain_grad,
        ln1_bias_grad,
        w_query_grad,
        b_query_grad,
        w_key_grad,
        w_value_grad,
        b_value_grad,
        w_output_grad,
        b_output_grad,
        ln2_gain_grad,
        ln2_bias_grad,
        w_in_grad,
        b_in_grad,
        w_out_grad,
        b_out_grad,
    )
    summed_grads = (
        lax.psum_scatter(grad_list[0], ("dp", "blk"), scatter_dimension=0, tiled=True),
        lax.psum_scatter(grad_list[1], ("dp", "blk"), scatter_dimension=0, tiled=True),
        lax.psum_scatter(grad_list[2], ("dp", "blk"), scatter_dimension=0, tiled=True),
        lax.psum_scatter(grad_list[3], ("dp", "blk"), scatter_dimension=0, tiled=True),
        lax.psum_scatter(grad_list[4], ("dp", "blk"), scatter_dimension=0, tiled=True),
        lax.psum_scatter(grad_list[5], ("dp", "blk"), scatter_dimension=0, tiled=True),
        lax.psum_scatter(grad_list[6], ("dp", "blk"), scatter_dimension=0, tiled=True),
        lax.psum_scatter(grad_list[7], ("dp", "blk"), scatter_dimension=0, tiled=True),
        lax.psum_scatter(grad_list[8], ("dp", "blk"), scatter_dimension=0, tiled=True),
        lax.psum_scatter(grad_list[9], ("dp", "blk"), scatter_dimension=0, tiled=True),
        lax.psum_scatter(grad_list[10], ("dp", "blk"), scatter_dimension=0, tiled=True),
        lax.psum_scatter(grad_list[11], ("dp", "blk"), scatter_dimension=0, tiled=True),
        lax.psum_scatter(grad_list[12], ("dp", "blk"), scatter_dimension=0, tiled=True),
        lax.psum_scatter(grad_list[13], ("dp", "blk"), scatter_dimension=0, tiled=True),
        lax.psum_scatter(grad_list[14], ("dp", "blk"), scatter_dimension=0, tiled=True),
    )
    return (
        output,
        input_grad,
        summed_grads[0],
        summed_grads[1],
        summed_grads[2],
        summed_grads[3],
        summed_grads[4],
        summed_grads[5],
        summed_grads[6],
        summed_grads[7],
        summed_grads[8],
        summed_grads[9],
        summed_grads[10],
        summed_grads[11],
        summed_grads[12],
        summed_grads[13],
        summed_grads[14],
    )


def solution(mesh):
    in_specs = (
        P("dp", "blk", None),
        P("dp"),
        P("dp", "blk", None),
        P(),
        P(),
        P(),
        P(),
        P(),
        P(),
        P(),
        P(),
        P(),
        P(),
        P(),
        P(),
        P(),
        P(),
        P(),
    )
    out_specs = (
        P("dp", "blk", None),
        P("dp", "blk", None),
        P(("dp", "blk")),
        P(("dp", "blk")),
        P(("dp", "blk"), None),
        P(("dp", "blk")),
        P(("dp", "blk"), None),
        P(("dp", "blk"), None),
        P(("dp", "blk")),
        P(("dp", "blk"), None),
        P(("dp", "blk")),
        P(("dp", "blk")),
        P(("dp", "blk")),
        P(("dp", "blk"), None),
        P(("dp", "blk")),
        P(("dp", "blk"), None),
        P(("dp", "blk")),
    )
    return jax.shard_map(body, mesh=mesh, in_specs=in_specs, out_specs=out_specs, check_vma=False)
```

profile of v0, /device:TPU:0, one launch (start us, length us, event | category | flops | bytes accessed | tf_op | source)
XLA Modules:
  0.0 1206.4 jit_solution(9834537358340709552)
XLA Ops:
  40.9 28.8 %all-gather.5.cloned.1.call-done = bf16[4,1024,768]{1,2,0:T(8,128)(2,1)} async-done(((bf16[4,256,768]{1,2,0:T(8,128)(2,1)}), bf16[4,1024,768]{1,2,0:T(8,128)(2,1)}) %all-gather.5.cloned.1.call-update) | async-done | bytes 6291472 | tf_op jit(solution)/shard_map/all_gather | solution.py:97
  69.7 22.8 %fusion.2 = (f32[4,12,256]{2,1,0:T(8,128)S(1)}, f32[4,12,256,1024]{3,2,1,0:T(8,128)}) fusion(pred[4,1024]{1,0:T(4,128)(4,1)S(1)} %iota_compare_fusion, bf16[4,1024,12,64]{1,3,2,0:T(8,128)(2,1)} %bitcast.159, bf16[4,256,12,64]{1,0,3,2:T(4,128)(2,1)} %reshape.252), kind=kOutput, calls=%fused_computation.14 | convolution fusion | flops 1648349184 | bytes 58249216 | tf_op jit(solution)/shard_map/sqhd,skhd->shqk/dot_general | solution.py:103
  92.6 22.1 %fusion.3 = f32[4,12,256]{2,1,0:T(8,128)S(1)} fusion(f32[4,12,256,1024]{3,2,1,0:T(8,128)} %get-tuple-element.212, f32[4,12,256]{2,1,0:T(8,128)S(1)} %broadcast_maximum_fusion, pred[4,1024]{1,0:T(4,128)(4,1)S(1)} %iota_compare_fusion), kind=kLoop, calls=%fused_computation.15 | loop fusion | flops 62902272 | bytes 50434048 | tf_op jit(solution)/shard_map/reduce_sum | solution.py:110
  118.5 22.3 %fusion.56 = (bf16[4,256,12,64]{1,3,2,0:T(8,128)(2,1)S(1)}, f32[4,256,12,64]{1,3,2,0:T(8,128)}) fusion(f32[4,256,12]{1,2,0:T(8,128)S(1)} %bitcast.184, bf16[4,1024,12,64]{1,3,2,0:T(8,128)(2,1)} %bitcast.160, f32[4,12,256,1024]{3,2,1,0:T(8,128)} %get-tuple-element.212, f32[4,12,256]{2,1,0:T(8,128)S(1)} %broadcast_maximum_fusion, ...), kind=kOutput, calls=%fused_computation.109 | convolution fusion | flops 1675100160 | bytes 61444096 | tf_op jit(solution)/shard_map/shqk,skhd->sqhd/dot_general | solution.py:111
  145.9 35.6 %multiply_convert_fusion.1 = (bf16[1024,3072]{1,0:T(8,128)(2,1)}, f32[1024,3072]{1,0:T(8,128)}, f32[1024,3072]{1,0:T(8,128)}) fusion(f32[3072]{0:T(1024)S(1)} %convert_element_type.134, bf16[768,3072]{1,0:T(8,128)(2,1)S(1)} %bitcast.188, f32[1024,768]{1,0:T(8,128)S(1)} %get-tuple-element.216, f32[768]{0:T(1024)S(1)} %convert_element_type.132, ...), kind=kOutput, calls=%fused_computation.23 | convolution fusion | flops 5043388416 | bytes 39348224 | tf_op jit(solution)/shard_map/dot_general | solution.py:129
  181.5 17.4 %convert_reduce_fusion = (f32[3072]{0:T(1024)}, bf16[1024,3072]{1,0:T(8,128)(2,1)}) fusion(f32[1024,3072]{1,0:T(8,128)} %get-tuple-element.204, bf16[1024,768]{1,0:T(8,128)(2,1)S(1)} %bitcast.162, bf16[3072,768]{1,0:T(8,128)(2,1)} %param.36, f32[1024,3072]{1,0:T(8,128)} %get-tuple-element.217, f32[3072]{0:T(1024)S(1)} %convert_element_type.134), kind=kOutput, calls=%fused_computation.21 | convolution fusion | flops 4885312512 | bytes 37773312 | tf_op jit(solution)/shard_map/dot_general | solution.py:32
  224.2 175.1 %while.13 = (s32[]{:T(128)}, f32[4,256,12,64]{1,3,2,0:T(8,128)}, bf16[2,512,4,1536]{3,1,0,2:T(8,128)(2,1)}, s32[2]{0:T(128)S(1)}, bf16[4,1024,768]{1,2,0:T(8,128...) while((s32[]{:T(128)}, f32[4,256,12,64]{1,3,2,0:T(8,128)}, ...), condition=%wide.region_10.11_spmd.clone, body=%wide.region_9.10_spmd.clone.sunk | while | flops 4094953984 | bytes 210919728 | solution.py:213
  232.4 10.7 divide_select_fusion.2
  243.1 11.9 fusion.124
  255.0 16.0 %multiply_convert_fusion.3 = bf16[4,12,512,256]{3,2,1,0:T(8,128)(2,1)} fusion(f32[4,12,512,256]{3,2,1,0:T(8,128)} %divide_select_fusion.2, f32[4,12,256]{2,1,0:T(8,128)S(1)} %get-tuple-element.342, bf16[4,512,12,64]{1,3,2,0:T(8,128)(2,1)} %bitcast.158, bf16[4,256,12,64]{1,3,2,0:T(8,128)(2,1)S(1)} %get-tuple-element.341), kind=kOutput, calls=%fused_computation.clone.1 | convolution fusion | flops 824180736 | bytes 42516480 | tf_op jit(solution)/shard_map/while/body/eval_jaxpr/sqhd,skhd->shqk/dot_general | solution.py:191
  280.3 10.7 broadcast_multiply_fusion.4
  330.2 11.9 fusion.124
  342.1 16.0 %multiply_convert_fusion.3 = bf16[4,12,512,256]{3,2,1,0:T(8,128)(2,1)} fusion(f32[4,12,512,256]{3,2,1,0:T(8,128)} %divide_select_fusion.2, f32[4,12,256]{2,1,0:T(8,128)S(1)} %get-tuple-element.342, bf16[4,512,12,64]{1,3,2,0:T(8,128)(2,1)} %bitcast.158, bf16[4,256,12,64]{1,3,2,0:T(8,128)(2,1)S(1)} %get-tuple-element.341), kind=kOutput, calls=%fused_computation.clone.1 | convolution fusion | flops 824180736 | bytes 42516480 | tf_op jit(solution)/shard_map/while/body/eval_jaxpr/sqhd,skhd->shqk/dot_general | solution.py:191
  368.3 10.7 broadcast_multiply_fusion.4
  412.9 11.1 fusion.61
  424.7 11.2 fusion.50
  436.2 62.3 %reduce-scatter.8.cloned.1.call-done = bf16[256,4,1536]{2,0,1:T(8,128)(2,1)} async-done(((bf16[1024,4,1536]{2,0,1:T(8,128)(2,1)}), bf16[256,4,1536]{2,0,1:T(8,128)(2,1)}) %reduce-scatter.8.cloned.1.call-update) | async-done | bytes 3145744 | tf_op jit(solution)/shard_map/reduce_scatter | solution.py:215
  528.4 40.4 %all-reduce.9 = (f32[768]{0:T(1024)S(1)}, f32[768]{0:T(1024)S(1)}, f32[768]{0:T(1024)S(1)}, f32[768]{0:T(1024)S(1)}, f32[768]{0:T(1024)S(1)}, /*index=5*/f32[768...) all-reduce(f32[768]{0:T(1024)S(1)} %get-tuple-element.159, ...), channel_id=3, replica_groups=mesh['dp'=8,'blk'=4] {'dp','blk'}, use_global_device_ids=true, to_apply=%region_15.16.clone | all-reduce | flops 9216 | bytes 73728
  579.0 24.3 %reduce-scatter.16.cloned.1.call-done = f32[24,768]{1,0:T(8,128)} async-done(((f32[768,768]{1,0:T(8,128)}), f32[24,768]{1,0:T(8,128)}) %reduce-scatter.16.cloned.1.call-update) | async-done | bytes 73744 | tf_op jit(solution)/shard_map/reduce_scatter | solution.py:261
  603.3 104.7 %reduce-scatter.10.cloned.1.call-done = f32[24,768]{1,0:T(8,128)} async-done(((f32[768,768]{1,0:T(8,128)}), f32[24,768]{1,0:T(8,128)}) %reduce-scatter.10.cloned.1.call-update) | async-done | bytes 73744 | tf_op jit(solution)/shard_map/reduce_scatter | solution.py:256
  708.0 140.9 %reduce-scatter.20.cloned.1.call-done = f32[96,768]{1,0:T(8,128)} async-done(((f32[3072,768]{1,0:T(8,128)}), f32[96,768]{1,0:T(8,128)}) %reduce-scatter.20.cloned.1.call-update) | async-done | bytes 294928 | tf_op jit(solution)/shard_map/reduce_scatter | solution.py:267
  848.9 142.0 %reduce-scatter.18.cloned.1.call-done = f32[24,3072]{1,0:T(8,128)} async-done(((f32[768,3072]{1,0:T(8,128)}), f32[24,3072]{1,0:T(8,128)}) %reduce-scatter.18.cloned.1.call-update) | async-done | bytes 294928 | tf_op jit(solution)/shard_map/reduce_scatter | solution.py:265
  990.9 103.7 %reduce-scatter.14.cloned.1.call-done = f32[24,768]{1,0:T(8,128)} async-done(((f32[768,768]{1,0:T(8,128)}), f32[24,768]{1,0:T(8,128)}) %reduce-scatter.14.cloned.1.call-update) | async-done | bytes 73744 | tf_op jit(solution)/shard_map/reduce_scatter | solution.py:259
  1094.6 104.8 %reduce-scatter.12.cloned.1.call-done = f32[24,768]{1,0:T(8,128)} async-done(((f32[768,768]{1,0:T(8,128)}), f32[24,768]{1,0:T(8,128)}) %reduce-scatter.12.cloned.1.call-update) | async-done | bytes 73744 | tf_op jit(solution)/shard_map/reduce_scatter | solution.py:258
  (243 shorter events, 207.5 us)
Async XLA Ops:
  7.2 12.6 %copy-start = (bf16[768,768]{1,0:T(8,128)(2,1)S(1)}, bf16[768,768]{1,0:T(8,128)(2,1)}, u32[]{:S(2)}) copy-start(bf16[768,768]{1,0:T(8,128)(2,1)} %param.28) | copy-start | bytes 3538948
  7.2 62.5 %all-gather.5.cloned.1.call-start = ((), (), s32[]{:S(2)}) async-start(), calls=%async_computation.8 | async-start | bytes 7864320 | tf_op jit(solution)/shard_map/all_gather | solution.py:97
  19.7 98.9 %all-gather.3.cloned.1.call-start = ((), (), s32[]{:S(2)}) async-start(), calls=%async_computation.7 | async-start | bytes 7864320 | tf_op jit(solution)/shard_map/all_gather | solution.py:98
  26.4 472.1 %reduce-scatter.8.cloned.1.call-start = ((), (), s32[]{:S(2)}) async-start(), calls=%async_computation.9 | async-start | bytes 15728640 | tf_op jit(solution)/shard_map/reduce_scatter | solution.py:215
  26.5 182.2 %copy-start.28 = (f32[768]{0:T(1024)}, f32[768]{0:T(1024)S(1)}, u32[]{:S(2)}) copy-start(f32[768]{0:T(1024)S(1)} %convert_element_type.131) | copy-start | bytes 9220
  26.5 118.2 %copy-start.34 = (f32[768]{0:T(1024)}, f32[768]{0:T(1024)S(1)}, u32[]{:S(2)}) copy-start(f32[768]{0:T(1024)S(1)} %convert_element_type.132) | copy-start | bytes 9220
  34.0 6.9 copy-start.44
  92.6 26.0 %copy-start.22 = (f32[4,12,256]{2,1,0:T(8,128)}, f32[4,12,256]{2,1,0:T(8,128)S(1)}, u32[]{:S(2)}) copy-start(f32[4,12,256]{2,1,0:T(8,128)S(1)} %broadcast_maximum_fusion) | copy-start | bytes 147460
  114.7 26.2 %copy-start.30 = (f32[4,12,256]{2,1,0:T(8,128)}, f32[4,12,256]{2,1,0:T(8,128)S(1)}, u32[]{:S(2)}) copy-start(f32[4,12,256]{2,1,0:T(8,128)S(1)} %fusion.3) | copy-start | bytes 147460
  144.2 64.5 %copy-start.6 = (f32[1024,768]{1,0:T(8,128)}, f32[1024,768]{1,0:T(8,128)S(1)}, u32[]{:S(2)}) copy-start(f32[1024,768]{1,0:T(8,128)S(1)} %get-tuple-element.216) | copy-start | bytes 9437188
  144.2 64.5 %copy-start.18 = (f32[1024]{0:T(1024)}, f32[1024]{0:T(1024)S(1)}, u32[]{:S(2)}) copy-start(f32[1024]{0:T(1024)S(1)} %broadcast_multiply_fusion.1) | copy-start | bytes 12292
  145.9 62.8 %copy-start.20 = (f32[1024]{0:T(1024)}, f32[1024]{0:T(1024)S(1)}, u32[]{:S(2)}) copy-start(f32[1024]{0:T(1024)S(1)} %fusion.40) | copy-start | bytes 12292
  145.9 35.6 %copy-start.9 = (bf16[4,256,768]{2,1,0:T(8,128)(2,1)S(1)}, bf16[4,256,768]{2,1,0:T(8,128)(2,1)}, u32[]{:S(2)}) copy-start(bf16[4,256,768]{2,1,0:T(8,128)(2,1)} %param.22) | copy-start | bytes 4718596
  225.5 6.9 copy-start.2
  312.6 6.9 copy-start.2
  399.4 204.0 %reduce-scatter.16.cloned.1.call-start = ((), (), s32[]{:S(2)}) async-start(), calls=%async_computation.13 | async-start | bytes 2433024 | tf_op jit(solution)/shard_map/reduce_scatter | solution.py:261
  404.6 303.4 %reduce-scatter.10.cloned.1.call-start = ((), (), s32[]{:S(2)}) async-start(), calls=%async_computation.10 | async-start | bytes 2433024 | tf_op jit(solution)/shard_map/reduce_scatter | solution.py:256
  412.8 436.1 %reduce-scatter.20.cloned.1.call-start = ((), (), s32[]{:S(2)}) async-start(), calls=%async_computation.15 | async-start | bytes 9732096 | tf_op jit(solution)/shard_map/reduce_scatter | solution.py:267
  424.0 566.9 %reduce-scatter.18.cloned.1.call-start = ((), (), s32[]{:S(2)}) async-start(), calls=%async_computation.14 | async-start | bytes 9732096 | tf_op jit(solution)/shard_map/reduce_scatter | solution.py:265
  435.9 658.7 %reduce-scatter.14.cloned.1.call-start = ((), (), s32[]{:S(2)}) async-start(), calls=%async_computation.12 | async-start | bytes 2433024 | tf_op jit(solution)/shard_map/reduce_scatter | solution.py:259
  503.3 696.1 %reduce-scatter.12.cloned.1.call-start = ((), (), s32[]{:S(2)}) async-start(), calls=%async_computation.11 | async-start | bytes 2433024 | tf_op jit(solution)/shard_map/reduce_scatter | solution.py:258
  505.1 10.0 copy-start.11
  505.2 10.0 copy-start.14
  525.1 49.0 %copy-start.39 = (f32[1024]{0:T(1024)S(1)}, f32[1024]{0:T(1024)}, u32[]{:S(2)}) copy-start(f32[1024]{0:T(1024)} %copy-done.38) | copy-start | bytes 12292
  (51 other events, 152.7 us)
Sparse Core Ops, SparseCore 0:
  19.8 49.8 all-gather.4
  71.3 47.2 all-gather.2
  399.4 99.0 reduce-scatter.7
  504.2 99.0 reduce-scatter.15
  609.9 98.0 reduce-scatter.9
  714.3 134.5 reduce-scatter.19
  856.4 134.4 reduce-scatter.17
  996.8 97.8 reduce-scatter.13
  1101.4 98.0 reduce-scatter.11
where the time goes:
time: 1210 us
  waiting for transfers between devices  716 us (59%)
  matrix products  296 us (24%)
  local copies, waits for them, and re-layouts  81.8 us (7%)
  other arithmetic  55.8 us (5%)
  blocking collectives  40.4 us (3%)
  between operations  15.2 us (1%)
    reduce_scatter x1, waiting for transfers between devices, body(): lax.psum_scatter(grad_list[11], ('dp', 'blk'), scatter_dimension=0, tiled...  142 us
    reduce_scatter x1, waiting for transfers between devices, body(): lax.psum_scatter(grad_list[13], ('dp', 'blk'), scatter_dimension=0, tiled...  141 us
    reduce_scatter x1, waiting for transfers between devices, body(): lax.psum_scatter(grad_list[4], ('dp', 'blk'), scatter_dimension=0, tiled=...  105 us
    reduce_scatter x1, waiting for transfers between devices, body(): lax.psum_scatter(grad_list[2], ('dp', 'blk'), scatter_dimension=0, tiled=...  105 us
    reduce_scatter x1, waiting for transfers between devices, body(): lax.psum_scatter(grad_list[5], ('dp', 'blk'), scatter_dimension=0, tiled=...  104 us
    reduce_scatter x1, waiting for transfers between devices, body(): lax.psum_scatter(key_terms.astype(jnp.bfloat16), 'blk', scatter_dimension...  62.3 us
    unnamed x1, blocking collectives  40.4 us
    dot_general x6, matrix products, contract_rows(): lax.dot_general(left, right, (((0,), (0,)), ((), ())), preferred_element_...  37.8 us
  transfers between devices with their start and end apart: 9, of which 9 were waited for; matrix products, arithmetic and copies ran while one was open for 11% of the time, Pallas kernels for 0%

commit v1 on v0

v1 whole, which is shorter than its diff:
```python
import functools

import jax
import jax.numpy as jnp
from jax import lax
from jax.experimental import pallas as pl
from jax.experimental.pallas import tpu as pltpu
from jax.sharding import PartitionSpec as P

H = 12
EPS = 1e-05
LOG2E = 1.4426950408889634
LN2 = 0.6931471805599453
INV_SQRT_2PI = 0.3989422804014327
F32 = jnp.float32
BF16 = jnp.bfloat16
VMEM_LIMIT = 56 * 2**20

NN = (((1,), (0,)), ((), ()))
NT = (((1,), (1,)), ((), ()))
TN = (((0,), (0,)), ((), ()))

TAIL_P = 0.28
TAIL_C = (
    0.116425338,
    0.068098667,
    0.267402196,
    -0.235117072,
    0.388714046,
    -0.105523175,
)


def dot(left, right, dims=NN):
    return lax.dot_general(left, right, dims, preferred_element_type=F32)


def params(**kw):
    return pltpu.CompilerParams(vmem_limit_bytes=VMEM_LIMIT, **kw)


def full(shape):
    return pl.BlockSpec(shape, lambda *_: (0,) * len(shape))


def center(v):
    mean = jnp.mean(v, axis=-1, keepdims=True)
    cent = v - mean
    var = jnp.mean(cent * cent, axis=-1, keepdims=True)
    rstd = lax.rsqrt(var + EPS)
    return cent * rstd, rstd


def gate(u):
    a = jnp.abs(u)
    den = 1.0 + TAIL_P * a
    t = pl.reciprocal(den, approx=True)
    t = t * (2.0 - den * t)
    e = jnp.exp2(u * u * (-0.5 * LOG2E))
    poly = TAIL_C[-1]
    for c in TAIL_C[-2::-1]:
        poly = poly * t + c
    tail = poly * t * e
    phi = jnp.where(u < 0.0, tail, 1.0 - tail)
    return phi, u * e * INV_SQRT_2PI


def qkv_kernel(scale, n_blk, *refs):
    xs = refs[:n_blk]
    gain, bias, wq, bq, wk, wv, bv, nt_ref, q_ref, k_ref, v_ref = refs[n_blk:]
    tok = xs[0].shape[0]

    @pl.when(pl.program_id(0) == 0)
    def _():
        for s in range(n_blk):
            n, _ = center(xs[s][...].astype(F32))
            n = n * gain[...] + bias[...]
            nt_ref[:, s * tok : (s + 1) * tok] = n.astype(BF16).T

    nt = nt_ref[...]
    q_ref[...] = ((dot(wq[...], nt, TN) + bq[...]) * scale).astype(BF16)
    k_ref[...] = dot(wk[...], nt, TN).astype(BF16)
    v_ref[...] = (dot(wv[...], nt, TN) + bv[...]).astype(BF16)


def attend_kernel(n_blk, live_ref, q_ref, k_ref, v_ref, c_ref, p_ref, il_ref):
    seq = q_ref.shape[1]
    tok = seq // n_blk
    s = dot(k_ref[...].T, q_ref[...])
    live = [live_ref[0, i] > 0 for i in range(n_blk)]
    m = None
    for i in range(n_blk):
        mi = jnp.max(s[i * tok : (i + 1) * tok], axis=0, keepdims=True)
        mi = jnp.where(live[i], mi, -1e30)
        m = mi if m is None else jnp.maximum(m, mi)
    total = None
    ps = []
    for i in range(n_blk):
        p = jnp.exp2(s[i * tok : (i + 1) * tok] - jnp.where(live[i], m, 1e30))
        li = jnp.sum(p, axis=0, keepdims=True)
        total = li if total is None else total + li
        pb = p.astype(BF16)
        p_ref[0, i * tok : (i + 1) * tok] = pb
        ps.append(pb)
    inv = 1.0 / total
    c_ref[...] = (dot(v_ref[...], jnp.concatenate(ps, axis=0)) * inv).astype(BF16)
    il_ref[0] = inv


def ffn_kernel(n_blk, *refs):
    xs = refs[:n_blk]
    gs = refs[n_blk : 2 * n_blk]
    (ct_ref, il_ref, wo_ref, bo_ref, gain_ref, bias_ref, win_ref, bin_ref, wout_ref, bout_ref) = refs[
        2 * n_blk : 2 * n_blk + 10
    ]
    rest = refs[2 * n_blk + 10 :]
    outs = rest[:n_blk]
    (gwout_ref, gwin_ref, gbin_ref, dmid_ref, dot_ref, gwo_ref, vec_ref) = rest[n_blk : n_blk + 7]
    mid, n2, n2t, g, acc_o, acc_d, act, dpre = rest[n_blk + 7 :]
    tok = xs[0].shape[0]
    j = pl.program_id(0)

    @pl.when(j == 0)
    def _():
        for s in range(n_blk):
            sl = slice(s * tok, (s + 1) * tok)
            m = xs[s][...].astype(F32) + dot(ct_ref[:, sl], wo_ref[...], TN) + bo_ref[...]
            mid[sl] = m
            acc_o[sl] = m + bout_ref[...]
            acc_d[sl] = jnp.zeros_like(m)
            n, _ = center(m)
            nb = (n * gain_ref[...] + bias_ref[...]).astype(BF16)
            n2[sl] = nb
            n2t[:, sl] = nb.T
            g[sl] = gs[s][...]

    bin_grad = None
    for s in range(n_blk):
        sl = slice(s * tok, (s + 1) * tok)
        pre = dot(n2[sl], win_ref[...]) + bin_ref[...]
        phi, slope = gate(pre)
        a = (pre * phi).astype(BF16)
        dact = dot(g[sl], wout_ref[...], NT)
        dp = (dact * (phi + slope)).astype(BF16)
        act[sl] = a
        dpre[sl] = dp
        col = jnp.sum(dp.astype(F32), axis=0, keepdims=True)
        bin_grad = col if bin_grad is None else bin_grad + col
        acc_o[sl] += dot(a, wout_ref[...])
        acc_d[sl] += dot(dp, win_ref[...], NT)
    gbin_ref[...] = bin_grad
    gwout_ref[...] = dot(act[...], g[...], TN).astype(BF16)
    gwin_ref[...] = dot(n2t[...], dpre[...]).astype(BF16)

    @pl.when(j == pl.num_programs(0) - 1)
    def _():
        head = wo_ref.shape[0] // H
        sums = [None] * 4
        for s in range(n_blk):
            sl = slice(s * tok, (s + 1) * tok)
            outs[s][...] = acc_o[sl].astype(BF16)
            n, rstd = center(mid[sl])
            e = acc_d[sl]
            gf = g[sl].astype(F32)
            f = e * gain_ref[...]
            dm = gf + rstd * (
                f - jnp.mean(f, axis=-1, keepdims=True) - n * jnp.mean(f * n, axis=-1, keepdims=True)
            )
            dmid_ref[sl] = dm
            db = dm.astype(BF16)
            n2[sl] = db
            for i, term in enumerate((gf, e * n, e, db.astype(F32))):
                col = jnp.sum(term, axis=0, keepdims=True)
                sums[i] = col if sums[i] is None else sums[i] + col
            dc = dot(wo_ref[...], db, NT)
            for h in range(H):
                hs = slice(h * head, (h + 1) * head)
                dot_ref[hs, sl] = (dc[hs] * il_ref[h, :, sl]).astype(BF16)
        for i in range(4):
            vec_ref[i : i + 1] = sums[i]
        gwo_ref[...] = dot(ct_ref[...], n2[...]).astype(BF16)


def attend_back_kernel(scale, p_ref, q_ref, k_ref, v_ref, do_ref, c_ref, dq_ref, dk_ref, dv_ref, ds):
    seq = q_ref.shape[1]
    do = do_ref[...]
    vh = v_ref[...].T
    delta = jnp.sum(do.astype(F32) * c_ref[...].astype(F32), axis=0, keepdims=True)
    step = seq // 2
    for c in range(2):
        sl = slice(c * step, (c + 1) * step)
        dp = dot(vh, do[:, sl])
        d = (p_ref[0, :, sl].astype(F32) * (dp - delta[:, sl])).astype(BF16)
        ds[:, sl] = d
        dq_ref[:, sl] = (dot(k_ref[...], d) * scale).astype(BF16)
    dv_ref[...] = dot(p_ref[0], do, NT).T.astype(BF16)
    dk_ref[...] = (dot(ds[...], q_ref[...], NT) * LN2).T.astype(BF16)


def input_kernel(n_blk, *refs):
    xs = refs[:n_blk]
    dmid_ref, gain_ref, dq_ref, dk_ref, dv_ref, wq_ref, wk_ref, wv_ref = refs[n_blk : n_blk + 8]
    outs = refs[n_blk + 8 : 2 * n_blk + 8]
    vec_ref = refs[2 * n_blk + 8]
    tok = xs[0].shape[0]
    sums = [None] * 2
    for s in range(n_blk):
        sl = slice(s * tok, (s + 1) * tok)
        et = dot(wq_ref[...], dq_ref[:, sl]) + dot(wk_ref[...], dk_ref[:, sl]) + dot(wv_ref[...], dv_ref[:, sl])
        e = et.T
        n, rstd = center(xs[s][...].astype(F32))
        f = e * gain_ref[...]
        dx = dmid_ref[sl] + rstd * (
            f - jnp.mean(f, axis=-1, keepdims=True) - n * jnp.mean(f * n, axis=-1, keepdims=True)
        )
        outs[s][...] = dx.astype(BF16)
        for i, term in enumerate((e * n, e)):
            col = jnp.sum(term, axis=0, keepdims=True)
            sums[i] = col if sums[i] is None else sums[i] + col
    for i in range(2):
        vec_ref[i : i + 1] = sums[i]


def qkv_grad_kernel(nt_ref, dq_ref, dk_ref, dv_ref, gq_ref, gk_ref, gv_ref, vec_ref):
    nt = nt_ref[...]
    ones = jnp.ones((8, nt.shape[1]), BF16)
    gq_ref[...] = dot(nt, dq_ref[...], NT).astype(BF16)
    gk_ref[...] = dot(nt, dk_ref[...], NT).astype(BF16)
    gv_ref[...] = dot(nt, dv_ref[...], NT).astype(BF16)
    vec_ref[0:1] = dot(ones, dq_ref[...], NT)[:1]
    vec_ref[1:2] = dot(ones, dv_ref[...], NT)[:1]


def body(
    inputs,
    lengths,
    out_grad,
    ln1_gain,
    ln1_bias,
    w_query,
    b_query,
    w_key,
    w_value,
    b_value,
    w_output,
    b_output,
    ln2_gain,
    ln2_bias,
    w_in,
    b_in,
    w_out,
    b_out,
):
    n_seq, tok, width = inputs.shape
    n_blk = lax.axis_size("blk")
    n_dp = lax.axis_size("dp")
    n_dev = n_blk * n_dp
    assert n_seq == n_blk
    seq = tok * n_blk
    hidden = w_in.shape[1]
    head = width // H
    scale = head ** (-0.5)
    blk = lax.axis_index("blk")
    me = lax.axis_index("dp") * n_blk + blk

    def swap(v, s):
        return lax.ppermute(v, "blk", [(i, i ^ s) for i in range(n_blk)])

    def spread(v):
        pick = [lax.dynamic_index_in_dim(v, blk ^ s, 0, keepdims=False) for s in range(n_blk)]
        return [pick[0]] + [swap(pick[s], s) for s in range(1, n_blk)]

    def collect(pieces):
        back = [pieces[0]] + [swap(pieces[s], s) for s in range(1, n_blk)]
        out = jnp.zeros((n_seq, tok, width), BF16)
        for s in range(n_blk):
            out = lax.dynamic_update_index_in_dim(out, back[s], blk ^ s, 0)
        return out

    row = lambda v: v.astype(F32).reshape(1, -1)
    column = lambda v: v.astype(F32).reshape(-1, 1)

    xs = spread(inputs)
    tied = lax.optimization_barrier((out_grad, xs))
    gs = spread(tied[0])
    xs = tied[1]
    live = ((blk ^ jnp.arange(n_blk)) * tok < lengths[blk]).astype(jnp.int32).reshape(1, n_blk)

    sds = jax.ShapeDtypeStruct
    piece = full((tok, width))
    wide = full((width, seq))
    n_col = 3
    cols = width // n_col
    strip = pl.BlockSpec((cols, seq), lambda j: (j, 0))
    nt, qt, kt, vt = pl.pallas_call(
        functools.partial(qkv_kernel, scale * LOG2E, n_blk),
        grid=(n_col,),
        in_specs=[piece] * n_blk
        + [full((1, width))] * 2
        + [pl.BlockSpec((width, cols), lambda j: (0, j)), pl.BlockSpec((cols, 1), lambda j: (j, 0))]
        + [pl.BlockSpec((width, cols), lambda j: (0, j))] * 2
        + [pl.BlockSpec((cols, 1), lambda j: (j, 0))],
        out_specs=[wide, strip, strip, strip],
        out_shape=[sds((width, seq), BF16)] * 4,
        compiler_params=params(),
        name="qkv",
    )(*xs, row(ln1_gain), row(ln1_bias), w_query, column(b_query), w_key, w_value, column(b_value))

    per_head = pl.BlockSpec((head, seq), lambda h: (h, 0))
    per_square = pl.BlockSpec((1, seq, seq), lambda h: (h, 0, 0))
    ct, probs, inv_total = pl.pallas_call(
        functools.partial(attend_kernel, n_blk),
        grid=(H,),
        in_specs=[pl.BlockSpec(memory_space=pltpu.SMEM), per_head, per_head, per_head],
        out_specs=[per_head, per_square, pl.BlockSpec((1, 1, seq), lambda h: (h, 0, 0))],
        out_shape=[sds((width, seq), BF16), sds((H, seq, seq), BF16), sds((H, 1, seq), F32)],
        compiler_params=params(),
        name="attend",
    )(live, qt, kt, vt)

    n_tile = 12
    tile = hidden // n_tile
    result = pl.pallas_call(
        functools.partial(ffn_kernel, n_blk),
        grid=(n_tile,),
        in_specs=[piece] * (2 * n_blk)
        + [
            wide,
            full((H, 1, seq)),
            full((width, width)),
            full((1, width)),
            full((1, width)),
            full((1, width)),
            pl.BlockSpec((width, tile), lambda j: (0, j)),
            pl.BlockSpec((1, tile), lambda j: (0, j)),
            pl.BlockSpec((tile, width), lambda j: (j, 0)),
            full((1, width)),
        ],
        out_specs=[piece] * n_blk
        + [
            pl.BlockSpec((tile, width), lambda j: (j, 0)),
            pl.BlockSpec((width, tile), lambda j: (0, j)),
            pl.BlockSpec((1, tile), lambda j: (0, j)),
            full((seq, width)),
            wide,
            full((width, width)),
            full((8, width)),
        ],
        out_shape=[sds((tok, width), BF16)] * n_blk
        + [
            sds((hidden, width), BF16),
            sds((width, hidden), BF16),
            sds((1, hidden), F32),
            sds((seq, width), F32),
            sds((width, seq), BF16),
            sds((width, width), BF16),
            sds((8, width), F32),
        ],
        scratch_shapes=[
            pltpu.VMEM((seq, width), F32),
            pltpu.VMEM((seq, width), BF16),
            pltpu.VMEM((width, seq), BF16),
            pltpu.VMEM((seq, width), BF16),
            pltpu.VMEM((seq, width), F32),
            pltpu.VMEM((seq, width), F32),
            pltpu.VMEM((seq, tile), BF16),
            pltpu.VMEM((seq, tile), BF16),
        ],
        compiler_params=params(),
        name="ffn",
    )(
        *xs,
        *gs,
        ct,
        inv_total,
        w_output,
        row(b_output),
        row(ln2_gain),
        row(ln2_bias),
        w_in,
        row(b_in),
        w_out,
        row(b_out),
    )
    out_pieces = result[:n_blk]
    g_wout, g_win, g_bin, dmid, dct, g_wo, vec2 = result[n_blk:]

    bits = (n_dev - 1).bit_length()
    assert n_dev == 1 << bits

    def scatter(grad, order, wire):
        share = grad.shape[0] // n_dev
        order = list(order) + [b for b in range(bits) if b not in order]
        axes = list(range(bits - 1, -1, -1))
        terms = [grad.reshape((2,) * bits + (share,) + grad.shape[1:])]
        for b in order:
            at = axes.index(b)
            axes.pop(at)
            mine = (me >> b) & 1
            send = None
            keep = []
            for t in terms:
                other = lax.dynamic_index_in_dim(t, 1 - mine, at, keepdims=False)
                send = other.astype(F32) if send is None else send + other.astype(F32)
                keep.append(lax.dynamic_index_in_dim(t, mine, at, keepdims=False))
            got = lax.ppermute(send.astype(wire), ("dp", "blk"), [(i, i ^ (1 << b)) for i in range(n_dev)])
            terms = keep + [got]
        total = terms[0].astype(F32)
        for t in terms[1:]:
            total = total + t.astype(F32)
        return total

    s_wout = scatter(g_wout, (0, 1, 2, 3, 4), BF16)
    s_win = scatter(g_win, (0, 2, 1, 3, 4), BF16)
    s_wo = scatter(g_wo, (0, 3, 4, 1, 2), BF16)
    output = collect(out_pieces)

    dqt, dkt, dvt = pl.pallas_call(
        functools.partial(attend_back_kernel, scale),
        grid=(H,),
        in_specs=[per_square] + [per_head] * 5,
        out_specs=[per_head] * 3,
        out_shape=[sds((width, seq), BF16)] * 3,
        scratch_shapes=[pltpu.VMEM((seq, seq), BF16)],
        compiler_params=params(),
        name="attend_back",
    )(probs, qt, kt, vt, dct, ct)

    result = pl.pallas_call(
        functools.partial(input_kernel, n_blk),
        in_specs=[piece] * n_blk
        + [full((seq, width)), full((1, width)), wide, wide, wide]
        + [full((width, width))] * 3,
        out_specs=[piece] * n_blk + [full((8, width))],
        out_shape=[sds((tok, width), BF16)] * n_blk + [sds((8, width), F32)],
        compiler_params=params(),
        name="input_grad",
    )(*xs, dmid, row(ln1_gain), dqt, dkt, dvt, w_query, w_key, w_value)
    input_grad = collect(result[:n_blk])
    vec1 = result[n_blk]

    col = pl.BlockSpec((width, cols), lambda j: (0, j))
    g_wq, g_wk, g_wv, vecq = pl.pallas_call(
        qkv_grad_kernel,
        grid=(n_col,),
        in_specs=[wide, strip, strip, strip],
        out_specs=[col, col, col, pl.BlockSpec((8, cols), lambda j: (0, j))],
        out_shape=[sds((width, width), BF16)] * 3 + [sds((8, width), F32)],
        compiler_params=params(),
        name="qkv_grad",
    )(nt, dqt, dkt, dvt)
    s_wq = scatter(g_wq, (0, 1, 2, 3, 4), BF16)
    s_wk = scatter(g_wk, (0, 2, 3, 4, 1), BF16)
    s_wv = scatter(g_wv, (0, 3, 4, 1, 2), BF16)

    vectors = [vec1[0], vec1[1], vecq[0], vecq[1], vec2[3], vec2[1], vec2[2], g_bin[0], vec2[0]]
    packed = jnp.concatenate([v.reshape(n_dev, -1) for v in vectors], axis=1)
    packed = scatter(packed, (0, 1, 2, 3, 4), F32).reshape(-1)
    parts = []
    at = 0
    for v in vectors:
        size = v.shape[0] // n_dev
        parts.append(packed[at : at + size])
        at += size
    p_ln1g, p_ln1b, p_bq, p_bv, p_bo, p_ln2g, p_ln2b, p_bin, p_bout = parts
    return (
        output,
        input_grad,
        p_ln1g,
        p_ln1b,
        s_wq,
        p_bq,
        s_wk,
        s_wv,
        p_bv,
        s_wo,
        p_bo,
        p_ln2g,
        p_ln2b,
        s_win,
        p_bin,
        s_wout,
        p_bout,
    )


def solution(mesh):
    whole = P(("dp", "blk"))
    rows = P(("dp", "blk"), None)
    tokens = P("dp", "blk", None)
    in_specs = (tokens, P("dp"), tokens) + (P(),) * 15
    out_specs = (
        tokens,
        tokens,
        whole,
        whole,
        rows,
        whole,
        rows,
        rows,
        whole,
        rows,
        whole,
        whole,
        whole,
        rows,
        whole,
        rows,
        whole,
    )
    return jax.shard_map(body, mesh=mesh, in_specs=in_specs, out_specs=out_specs, check_vma=False)
```

time: 1210 us -> 338 us (0.28)
  waiting for transfers between devices: 716 us -> 103 us
  matrix products: 296 us -> 0 us
  Pallas kernels: 0 us -> 70.9 us
  starting transfers between devices: 0.84 us -> 52 us
  blocking collectives: 40.4 us -> 0 us
  other arithmetic: 55.8 us -> 18.2 us
  between operations: 15.2 us -> 1.5 us
    reduce_scatter x7 -> x0, waiting for transfers between devices: 683 us -> none  [the longest x1 142 us: body(): lax.psum_scatter(grad_list[11], ('dp', 'blk'), scatter_dimension=0, tiled...]
    dot_general x30 -> x0, matrix products: 296 us -> none  [the longest x6 37.8 us: contract_rows(): lax.dot_general(left, right, (((0,), (0,)), ((), ())), preferred_element_...]
    ppermute x0 -> x47, waiting for transfers between devices: none -> 103 us  [the longest x35 52.3 us: scatter(): lax.ppermute(send.astype(wire), ('dp', 'blk'), [(i, i ^ 1 << b) for i in...]
    pallas_call x0 -> x4, Pallas kernels: none -> 70.9 us  [the longest x1 29.9 us: body(): pl.pallas_call(functools.partial(attend_back_kernel, scale), grid=(H,), i...]
    pallas_call x0 -> x3, local copies, waits for them, and re-layouts: none -> 69.3 us  [the longest x2 59.1 us: body(): pl.pallas_call(functools.partial(ffn_kernel, n_blk), grid=(n_tile,), in_s...]
    ppermute x0 -> x47, starting transfers between devices: none -> 52 us  [the longest x35 42 us: scatter(): lax.ppermute(send.astype(wire), ('dp', 'blk'), [(i, i ^ 1 << b) for i in...]
    unnamed x1 -> x0, blocking collectives: 40.4 us -> none
    reduce_sum x11 -> x0, other arithmetic: 35.3 us -> none  [the longest x1 22.1 us: body(): absorb_row_total = jnp.sum(weights, axis=-1)]
  transfers between devices with their start and end apart: 9 -> 47, of which waited for: 9 -> 22; matrix products, arithmetic and copies ran while one was open for 11% -> 12% of each run, Pallas kernels for 0% -> 21%
where the time goes in v1:
time: 338 us; the launch traced here: 337 us
  waiting for transfers between devices  103 us (30%)
  local copies, waits for them, and re-layouts  91.9 us (27%)
  Pallas kernels  70.9 us (21%)
  starting transfers between devices  52 us (15%)
  other arithmetic  18.2 us (5%)
    pallas_call x2, local copies, waits for them, and re-layouts, body(): pl.pallas_call(functools.partial(ffn_kernel, n_blk), grid=(n_tile,), in_s...  59.1 us
    ppermute x35, waiting for transfers between devices, scatter(): lax.ppermute(send.astype(wire), ('dp', 'blk'), [(i, i ^ 1 << b) for i in...  52.3 us
    ppermute x12, waiting for transfers between devices, swap(): return lax.ppermute(v, 'blk', [(i, i ^ s) for i in range(n_blk)])  50.4 us
    ppermute x35, starting transfers between devices, scatter(): lax.ppermute(send.astype(wire), ('dp', 'blk'), [(i, i ^ 1 << b) for i in...  42 us
    pallas_call x1, Pallas kernels, body(): pl.pallas_call(functools.partial(attend_back_kernel, scale), grid=(H,), i...  29.9 us
    pallas_call x1, Pallas kernels, body(): pl.pallas_call(functools.partial(attend_kernel, n_blk), grid=(H,), in_spe...  24.3 us
    convert_element_type x24, other arithmetic, scatter(): send.astype(wire)  10.3 us
    pallas_call x1, local copies, waits for them, and re-layouts, body(): pl.pallas_call(functools.partial(input_kernel, n_blk), in_specs=[piece] *...  10.1 us
  transfers between devices with their start and end apart: 47, of which 22 were waited for; matrix products, arithmetic and copies ran while one was open for 12% of the time, Pallas kernels for 21%

profile of v1, /device:TPU:0, one launch (start us, length us, event | category | flops | bytes accessed | tf_op | source)
XLA Modules:
  0.0 337.2 jit_solution(16805151347511172504)
XLA Ops:
  0.7 2.3 dynamic-slice_bitcast_fusion.10
  3.5 2.5 collective-permute-start.1
  6.1 9.8 %collective-permute-done.1.refs_2_ = bf16[256,768]{1,0:T(8,128)(2,1)S(1)} collective-permute-done((bf16[256,768]{1,0:T(8,128)(2,1)S(1)}, bf16[256,768]{1,0:T(8,128)(2,1)S(1)}, u32[]{:S(2)}, u32[]{:S(2)}) %collective-permute-start.1) | collective-permute-done | bytes 393248 | tf_op jit(solution)/shard_map/ppermute | solution.py:267
  15.9 8.1 %collective-permute-done.2.refs_3_ = bf16[256,768]{1,0:T(8,128)(2,1)S(1)} collective-permute-done((bf16[256,768]{1,0:T(8,128)(2,1)S(1)}, bf16[256,768]{1,0:T(8,128)(2,1)S(1)}, u32[]{:S(2)}, u32[]{:S(2)}) %collective-permute-start.2) | collective-permute-done | bytes 393248 | tf_op jit(solution)/shard_map/ppermute | solution.py:267
  32.0 8.6 %qkv.1 = (bf16[768,1024]{1,0:T(8,128)(2,1)}, bf16[768,1024]{1,0:T(8,128)(2,1)}, bf16[768,1024]{1,0:T(8,128)(2,1)}, bf16[768,1024]{1,0:T(8,128)(2,1)}) custom-call(bf16[256,768]{1,0:T(8,128)(2,1)} %get-tuple-element.52.refs_0_, bf16[256,768]{1,0:T(8,128)(2,1)} %copy-done.5, bf16[256,768]{1,0:T(8,128)(2,1)} %copy-done.8, bf16[256,768]{1,0:T(8,128)(2,1)} %copy-done.11, ...), custom_call_target="tpu_custom_call" | custom-call | tf_op jit(solution)/shard_map/qkv/pallas_call | solution.py:295
  40.6 24.3 %attend.1 = (bf16[768,1024]{1,0:T(8,128)(2,1)}, bf16[12,1024,1024]{2,1,0:T(8,128)(2,1)}, f32[12,1,1024]{2,1,0:T(1,128)}) custom-call(s32[1,4]{1,0:T(1,128)} %compare_convert_fusion.live_ref, bf16[768,1024]{1,0:T(8,128)(2,1)} %get-tuple-element.57.q_ref, bf16[768,1024]{1,0:T(8,128)(2,1)} %get-tuple-element.58.k_ref, bf16[768,1024]{1,0:T(8,128)(2,1)} %get-tuple-element.59.v_ref), custom_call_target="tpu_custom_call" | custom-call | tf_op jit(solution)/shard_map/attend/pallas_call | solution.py:311
  66.9 58.6 %ffn.1 = (bf16[4,256,768]{2,1,0:T(8,128)(2,1)}, bf16[256,768]{1,0:T(8,128)(2,1)}, bf16[256,768]{1,0:T(8,128)(2,1)}, bf16[256,768]{1,0:T(8,128)(2,1)}, f32[1024,7...) fusion(bf16[4,256,768]{2,1,0:T(8,128)(2,1)} %broadcast.27.clone, ...), kind=kCustom, calls=%fused_computation.39 | custom fusion | bytes 32354308 | tf_op jit(solution)/shard_map/ffn/pallas_call | solution.py:323
  128.7 29.9 %attend_back.1 = (bf16[768,1024]{1,0:T(8,128)(2,1)}, bf16[768,1024]{1,0:T(8,128)(2,1)}, bf16[768,1024]{1,0:T(8,128)(2,1)}) custom-call(bf16[12,1024,1024]{2,1,0:T(8,128)(2,1)} %get-tuple-element.67.p_ref, bf16[768,1024]{1,0:T(8,128)(2,1)} %get-tuple-element.57.q_ref, bf16[768,1024]{1,0:T(8,128)(2,1)} %get-tuple-element.58.k_ref, ...), custom_call_target="tpu_custom_call" | custom-call | tf_op jit(solution)/shard_map/attend_back/pallas_call | solution.py:418
  158.7 8.1 %qkv_grad.1 = (bf16[768,768]{1,0:T(8,128)(2,1)}, bf16[768,768]{1,0:T(8,128)(2,1)}, bf16[768,768]{1,0:T(8,128)(2,1)}, f32[8,768]{1,0:T(8,128)}) custom-call(bf16[768,1024]{1,0:T(8,128)(2,1)} %get-tuple-element.77.nt_ref, bf16[768,1024]{1,0:T(8,128)(2,1)} %get-tuple-element.69.dq_ref, bf16[768,1024]{1,0:T(8,128)(2,1)} %get-tuple-element.70.dk_ref, ...), custom_call_target="tpu_custom_call" | custom-call | tf_op jit(solution)/shard_map/qkv_grad/pallas_call | solution.py:443
  168.2 10.1 %input_grad.1 = (bf16[4,256,768]{2,1,0:T(8,128)(2,1)S(1)}, bf16[256,768]{1,0:T(8,128)(2,1)}, bf16[256,768]{1,0:T(8,128)(2,1)}, bf16[256,768]{1,0:T(8,128)(2,1)}, f32[8,768]{1,0:T(8,128)S(1)}) fusion(bf16[4,256,768]{2,1,0:T(8,128)(2,1)S(1)} %broadcast.27, s32[]{:T(128)S(6)} %select_n.300, bf16[256,768]{1,0:T(8,128)(2,1)S(1)} %copy-done.2, ...), kind=kCustom, calls=%fused_computation.35 | custom fusion | bytes 14576644 | tf_op jit(solution)/shard_map/input_grad/pallas_call | solution.py:429
  195.7 2.7 collective-permute-start.16
  203.2 7.5 %collective-permute-done.10 = bf16[256,768]{1,0:T(8,128)(2,1)S(1)} collective-permute-done((bf16[256,768]{1,0:T(8,128)(2,1)}, bf16[256,768]{1,0:T(8,128)(2,1)S(1)}, u32[]{:S(2)}, u32[]{:S(2)}) %collective-permute-start.10) | collective-permute-done | bytes 393248 | tf_op jit(solution)/shard_map/ppermute | solution.py:267
  210.8 7.5 %collective-permute-done.11 = bf16[256,768]{1,0:T(8,128)(2,1)S(1)} collective-permute-done((bf16[256,768]{1,0:T(8,128)(2,1)S(1)}, bf16[256,768]{1,0:T(8,128)(2,1)S(1)}, u32[]{:S(2)}, u32[]{:S(2)}) %collective-permute-start.11) | collective-permute-done | bytes 393248 | tf_op jit(solution)/shard_map/ppermute | solution.py:267
  220.0 10.4 %collective-permute-done.7 = bf16[256,768]{1,0:T(8,128)(2,1)S(1)} collective-permute-done((bf16[256,768]{1,0:T(8,128)(2,1)}, bf16[256,768]{1,0:T(8,128)(2,1)S(1)}, u32[]{:S(2)}, u32[]{:S(2)}) %collective-permute-start.7) | collective-permute-done | bytes 393248 | tf_op jit(solution)/shard_map/ppermute | solution.py:267
  230.4 7.1 %collective-permute-done.8 = bf16[256,768]{1,0:T(8,128)(2,1)S(1)} collective-permute-done((bf16[256,768]{1,0:T(8,128)(2,1)S(1)}, bf16[256,768]{1,0:T(8,128)(2,1)S(1)}, u32[]{:S(2)}, u32[]{:S(2)}) %collective-permute-start.8) | collective-permute-done | bytes 393248 | tf_op jit(solution)/shard_map/ppermute | solution.py:267
  243.4 4.8 %collective-permute-done.33 = bf16[2,2,2,24,768]{4,3,2,1,0:T(8,128)(2,1)S(1)} collective-permute-done((bf16[2,2,2,24,768]{4,3,2,1,0:T(8,128)(2,1)S(1)}, bf16[2,2,2,24,768]{4,3,2,1,0:T(8,128)(2,1)S(1)}, u32[]{:S(2)}, u32[]{:S(2)}) %collective-permute-start.33) | collective-permute-done | bytes 294944 | tf_op jit(solution)/shard_map/ppermute | solution.py:406
  249.8 4.3 %collective-permute-done.28 = bf16[2,2,2,24,768]{4,3,2,1,0:T(8,128)(2,1)S(1)} collective-permute-done((bf16[2,2,2,24,768]{4,3,2,1,0:T(8,128)(2,1)S(1)}, bf16[2,2,2,24,768]{4,3,2,1,0:T(8,128)(2,1)S(1)}, u32[]{:S(2)}, u32[]{:S(2)}) %collective-permute-start.28) | collective-permute-done | bytes 294944 | tf_op jit(solution)/shard_map/ppermute | solution.py:406
  255.3 2.7 collective-permute-start.29
  265.1 2.9 collective-permute-done.34
  273.5 18.1 %collective-permute-done.19 = bf16[2,2,24,768]{3,2,0,1:T(8,128)(2,1)S(1)} collective-permute-done((bf16[2,2,24,768]{3,2,0,1:T(8,128)(2,1)S(1)}, bf16[2,2,24,768]{3,2,0,1:T(8,128)(2,1)S(1)}, u32[]{:S(2)}, u32[]{:S(2)}) %collective-permute-start.19) | collective-permute-done | bytes 147488 | tf_op jit(solution)/shard_map/ppermute | solution.py:406
  307.6 5.7 %collective-permute-done.44 = bf16[2,2,96,768]{3,2,0,1:T(8,128)(2,1)S(1)} collective-permute-done((bf16[2,2,96,768]{3,2,0,1:T(8,128)(2,1)S(1)}, bf16[2,2,96,768]{3,2,0,1:T(8,128)(2,1)S(1)}, u32[]{:S(2)}, u32[]{:S(2)}) %collective-permute-start.44) | collective-permute-done | bytes 589856 | tf_op jit(solution)/shard_map/ppermute | solution.py:406
  317.4 6.5 %collective-permute-done.45 = bf16[2,96,768]{2,1,0:T(8,128)(2,1)S(1)} collective-permute-done((bf16[2,96,768]{2,1,0:T(8,128)(2,1)S(1)}, bf16[2,96,768]{2,1,0:T(8,128)(2,1)S(1)}, u32[]{:S(2)}, u32[]{:S(2)}) %collective-permute-start.45) | collective-permute-done | bytes 294944 | tf_op jit(solution)/shard_map/ppermute | solution.py:406
  324.9 2.3 collective-permute-start.46
  330.3 2.3 collective-permute-done.46
  (239 shorter events, 88.5 us)
Async XLA Ops:
  3.5 12.5 %collective-permute-start.1 = (bf16[256,768]{1,0:T(8,128)(2,1)S(1)}, bf16[256,768]{1,0:T(8,128)(2,1)S(1)}, u32[]{:S(2)}, u32[]{:S(2)}) collective-permute-start(bf16[256,768]{1,0:T(8,128)(2,1)S(1)} %get-tuple-element.134), channel_id=1, source_target_pairs={{0,2},{1,3},{2,0},{3,1},{4,6},{5,7},{6,4},{7,5},{8,10},{9,11},{10,... | collective-permute-start | bytes 1179656 | tf_op jit(solution)/shard_map/ppermute | solution.py:267
  5.9 18.0 %collective-permute-start.2 = (bf16[256,768]{1,0:T(8,128)(2,1)S(1)}, bf16[256,768]{1,0:T(8,128)(2,1)S(1)}, u32[]{:S(2)}, u32[]{:S(2)}) collective-permute-start(bf16[256,768]{1,0:T(8,128)(2,1)S(1)} %get-tuple-element.131), channel_id=1, source_target_pairs={{0,3},{1,2},{2,1},{3,0},{4,7},{5,6},{6,5},{7,4},{8,11},{9,10},{10,... | collective-permute-start | bytes 1179656 | tf_op jit(solution)/shard_map/ppermute | solution.py:267
  25.2 39.7 %collective-permute-start.3 = (bf16[256,768]{1,0:T(8,128)(2,1)}, bf16[256,768]{1,0:T(8,128)(2,1)}, u32[]{:S(2)}, u32[]{:S(2)}) collective-permute-start(bf16[256,768]{1,0:T(8,128)(2,1)} %get-tuple-element.129), channel_id=1, source_target_pairs={{0,1},{1,0},{2,3},{3,2},{4,5},{5,4},{6,7},{7,6},{8,9},{9,8},{10,11... | collective-permute-start | bytes 1179656 | tf_op jit(solution)/shard_map/ppermute | solution.py:267
  25.3 39.5 %collective-permute-start.4 = (bf16[256,768]{1,0:T(8,128)(2,1)}, bf16[256,768]{1,0:T(8,128)(2,1)}, u32[]{:S(2)}, u32[]{:S(2)}) collective-permute-start(bf16[256,768]{1,0:T(8,128)(2,1)} %get-tuple-element.128), channel_id=1, source_target_pairs={{0,2},{1,3},{2,0},{3,1},{4,6},{5,7},{6,4},{7,5},{8,10},{9,11},{10,... | collective-permute-start | bytes 1179656 | tf_op jit(solution)/shard_map/ppermute | solution.py:267
  27.0 37.9 %collective-permute-start.5 = (bf16[256,768]{1,0:T(8,128)(2,1)}, bf16[256,768]{1,0:T(8,128)(2,1)}, u32[]{:S(2)}, u32[]{:S(2)}) collective-permute-start(bf16[256,768]{1,0:T(8,128)(2,1)} %get-tuple-element.127), channel_id=1, source_target_pairs={{0,3},{1,2},{2,1},{3,0},{4,7},{5,6},{6,5},{7,4},{8,11},{9,10},{10,... | collective-permute-start | bytes 1179656 | tf_op jit(solution)/shard_map/ppermute | solution.py:267
  128.3 127.0 %collective-permute-start.42 = (bf16[2,2,2,2,96,768]{5,4,3,2,1,0:T(8,128)(2,1)}, bf16[2,2,2,2,96,768]{5,4,3,2,1,0:T(8,128)(2,1)}, u32[]{:S(2)}, u32[]{:S(2)}) collective-permute-start(bf16[2,2,2,2,96,768]{5,4,3,2,1,0:T(8,128)(2,1)} %dynamic-slice_bitcast_fusion), channel_id=1, source_target_pairs={{0,1},{1,0},{2,3},{3,2},{4,5},{5,4},{6,7},{7,6},{8,9},{9,8},{10,11... | collective-permute-start | bytes 7077896 | tf_op jit(solution)/shard_map/ppermute | solution.py:406
  184.0 75.7 %collective-permute-start.37 = (bf16[2,2,2,2,24,3072]{5,4,3,2,1,0:T(8,128)(2,1)S(1)}, bf16[2,2,2,2,24,3072]{5,4,3,2,1,0:T(8,128)(2,1)S(1)}, u32[]{:S(2)}, u32[]{:S(2)}) collective-permute-start(bf16[2,2,2,2,24,3072]{5,4,3,2,1,0:T(8,128)(2,1)S(1)} %dynamic-slice_bitcast_fusion.1), channel_id=1, source_target_pairs={{0,1},{1,0},{2,3},{3,2},{4,5},{5,4},{6,7},{7,6},{8,9},{9,8},{10,11... | collective-permute-start | bytes 7077896 | tf_op jit(solution)/shard_map/ppermute | solution.py:406
  200.2 18.0 %collective-permute-start.11 = (bf16[256,768]{1,0:T(8,128)(2,1)S(1)}, bf16[256,768]{1,0:T(8,128)(2,1)S(1)}, u32[]{:S(2)}, u32[]{:S(2)}) collective-permute-start(bf16[256,768]{1,0:T(8,128)(2,1)S(1)} %copy-done.22), channel_id=1, source_target_pairs={{0,3},{1,2},{2,1},{3,0},{4,7},{5,6},{6,5},{7,4},{8,11},{9,10},{10,... | collective-permute-start | bytes 1179656 | tf_op jit(solution)/shard_map/ppermute | solution.py:267
  201.6 18.1 %collective-permute-start.6 = (bf16[256,768]{1,0:T(8,128)(2,1)}, bf16[256,768]{1,0:T(8,128)(2,1)S(1)}, u32[]{:S(2)}, u32[]{:S(2)}) collective-permute-start(bf16[256,768]{1,0:T(8,128)(2,1)} %get-tuple-element.108), channel_id=1, source_target_pairs={{0,1},{1,0},{2,3},{3,2},{4,5},{5,4},{6,7},{7,6},{8,9},{9,8},{10,11... | collective-permute-start | bytes 1179656 | tf_op jit(solution)/shard_map/ppermute | solution.py:267
  210.7 27.3 %collective-permute-start.32 = (bf16[2,2,2,2,24,768]{5,4,3,2,1,0:T(8,128)(2,1)S(1)}, bf16[2,2,2,2,24,768]{5,4,3,2,1,0:T(8,128)(2,1)S(1)}, u32[]{:S(2)}, u32[]{:S(2)}) collective-permute-start(bf16[2,2,2,2,24,768]{5,4,3,2,1,0:T(8,128)(2,1)S(1)} %dynamic-slice_bitcast_fusion.2), channel_id=1, source_target_pairs={{0,1},{1,0},{2,3},{3,2},{4,5},{5,4},{6,7},{7,6},{8,9},{9,8},{10,11... | collective-permute-start | bytes 1769480 | tf_op jit(solution)/shard_map/ppermute | solution.py:406
  219.8 17.8 %collective-permute-start.8 = (bf16[256,768]{1,0:T(8,128)(2,1)S(1)}, bf16[256,768]{1,0:T(8,128)(2,1)S(1)}, u32[]{:S(2)}, u32[]{:S(2)}) collective-permute-start(bf16[256,768]{1,0:T(8,128)(2,1)S(1)} %copy-done.21), channel_id=1, source_target_pairs={{0,3},{1,2},{2,1},{3,0},{4,7},{5,6},{6,5},{7,4},{8,11},{9,10},{10,... | collective-permute-start | bytes 1179656 | tf_op jit(solution)/shard_map/ppermute | solution.py:267
  241.0 13.1 %collective-permute-start.28 = (bf16[2,2,2,24,768]{4,3,2,1,0:T(8,128)(2,1)S(1)}, bf16[2,2,2,24,768]{4,3,2,1,0:T(8,128)(2,1)S(1)}, u32[]{:S(2)}, u32[]{:S(2)}) collective-permute-start(bf16[2,2,2,24,768]{4,3,2,1,0:T(8,128)(2,1)S(1)} %fusion.7), channel_id=1, source_target_pairs={{0,8},{1,9},{2,10},{3,11},{4,12},{5,13},{6,14},{7,15},{8,0},{9,1},... | collective-permute-start | bytes 884744 | tf_op jit(solution)/shard_map/ppermute | solution.py:406
  241.7 19.9 %collective-permute-start.23 = (bf16[2,2,2,24,768]{4,3,2,1,0:T(8,128)(2,1)S(1)}, bf16[2,2,2,24,768]{4,3,2,1,0:T(8,128)(2,1)S(1)}, u32[]{:S(2)}, u32[]{:S(2)}) collective-permute-start(bf16[2,2,2,24,768]{4,3,2,1,0:T(8,128)(2,1)S(1)} %fusion.8), channel_id=1, source_target_pairs={{0,4},{1,5},{2,6},{3,7},{4,0},{5,1},{6,2},{7,3},{8,12},{9,13},{10,... | collective-permute-start | bytes 884744 | tf_op jit(solution)/shard_map/ppermute | solution.py:406
  248.2 15.2 %collective-permute-start.18 = (bf16[2,2,2,24,768]{4,3,2,1,0:T(8,128)(2,1)S(1)}, bf16[2,2,2,24,768]{4,3,2,1,0:T(8,128)(2,1)S(1)}, u32[]{:S(2)}, u32[]{:S(2)}) collective-permute-start(bf16[2,2,2,24,768]{4,3,2,1,0:T(8,128)(2,1)S(1)} %fusion.9), channel_id=1, source_target_pairs={{0,2},{1,3},{2,0},{3,1},{4,6},{5,7},{6,4},{7,5},{8,10},{9,11},{10,... | collective-permute-start | bytes 884744 | tf_op jit(solution)/shard_map/ppermute | solution.py:406
  254.1 13.9 %collective-permute-start.34 = (bf16[2,2,24,768]{3,2,0,1:T(8,128)(2,1)S(1)}, bf16[2,2,24,768]{3,2,0,1:T(8,128)(2,1)S(1)}, u32[]{:S(2)}, u32[]{:S(2)}) collective-permute-start(bf16[2,2,24,768]{3,2,0,1:T(8,128)(2,1)S(1)} %copy.82), channel_id=1, source_target_pairs={{0,16},{1,17},{2,18},{3,19},{4,20},{5,21},{6,22},{7,23},{8,24},{9,... | collective-permute-start | bytes 442376 | tf_op jit(solution)/shard_map/ppermute | solution.py:406
  255.3 14.7 %collective-permute-start.29 = (bf16[2,2,24,768]{3,2,0,1:T(8,128)(2,1)S(1)}, bf16[2,2,24,768]{3,2,0,1:T(8,128)(2,1)S(1)}, u32[]{:S(2)}, u32[]{:S(2)}) collective-permute-start(bf16[2,2,24,768]{3,2,0,1:T(8,128)(2,1)S(1)} %copy.76), channel_id=1, source_target_pairs={{0,16},{1,17},{2,18},{3,19},{4,20},{5,21},{6,22},{7,23},{8,24},{9,... | collective-permute-start | bytes 442376 | tf_op jit(solution)/shard_map/ppermute | solution.py:406
  259.7 39.5 %collective-permute-start.43 = (bf16[2,2,2,96,768]{4,3,2,1,0:T(8,128)(2,1)S(1)}, bf16[2,2,2,96,768]{4,3,2,1,0:T(8,128)(2,1)S(1)}, u32[]{:S(2)}, u32[]{:S(2)}) collective-permute-start(bf16[2,2,2,96,768]{4,3,2,1,0:T(8,128)(2,1)S(1)} %fusion), channel_id=1, source_target_pairs={{0,2},{1,3},{2,0},{3,1},{4,6},{5,7},{6,4},{7,5},{8,10},{9,11},{10,... | collective-permute-start | bytes 3538952 | tf_op jit(solution)/shard_map/ppermute | solution.py:406
  261.7 39.7 %collective-permute-start.38 = (bf16[2,2,2,24,3072]{4,3,2,1,0:T(8,128)(2,1)S(1)}, bf16[2,2,2,24,3072]{4,3,2,1,0:T(8,128)(2,1)S(1)}, u32[]{:S(2)}, u32[]{:S(2)}) collective-permute-start(bf16[2,2,2,24,3072]{4,3,2,1,0:T(8,128)(2,1)S(1)} %fusion.1), channel_id=1, source_target_pairs={{0,4},{1,5},{2,6},{3,7},{4,0},{5,1},{6,2},{7,3},{8,12},{9,13},{10,... | collective-permute-start | bytes 3538952 | tf_op jit(solution)/shard_map/ppermute | solution.py:406
  268.0 23.6 %collective-permute-start.19 = (bf16[2,2,24,768]{3,2,0,1:T(8,128)(2,1)S(1)}, bf16[2,2,24,768]{3,2,0,1:T(8,128)(2,1)S(1)}, u32[]{:S(2)}, u32[]{:S(2)}) collective-permute-start(bf16[2,2,24,768]{3,2,0,1:T(8,128)(2,1)S(1)} %copy.67), channel_id=1, source_target_pairs={{0,4},{1,5},{2,6},{3,7},{4,0},{5,1},{6,2},{7,3},{8,12},{9,13},{10,... | collective-permute-start | bytes 442376 | tf_op jit(solution)/shard_map/ppermute | solution.py:406
  270.0 22.0 %collective-permute-start.35 = (bf16[2,24,768]{2,1,0:T(8,128)(2,1)S(1)}, bf16[2,24,768]{2,1,0:T(8,128)(2,1)S(1)}, u32[]{:S(2)}, u32[]{:S(2)}) collective-permute-start(bf16[2,24,768]{2,1,0:T(8,128)(2,1)S(1)} %fusion.18), channel_id=1, source_target_pairs={{0,2},{1,3},{2,0},{3,1},{4,6},{5,7},{6,4},{7,5},{8,10},{9,11},{10,... | collective-permute-start | bytes 221192 | tf_op jit(solution)/shard_map/ppermute | solution.py:406
  272.9 20.8 %collective-permute-start.30 = (bf16[2,24,768]{2,1,0:T(8,128)(2,1)S(1)}, bf16[2,24,768]{2,1,0:T(8,128)(2,1)S(1)}, u32[]{:S(2)}, u32[]{:S(2)}) collective-permute-start(bf16[2,24,768]{2,1,0:T(8,128)(2,1)S(1)} %fusion.19), channel_id=1, source_target_pairs={{0,2},{1,3},{2,0},{3,1},{4,6},{5,7},{6,4},{7,5},{8,10},{9,11},{10,... | collective-permute-start | bytes 221192 | tf_op jit(solution)/shard_map/ppermute | solution.py:406
  299.2 17.6 %collective-permute-start.21 = (bf16[24,768]{1,0:T(8,128)(2,1)S(1)}, bf16[24,768]{1,0:T(8,128)(2,1)S(1)}, u32[]{:S(2)}, u32[]{:S(2)}) collective-permute-start(bf16[24,768]{1,0:T(8,128)(2,1)S(1)} %fusion.28), channel_id=1, source_target_pairs={{0,16},{1,17},{2,18},{3,19},{4,20},{5,21},{6,22},{7,23},{8,24},{9,... | collective-permute-start | bytes 110600 | tf_op jit(solution)/shard_map/ppermute | solution.py:406
  303.2 12.7 %collective-permute-start.39 = (bf16[2,2,24,3072]{3,2,0,1:T(8,128)(2,1)S(1)}, bf16[2,2,24,3072]{3,2,0,1:T(8,128)(2,1)S(1)}, u32[]{:S(2)}, u32[]{:S(2)}) collective-permute-start(bf16[2,2,24,3072]{3,2,0,1:T(8,128)(2,1)S(1)} %copy.89), channel_id=1, source_target_pairs={{0,2},{1,3},{2,0},{3,1},{4,6},{5,7},{6,4},{7,5},{8,10},{9,11},{10,... | collective-permute-start | bytes 1769480 | tf_op jit(solution)/shard_map/ppermute | solution.py:406
  316.1 12.5 %collective-permute-start.40 = (bf16[2,24,3072]{2,1,0:T(8,128)(2,1)S(1)}, bf16[2,24,3072]{2,1,0:T(8,128)(2,1)S(1)}, u32[]{:S(2)}, u32[]{:S(2)}) collective-permute-start(bf16[2,24,3072]{2,1,0:T(8,128)(2,1)S(1)} %fusion.5), channel_id=1, source_target_pairs={{0,8},{1,9},{2,10},{3,11},{4,12},{5,13},{6,14},{7,15},{8,0},{9,1},... | collective-permute-start | bytes 884744 | tf_op jit(solution)/shard_map/ppermute | solution.py:406
  (61 other events, 844.4 us)

commit v2 on v1

--- a/solution.py
+++ b/solution.py
@@ -12,6 +12,7 @@
 LOG2E = 1.4426950408889634
 LN2 = 0.6931471805599453
 INV_SQRT_2PI = 0.3989422804014327
+SQRT_HALF = 0.7071067811865476
 F32 = jnp.float32
 BF16 = jnp.bfloat16
 VMEM_LIMIT = 56 * 2**20
@@ -20,23 +21,16 @@
 NT = (((1,), (1,)), ((), ()))
 TN = (((0,), (0,)), ((), ()))
 
-TAIL_P = 0.28
-TAIL_C = (
-    0.116425338,
-    0.068098667,
-    0.267402196,
-    -0.235117072,
-    0.388714046,
-    -0.105523175,
-)
-
-
 def dot(left, right, dims=NN):
     return lax.dot_general(left, right, dims, preferred_element_type=F32)
 
 
 def params(**kw):
     return pltpu.CompilerParams(vmem_limit_bytes=VMEM_LIMIT, **kw)
+
+
+def cost(macs, nbytes, exps=0):
+    return pl.CostEstimate(flops=2 * macs, bytes_accessed=nbytes, transcendentals=exps)
 
 
 def full(shape):
@@ -52,35 +46,9 @@
 
 
 def gate(u):
-    a = jnp.abs(u)
-    den = 1.0 + TAIL_P * a
-    t = pl.reciprocal(den, approx=True)
-    t = t * (2.0 - den * t)
+    phi = 0.5 + 0.5 * lax.erf(u * SQRT_HALF)
     e = jnp.exp2(u * u * (-0.5 * LOG2E))
-    poly = TAIL_C[-1]
-    for c in TAIL_C[-2::-1]:
-        poly = poly * t + c
-    tail = poly * t * e
-    phi = jnp.where(u < 0.0, tail, 1.0 - tail)
     return phi, u * e * INV_SQRT_2PI
-
-
-def qkv_kernel(scale, n_blk, *refs):
-    xs = refs[:n_blk]
-    gain, bias, wq, bq, wk, wv, bv, nt_ref, q_ref, k_ref, v_ref = refs[n_blk:]
-    tok = xs[0].shape[0]
-
-    @pl.when(pl.program_id(0) == 0)
-    def _():
-        for s in range(n_blk):
-            n, _ = center(xs[s][...].astype(F32))
-            n = n * gain[...] + bias[...]
-            nt_ref[:, s * tok : (s + 1) * tok] = n.astype(BF16).T
-
-    nt = nt_ref[...]
-    q_ref[...] = ((dot(wq[...], nt, TN) + bq[...]) * scale).astype(BF16)
-    k_ref[...] = dot(wk[...], nt, TN).astype(BF16)
-    v_ref[...] = (dot(wv[...], nt, TN) + bv[...]).astype(BF16)
 
 
 def attend_kernel(n_blk, live_ref, q_ref, k_ref, v_ref, c_ref, p_ref, il_ref):
@@ -107,24 +75,148 @@
     il_ref[0] = inv
 
 
+MESH = pl.DeviceIdType.MESH
+
+
+def greet(partners):
+    barrier = pltpu.get_barrier_semaphore()
+    for where in partners:
+        pl.semaphore_signal(barrier, inc=1, device_id=where, device_id_type=MESH)
+    pl.semaphore_wait(barrier, len(partners))
+
+
+def qkv_spread_kernel(
+    scale,
+    n_blk,
+    x_any,
+    gain,
+    bias,
+    wq_any,
+    bq,
+    wk_any,
+    wv_any,
+    bv,
+    xs_any,
+    nt_any,
+    q_any,
+    k_any,
+    v_any,
+    xbuf,
+    wbuf,
+    wt,
+    nt,
+    qkv,
+    send,
+    recv,
+    wsem,
+    osem,
+    xsem,
+):
+    tok, width = xbuf.shape[1:]
+    dp = lax.axis_index("dp")
+    blk = lax.axis_index("blk")
+    own = pltpu.make_async_copy(x_any.at[blk], xbuf.at[0], xsem)
+    own.start()
+    loads = [
+        pltpu.make_async_copy(w, wbuf.at[i], wsem.at[i]) for i, w in enumerate((wq_any, wk_any, wv_any))
+    ]
+    for load in loads:
+        load.start()
+    greet([(dp, blk ^ s) for s in range(1, n_blk)])
+    order = list(range(n_blk - 1, 0, -1))
+    copies = {}
+    for s in order:
+        copies[s] = pltpu.make_async_remote_copy(
+            src_ref=x_any.at[blk ^ s],
+            dst_ref=xbuf.at[s],
+            send_sem=send.at[s - 1],
+            recv_sem=recv.at[s - 1],
+            device_id=(dp, blk ^ s),
+            device_id_type=MESH,
+        )
+        copies[s].start()
+    for i, load in enumerate(loads):
+        load.wait()
+        wt[i] = wbuf[i].T
+    writes = []
+    for s in range(n_blk):
+        if s == 0:
+            own.wait()
+        else:
+            copies[s].wait_recv()
+        sl = slice(s * tok, (s + 1) * tok)
+        n, _ = center(xbuf[s].astype(F32))
+        n = (n * gain[...] + bias[...]).astype(BF16).T
+        nt[:, sl] = n
+        qkv[0, :, sl] = ((dot(wt[0], n) + bq[...]) * scale).astype(BF16)
+        qkv[1, :, sl] = dot(wt[1], n).astype(BF16)
+        qkv[2, :, sl] = (dot(wt[2], n) + bv[...]).astype(BF16)
+        for i, (src, dst) in enumerate(
+            (
+                (xbuf.at[s], xs_any.at[s]),
+                (nt.at[:, sl], nt_any.at[:, sl]),
+                (qkv.at[0, :, sl], q_any.at[:, sl]),
+                (qkv.at[1, :, sl], k_any.at[:, sl]),
+                (qkv.at[2, :, sl], v_any.at[:, sl]),
+            )
+        ):
+            write = pltpu.make_async_copy(src, dst, osem.at[s, i])
+            write.start()
+            writes.append(write)
+    for s in order:
+        copies[s].wait_send()
+    for write in writes:
+        write.wait()
+
+
+def attend_spread_kernel(n_blk, live_ref, q_ref, k_ref, v_ref, g_any, c_ref, p_ref, il_ref, gs_any, send, recv, osem):
+    h = pl.program_id(0)
+    dp = lax.axis_index("dp")
+    blk = lax.axis_index("blk")
+
+    def copy(s):
+        return pltpu.make_async_remote_copy(
+            src_ref=g_any.at[blk ^ s],
+            dst_ref=gs_any.at[s],
+            send_sem=send.at[s - 1],
+            recv_sem=recv.at[s - 1],
+            device_id=(dp, blk ^ s),
+            device_id_type=MESH,
+        )
+
+    own = pltpu.make_async_copy(g_any.at[blk], gs_any.at[0], osem)
+
+    @pl.when(h == 0)
+    def _():
+        greet([(dp, blk ^ s) for s in range(1, n_blk)])
+        own.start()
+        for s in range(1, n_blk):
+            copy(s).start()
+
+    attend_kernel(n_blk, live_ref, q_ref, k_ref, v_ref, c_ref, p_ref, il_ref)
+
+    @pl.when(h == pl.num_programs(0) - 1)
+    def _():
+        own.wait()
+        for s in range(1, n_blk):
+            copy(s).wait()
+
+
 def ffn_kernel(n_blk, *refs):
-    xs = refs[:n_blk]
-    gs = refs[n_blk : 2 * n_blk]
-    (ct_ref, il_ref, wo_ref, bo_ref, gain_ref, bias_ref, win_ref, bin_ref, wout_ref, bout_ref) = refs[
-        2 * n_blk : 2 * n_blk + 10
-    ]
-    rest = refs[2 * n_blk + 10 :]
+    x_ref, g = refs[:2]
+    (ct_ref, il_ref, wo_ref, bo_ref, gain_ref, bias_ref, win_ref, bin_ref, wout_ref, bout_ref) = refs[2:12]
+    rest = refs[12:]
     outs = rest[:n_blk]
     (gwout_ref, gwin_ref, gbin_ref, dmid_ref, dot_ref, gwo_ref, vec_ref) = rest[n_blk : n_blk + 7]
-    mid, n2, n2t, g, acc_o, acc_d, act, dpre = rest[n_blk + 7 :]
-    tok = xs[0].shape[0]
+    mid, n2, n2t, acc_o, acc_d, act, dpre = rest[n_blk + 7 :]
+    tok = outs[0].shape[0]
     j = pl.program_id(0)
 
     @pl.when(j == 0)
     def _():
         for s in range(n_blk):
             sl = slice(s * tok, (s + 1) * tok)
-            m = xs[s][...].astype(F32) + dot(ct_ref[:, sl], wo_ref[...], TN) + bo_ref[...]
+            m = x_ref[sl].astype(F32) + dot(ct_ref[:, sl], wo_ref[...], TN) + bo_ref[...]
             mid[sl] = m
             acc_o[sl] = m + bout_ref[...]
             acc_d[sl] = jnp.zeros_like(m)
@@ -132,7 +224,6 @@
             nb = (n * gain_ref[...] + bias_ref[...]).astype(BF16)
             n2[sl] = nb
             n2t[:, sl] = nb.T
-            g[sl] = gs[s][...]
 
     bin_grad = None
     for s in range(n_blk):
@@ -197,18 +288,16 @@
     dk_ref[...] = (dot(ds[...], q_ref[...], NT) * LN2).T.astype(BF16)
 
 
-def input_kernel(n_blk, *refs):
-    xs = refs[:n_blk]
-    dmid_ref, gain_ref, dq_ref, dk_ref, dv_ref, wq_ref, wk_ref, wv_ref = refs[n_blk : n_blk + 8]
-    outs = refs[n_blk + 8 : 2 * n_blk + 8]
-    vec_ref = refs[2 * n_blk + 8]
-    tok = xs[0].shape[0]
+def input_kernel(n_blk, x_ref, dmid_ref, gain_ref, dq_ref, dk_ref, dv_ref, wq_ref, wk_ref, wv_ref, *rest):
+    outs = rest[:n_blk]
+    vec_ref = rest[n_blk]
+    tok = outs[0].shape[0]
     sums = [None] * 2
     for s in range(n_blk):
         sl = slice(s * tok, (s + 1) * tok)
         et = dot(wq_ref[...], dq_ref[:, sl]) + dot(wk_ref[...], dk_ref[:, sl]) + dot(wv_ref[...], dv_ref[:, sl])
         e = et.T
-        n, rstd = center(xs[s][...].astype(F32))
+        n, rstd = center(x_ref[sl].astype(F32))
         f = e * gain_ref[...]
         dx = dmid_ref[sl] + rstd * (
             f - jnp.mean(f, axis=-1, keepdims=True) - n * jnp.mean(f * n, axis=-1, keepdims=True)
@@ -266,10 +355,6 @@
     def swap(v, s):
         return lax.ppermute(v, "blk", [(i, i ^ s) for i in range(n_blk)])
 
-    def spread(v):
-        pick = [lax.dynamic_index_in_dim(v, blk ^ s, 0, keepdims=False) for s in range(n_blk)]
-        return [pick[0]] + [swap(pick[s], s) for s in range(1, n_blk)]
-
     def collect(pieces):
         back = [pieces[0]] + [swap(pieces[s], s) for s in range(1, n_blk)]
         out = jnp.zeros((n_seq, tok, width), BF16)
@@ -280,10 +365,6 @@
     row = lambda v: v.astype(F32).reshape(1, -1)
     column = lambda v: v.astype(F32).reshape(-1, 1)
 
-    xs = spread(inputs)
-    tied = lax.optimization_barrier((out_grad, xs))
-    gs = spread(tied[0])
-    xs = tied[1]
     live = ((blk ^ jnp.arange(n_blk)) * tok < lengths[blk]).astype(jnp.int32).reshape(1, n_blk)
 
     sds = jax.ShapeDtypeStruct
@@ -292,38 +373,59 @@
     n_col = 3
     cols = width // n_col
     strip = pl.BlockSpec((cols, seq), lambda j: (j, 0))
-    nt, qt, kt, vt = pl.pallas_call(
-        functools.partial(qkv_kernel, scale * LOG2E, n_blk),
-        grid=(n_col,),
-        in_specs=[piece] * n_blk
-        + [full((1, width))] * 2
-        + [pl.BlockSpec((width, cols), lambda j: (0, j)), pl.BlockSpec((cols, 1), lambda j: (j, 0))]
-        + [pl.BlockSpec((width, cols), lambda j: (0, j))] * 2
-        + [pl.BlockSpec((cols, 1), lambda j: (j, 0))],
-        out_specs=[wide, strip, strip, strip],
-        out_shape=[sds((width, seq), BF16)] * 4,
-        compiler_params=params(),
+    anywhere = pl.BlockSpec(memory_space=pl.ANY)
+    vmem = pl.BlockSpec(memory_space=pltpu.VMEM)
+    xs, nt, qt, kt, vt = pl.pallas_call(
+        functools.partial(qkv_spread_kernel, scale * LOG2E, n_blk),
+        in_specs=[anywhere, vmem, vmem, anywhere, vmem, anywhere, anywhere, vmem],
+        out_specs=[anywhere] * 5,
+        out_shape=[sds((n_blk, tok, width), BF16)] + [sds((width, seq), BF16)] * 4,
+        scratch_shapes=[
+            pltpu.VMEM((n_blk, tok, width), BF16),
+            pltpu.VMEM((3, width, width), BF16),
+            pltpu.VMEM((3, width, width), BF16),
+            pltpu.VMEM((width, seq), BF16),
+            pltpu.VMEM((3, width, seq), BF16),
+            pltpu.SemaphoreType.DMA((n_blk - 1,)),
+            pltpu.SemaphoreType.DMA((n_blk - 1,)),
+            pltpu.SemaphoreType.DMA((3,)),
+            pltpu.SemaphoreType.DMA((n_blk, 5)),
+            pltpu.SemaphoreType.DMA,
+        ],
+        compiler_params=params(collective_id=0, has_side_effects=True),
+        cost_estimate=cost(3 * seq * width * width, 14 * seq * width),
         name="qkv",
-    )(*xs, row(ln1_gain), row(ln1_bias), w_query, column(b_query), w_key, w_value, column(b_value))
+    )(inputs, row(ln1_gain), row(ln1_bias), w_query, column(b_query), w_key, w_value, column(b_value))
 
     per_head = pl.BlockSpec((head, seq), lambda h: (h, 0))
     per_square = pl.BlockSpec((1, seq, seq), lambda h: (h, 0, 0))
-    ct, probs, inv_total = pl.pallas_call(
-        functools.partial(attend_kernel, n_blk),
+    ct, probs, inv_total, gs = pl.pallas_call(
+        functools.partial(attend_spread_kernel, n_blk),
         grid=(H,),
-        in_specs=[pl.BlockSpec(memory_space=pltpu.SMEM), per_head, per_head, per_head],
-        out_specs=[per_head, per_square, pl.BlockSpec((1, 1, seq), lambda h: (h, 0, 0))],
-        out_shape=[sds((width, seq), BF16), sds((H, seq, seq), BF16), sds((H, 1, seq), F32)],
-        compiler_params=params(),
+        in_specs=[pl.BlockSpec(memory_space=pltpu.SMEM), per_head, per_head, per_head, anywhere],
+        out_specs=[per_head, per_square, pl.BlockSpec((1, 1, seq), lambda h: (h, 0, 0)), anywhere],
+        out_shape=[
+            sds((width, seq), BF16),
+            sds((H, seq, seq), BF16),
+            sds((H, 1, seq), F32),
+            sds((n_blk, tok, width), BF16),
+        ],
+        scratch_shapes=[
+            pltpu.SemaphoreType.DMA((n_blk - 1,)),
+            pltpu.SemaphoreType.DMA((n_blk - 1,)),
+            pltpu.SemaphoreType.DMA,
+        ],
+        compiler_params=params(collective_id=1, has_side_effects=True),
+        cost_estimate=cost(8 * seq * seq * width, 2 * H * seq * seq, H * seq * seq),
         name="attend",
-    )(live, qt, kt, vt)
-
-    n_tile = 12
+    )(live, qt, kt, vt, out_grad)
+
+    n_tile = 4
     tile = hidden // n_tile
     result = pl.pallas_call(
         functools.partial(ffn_kernel, n_blk),
         grid=(n_tile,),
-        in_specs=[piece] * (2 * n_blk)
+        in_specs=[full((seq, width))] * 2
         + [
             wide,
             full((H, 1, seq)),
@@ -360,17 +462,17 @@
             pltpu.VMEM((seq, width), F32),
             pltpu.VMEM((seq, width), BF16),
             pltpu.VMEM((width, seq), BF16),
-            pltpu.VMEM((seq, width), BF16),
             pltpu.VMEM((seq, width), F32),
             pltpu.VMEM((seq, width), F32),
             pltpu.VMEM((seq, tile), BF16),
             pltpu.VMEM((seq, tile), BF16),
         ],
         compiler_params=params(),
+        cost_estimate=cost(8 * seq * width * hidden, 8 * width * hidden),
         name="ffn",
     )(
-        *xs,
-        *gs,
+        xs.reshape(seq, width),
+        gs.reshape(seq, width),
         ct,
         inv_total,
         w_output,
@@ -423,19 +525,21 @@
         out_shape=[sds((width, seq), BF16)] * 3,
         scratch_shapes=[pltpu.VMEM((seq, seq), BF16)],
         compiler_params=params(),
+        cost_estimate=cost(10 * seq * seq * width, 2 * H * seq * seq),
         name="attend_back",
     )(probs, qt, kt, vt, dct, ct)
 
     result = pl.pallas_call(
         functools.partial(input_kernel, n_blk),
-        in_specs=[piece] * n_blk
-        + [full((seq, width)), full((1, width)), wide, wide, wide]
+        in_specs=[full((seq, width))] * 2
+        + [full((1, width)), wide, wide, wide]
         + [full((width, width))] * 3,
         out_specs=[piece] * n_blk + [full((8, width))],
         out_shape=[sds((tok, width), BF16)] * n_blk + [sds((8, width), F32)],
         compiler_params=params(),
+        cost_estimate=cost(3 * seq * width * width, 14 * seq * width),
         name="input_grad",
-    )(*xs, dmid, row(ln1_gain), dqt, dkt, dvt, w_query, w_key, w_value)
+    )(xs.reshape(seq, width), dmid, row(ln1_gain), dqt, dkt, dvt, w_query, w_key, w_value)
     input_grad = collect(result[:n_blk])
     vec1 = result[n_blk]
 
@@ -447,6 +551,7 @@
         out_specs=[col, col, col, pl.BlockSpec((8, cols), lambda j: (0, j))],
         out_shape=[sds((width, width), BF16)] * 3 + [sds((8, width), F32)],
         compiler_params=params(),
+        cost_estimate=cost(3 * seq * width * width, 14 * seq * width),
         name="qkv_grad",
     )(nt, dqt, dkt, dvt)
     s_wq = scatter(g_wq, (0, 1, 2, 3, 4), BF16)

time: 338 us -> 342 us (1.012)
  other arithmetic: 18.2 us -> 86.8 us
  local copies, waits for them, and re-layouts: 91.9 us -> 35.8 us
  waiting for transfers between devices: 103 us -> 80.7 us
  Pallas kernels: 70.9 us -> 91.7 us
  starting transfers between devices: 52 us -> 43.8 us
    pallas_call x2 -> x1, local copies, waits for them, and re-layouts: 59.1 us -> 0.51 us  [body(): pl.pallas_call(functools.partial(ffn_kernel, n_blk), grid=(n_tile,), in_s...]
    pallas_call x1 -> x2, other arithmetic: 0.68 us -> 56.2 us  [body(): pl.pallas_call(functools.partial(ffn_kernel, n_blk), grid=(n_tile,), in_s...]
    ppermute x12 -> x6, waiting for transfers between devices: 50.4 us -> 19.7 us  [swap(): return lax.ppermute(v, 'blk', [(i, i ^ s) for i in range(n_blk)])]
    pallas_call x2, Pallas kernels: 32.8 us -> 53.8 us  [the longest x1 27.2 us: body(): pl.pallas_call(functools.partial(qkv_spread_kernel, scale * LOG2E, n_blk)...]
    pallas_call x1 -> x0, local copies, waits for them, and re-layouts: 10.1 us -> none  [body(): pl.pallas_call(functools.partial(input_kernel, n_blk), in_specs=[piece] *...]
    pallas_call x0 -> x1, other arithmetic: none -> 9.49 us  [body(): pl.pallas_call(functools.partial(input_kernel, n_blk), in_specs=[full((se...]
    ppermute x35, waiting for transfers between devices: 52.3 us -> 61 us  [scatter(): lax.ppermute(send.astype(wire), ('dp', 'blk'), [(i, i ^ 1 << b) for i in...]
    ppermute x12 -> x6, starting transfers between devices: 10.1 us -> 2.73 us  [swap(): return lax.ppermute(v, 'blk', [(i, i ^ s) for i in range(n_blk)])]
  transfers between devices with their start and end apart: 47 -> 41, of which waited for: 22 -> 18; matrix products, arithmetic and copies ran while one was open for 12% -> 14% of each run, Pallas kernels for 21% -> 11%
where the time goes in v2:
time: 342 us; the launch traced here: 340 us
  Pallas kernels  91.7 us (27%)
  other arithmetic  86.8 us (25%)
  waiting for transfers between devices  80.7 us (24%)
  starting transfers between devices  43.8 us (13%)
  local copies, waits for them, and re-layouts  35.8 us (10%)
    ppermute x35, waiting for transfers between devices, scatter(): lax.ppermute(send.astype(wire), ('dp', 'blk'), [(i, i ^ 1 << b) for i in...  61 us
    pallas_call x2, other arithmetic, body(): pl.pallas_call(functools.partial(ffn_kernel, n_blk), grid=(n_tile,), in_s...  56.2 us
    ppermute x35, starting transfers between devices, scatter(): lax.ppermute(send.astype(wire), ('dp', 'blk'), [(i, i ^ 1 << b) for i in...  41.1 us
    pallas_call x1, Pallas kernels, body(): pl.pallas_call(functools.partial(attend_back_kernel, scale), grid=(H,), i...  29.9 us
    pallas_call x1, Pallas kernels, body(): pl.pallas_call(functools.partial(qkv_spread_kernel, scale * LOG2E, n_blk)...  27.2 us
    pallas_call x1, Pallas kernels, body(): pl.pallas_call(functools.partial(attend_spread_kernel, n_blk), grid=(H,),...  26.6 us
    ppermute x6, waiting for transfers between devices, swap(): return lax.ppermute(v, 'blk', [(i, i ^ s) for i in range(n_blk)])  19.7 us
    convert_element_type x24, other arithmetic, scatter(): send.astype(wire)  11.6 us
  transfers between devices with their start and end apart: 41, of which 18 were waited for; matrix products, arithmetic and copies ran while one was open for 14% of the time, Pallas kernels for 11%

profile of v2, /device:TPU:0, one launch (start us, length us, event | category | flops | bytes accessed | tf_op | source)
XLA Modules:
  0.0 340.2 jit_solution(493385213444692690)
XLA Ops:
  12.2 27.2 %qkv.1 = (bf16[4,256,768]{2,1,0:T(8,128)(2,1)}, bf16[768,1024]{1,0:T(8,128)(2,1)}, bf16[768,1024]{1,0:T(8,128)(2,1)}, bf16[768,1024]{1,0:T(8,128)(2,1)}, bf16[768,1024]{1,0:T(8,128)(2,1)}) custom-call(bf16[4,256,768]{2,1,0:T(8,128)(2,1)} %x_any.1, f32[1,768]{1,0:T(1,128)} %reshape.894.gain, f32[1,768]{1,0:T(1,128)} %reshape.896.bias, ...), custom_call_target="tpu_custom_call" | custom-call | flops 3623878656 | bytes 11010048 | tf_op jit(solution)/shard_map/qkv/pallas_call | solution.py:378
  39.4 26.6 %attend.1 = (bf16[768,1024]{1,0:T(8,128)(2,1)}, bf16[12,1024,1024]{2,1,0:T(8,128)(2,1)}, f32[12,1,1024]{2,1,0:T(1,128)}, bf16[4,256,768]{2,1,0:T(8,128)(2,1)}) custom-call(s32[1,4]{1,0:T(1,128)} %compare_convert_fusion.live_ref, bf16[768,1024]{1,0:T(8,128)(2,1)} %get-tuple-element.50.q_ref, bf16[768,1024]{1,0:T(8,128)(2,1)} %get-tuple-element.51.k_ref, ...), custom_call_target="tpu_custom_call" | custom-call | flops 12884901888 | bytes 25165824 | tf_op jit(solution)/shard_map/attend/pallas_call | solution.py:402
  67.2 55.6 %ffn.1 = (bf16[4,256,768]{2,1,0:T(8,128)(2,1)}, bf16[256,768]{1,0:T(8,128)(2,1)}, bf16[256,768]{1,0:T(8,128)(2,1)}, bf16[256,768]{1,0:T(8,128)(2,1)}, f32[1024,7...) fusion(bf16[4,256,768]{2,1,0:T(8,128)(2,1)} %broadcast.27.clone, ...), kind=kCustom, calls=%fused_computation.39 | custom fusion | flops 38654705664 | bytes 32354308 | tf_op jit(solution)/shard_map/ffn/pallas_call | solution.py:425
  125.8 29.9 %attend_back.1 = (bf16[768,1024]{1,0:T(8,128)(2,1)}, bf16[768,1024]{1,0:T(8,128)(2,1)}, bf16[768,1024]{1,0:T(8,128)(2,1)}) custom-call(bf16[12,1024,1024]{2,1,0:T(8,128)(2,1)} %get-tuple-element.61.p_ref, bf16[768,1024]{1,0:T(8,128)(2,1)} %get-tuple-element.50.q_ref, bf16[768,1024]{1,0:T(8,128)(2,1)} %get-tuple-element.51.k_ref, ...), custom_call_target="tpu_custom_call" | custom-call | flops 16106127360 | bytes 25165824 | tf_op jit(solution)/shard_map/attend_back/pallas_call | solution.py:520
  155.7 8.1 %qkv_grad.1 = (bf16[768,768]{1,0:T(8,128)(2,1)}, bf16[768,768]{1,0:T(8,128)(2,1)}, bf16[768,768]{1,0:T(8,128)(2,1)}, f32[8,768]{1,0:T(8,128)}) custom-call(bf16[768,1024]{1,0:T(8,128)(2,1)} %get-tuple-element.71.nt_ref, bf16[768,1024]{1,0:T(8,128)(2,1)} %get-tuple-element.63.dq_ref, bf16[768,1024]{1,0:T(8,128)(2,1)} %get-tuple-element.64.dk_ref, ...), custom_call_target="tpu_custom_call" | custom-call | flops 3623878656 | bytes 11010048 | tf_op jit(solution)/shard_map/qkv_grad/pallas_call | solution.py:547
  166.2 9.5 %input_grad.1 = (bf16[4,256,768]{2,1,0:T(8,128)(2,1)S(1)}, bf16[256,768]{1,0:T(8,128)(2,1)}, bf16[256,768]{1,0:T(8,128)(2,1)}, bf16[256,768]{1,0:T(8,128)(2,1)}, f32[8,768]{1,0:T(8,128)S(1)}) fusion(bf16[4,256,768]{2,1,0:T(8,128)(2,1)S(1)} %broadcast.27, s32[]{:T(128)S(6)} %select_n.291, bf16[1024,768]{1,0:T(8,128)(2,1)S(1)} %bitcast.665, ...), kind=kCustom, calls=%fused_computation.35 | custom fusion | flops 3623878656 | bytes 14576644 | tf_op jit(solution)/shard_map/input_grad/pallas_call | solution.py:532
  185.2 8.4 %collective-permute-done.7 = f32[2,2,2,1,288]{4,3,2,1,0:T(1,128)S(1)} collective-permute-done((f32[2,2,2,1,288]{4,3,2,1,0:T(1,128)S(1)}, f32[2,2,2,1,288]{4,3,2,1,0:T(1,128)S(1)}, u32[]{:S(2)}, u32[]{:S(2)}) %collective-permute-start.7) | collective-permute-done | bytes 9248 | tf_op jit(solution)/shard_map/ppermute | solution.py:508
  201.6 2.6 collective-permute-start.10
  213.1 7.3 %collective-permute-done.1 = bf16[256,768]{1,0:T(8,128)(2,1)S(1)} collective-permute-done((bf16[256,768]{1,0:T(8,128)(2,1)}, bf16[256,768]{1,0:T(8,128)(2,1)S(1)}, u32[]{:S(2)}, u32[]{:S(2)}) %collective-permute-start.1) | collective-permute-done | bytes 393248 | tf_op jit(solution)/shard_map/ppermute | solution.py:356
  223.1 4.9 %collective-permute-done.5 = bf16[256,768]{1,0:T(8,128)(2,1)S(1)} collective-permute-done((bf16[256,768]{1,0:T(8,128)(2,1)S(1)}, bf16[256,768]{1,0:T(8,128)(2,1)S(1)}, u32[]{:S(2)}, u32[]{:S(2)}) %collective-permute-start.5) | collective-permute-done | bytes 393248 | tf_op jit(solution)/shard_map/ppermute | solution.py:356
  229.0 7.5 %collective-permute-done.2 = bf16[256,768]{1,0:T(8,128)(2,1)S(1)} collective-permute-done((bf16[256,768]{1,0:T(8,128)(2,1)S(1)}, bf16[256,768]{1,0:T(8,128)(2,1)S(1)}, u32[]{:S(2)}, u32[]{:S(2)}) %collective-permute-start.2) | collective-permute-done | bytes 393248 | tf_op jit(solution)/shard_map/ppermute | solution.py:356
  242.8 5.8 %collective-permute-done.27 = bf16[2,2,2,24,768]{4,3,2,1,0:T(8,128)(2,1)S(1)} collective-permute-done((bf16[2,2,2,24,768]{4,3,2,1,0:T(8,128)(2,1)S(1)}, bf16[2,2,2,24,768]{4,3,2,1,0:T(8,128)(2,1)S(1)}, u32[]{:S(2)}, u32[]{:S(2)}) %collective-permute-start.27) | collective-permute-done | bytes 294944 | tf_op jit(solution)/shard_map/ppermute | solution.py:508
  249.1 5.1 %collective-permute-done.22 = bf16[2,2,2,24,768]{4,3,2,1,0:T(8,128)(2,1)S(1)} collective-permute-done((bf16[2,2,2,24,768]{4,3,2,1,0:T(8,128)(2,1)S(1)}, bf16[2,2,2,24,768]{4,3,2,1,0:T(8,128)(2,1)S(1)}, u32[]{:S(2)}, u32[]{:S(2)}) %collective-permute-start.22) | collective-permute-done | bytes 294944 | tf_op jit(solution)/shard_map/ppermute | solution.py:508
  254.2 2.6 collective-permute-start.28
  264.9 3.0 collective-permute-done.28
  270.5 2.1 collective-permute-done.18
  273.5 17.7 %collective-permute-done.13 = bf16[2,2,24,768]{3,2,0,1:T(8,128)(2,1)S(1)} collective-permute-done((bf16[2,2,24,768]{3,2,0,1:T(8,128)(2,1)S(1)}, bf16[2,2,24,768]{3,2,0,1:T(8,128)(2,1)S(1)}, u32[]{:S(2)}, u32[]{:S(2)}) %collective-permute-start.13) | collective-permute-done | bytes 147488 | tf_op jit(solution)/shard_map/ppermute | solution.py:508
  291.2 2.6 collective-permute-start.19
  299.8 2.5 collective-permute-start.15
  308.4 6.4 %collective-permute-done.38 = bf16[2,2,96,768]{3,2,0,1:T(8,128)(2,1)S(1)} collective-permute-done((bf16[2,2,96,768]{3,2,0,1:T(8,128)(2,1)S(1)}, bf16[2,2,96,768]{3,2,0,1:T(8,128)(2,1)S(1)}, u32[]{:S(2)}, u32[]{:S(2)}) %collective-permute-start.38) | collective-permute-done | bytes 589856 | tf_op jit(solution)/shard_map/ppermute | solution.py:508
  316.0 2.3 collective-permute-start.39
  320.5 4.4 %collective-permute-done.39 = bf16[2,96,768]{2,1,0:T(8,128)(2,1)S(1)} collective-permute-done((bf16[2,96,768]{2,1,0:T(8,128)(2,1)S(1)}, bf16[2,96,768]{2,1,0:T(8,128)(2,1)S(1)}, u32[]{:S(2)}, u32[]{:S(2)}) %collective-permute-start.39) | collective-permute-done | bytes 294944 | tf_op jit(solution)/shard_map/ppermute | solution.py:508
  327.0 2.6 collective-permute-done.34
  333.9 4.4 %collective-permute-done.35 = bf16[24,3072]{1,0:T(8,128)(2,1)S(1)} collective-permute-done((bf16[24,3072]{1,0:T(8,128)(2,1)S(1)}, bf16[24,3072]{1,0:T(8,128)(2,1)S(1)}, u32[]{:S(2)}, u32[]{:S(2)}) %collective-permute-start.35) | collective-permute-done | bytes 147488 | tf_op jit(solution)/shard_map/ppermute | solution.py:508
  (184 shorter events, 90.1 us)
Async XLA Ops:
  125.6 131.3 %collective-permute-start.36 = (bf16[2,2,2,2,96,768]{5,4,3,2,1,0:T(8,128)(2,1)}, bf16[2,2,2,2,96,768]{5,4,3,2,1,0:T(8,128)(2,1)}, u32[]{:S(2)}, u32[]{:S(2)}) collective-permute-start(bf16[2,2,2,2,96,768]{5,4,3,2,1,0:T(8,128)(2,1)} %dynamic-slice_bitcast_fusion), channel_id=1, source_target_pairs={{0,1},{1,0},{2,3},{3,2},{4,5},{5,4},{6,7},{7,6},{8,9},{9,8},{10,11... | collective-permute-start | bytes 7077896 | tf_op jit(solution)/shard_map/ppermute | solution.py:508
  181.4 77.8 %collective-permute-start.31 = (bf16[2,2,2,2,24,3072]{5,4,3,2,1,0:T(8,128)(2,1)S(1)}, bf16[2,2,2,2,24,3072]{5,4,3,2,1,0:T(8,128)(2,1)}, u32[]{:S(2)}, u32[]{:S(2)}) collective-permute-start(bf16[2,2,2,2,24,3072]{5,4,3,2,1,0:T(8,128)(2,1)S(1)} %dynamic-slice_bitcast_fusion.1), channel_id=1, source_target_pairs={{0,1},{1,0},{2,3},{3,2},{4,5},{5,4},{6,7},{7,6},{8,9},{9,8},{10,11... | collective-permute-start | bytes 7077896 | tf_op jit(solution)/shard_map/ppermute | solution.py:508
  181.6 26.7 %collective-permute-start.3 = (bf16[256,768]{1,0:T(8,128)(2,1)}, bf16[256,768]{1,0:T(8,128)(2,1)}, u32[]{:S(2)}, u32[]{:S(2)}) collective-permute-start(bf16[256,768]{1,0:T(8,128)(2,1)} %get-tuple-element.114), channel_id=1, source_target_pairs={{0,1},{1,0},{2,3},{3,2},{4,5},{5,4},{6,7},{7,6},{8,9},{9,8},{10,11... | collective-permute-start | bytes 1179656 | tf_op jit(solution)/shard_map/ppermute | solution.py:356
  182.0 29.7 %collective-permute-start.4 = (bf16[256,768]{1,0:T(8,128)(2,1)}, bf16[256,768]{1,0:T(8,128)(2,1)}, u32[]{:S(2)}, u32[]{:S(2)}) collective-permute-start(bf16[256,768]{1,0:T(8,128)(2,1)} %get-tuple-element.116), channel_id=1, source_target_pairs={{0,2},{1,3},{2,0},{3,1},{4,6},{5,7},{6,4},{7,5},{8,10},{9,11},{10,... | collective-permute-start | bytes 1179656 | tf_op jit(solution)/shard_map/ppermute | solution.py:356
  182.4 11.2 %collective-permute-start.7 = (f32[2,2,2,1,288]{4,3,2,1,0:T(1,128)S(1)}, f32[2,2,2,1,288]{4,3,2,1,0:T(1,128)S(1)}, u32[]{:S(2)}, u32[]{:S(2)}) collective-permute-start(f32[2,2,2,1,288]{4,3,2,1,0:T(1,128)S(1)} %fusion.72), channel_id=1, source_target_pairs={{0,2},{1,3},{2,0},{3,1},{4,6},{5,7},{6,4},{7,5},{8,10},{9,11},{10,... | collective-permute-start | bytes 27656 | tf_op jit(solution)/shard_map/ppermute | solution.py:508
  208.3 12.1 %collective-permute-start.1 = (bf16[256,768]{1,0:T(8,128)(2,1)}, bf16[256,768]{1,0:T(8,128)(2,1)S(1)}, u32[]{:S(2)}, u32[]{:S(2)}) collective-permute-start(bf16[256,768]{1,0:T(8,128)(2,1)} %get-tuple-element.94), channel_id=1, source_target_pairs={{0,2},{1,3},{2,0},{3,1},{4,6},{5,7},{6,4},{7,5},{8,10},{9,11},{10,... | collective-permute-start | bytes 1179656 | tf_op jit(solution)/shard_map/ppermute | solution.py:356
  210.7 26.8 %collective-permute-start.26 = (bf16[2,2,2,2,24,768]{5,4,3,2,1,0:T(8,128)(2,1)S(1)}, bf16[2,2,2,2,24,768]{5,4,3,2,1,0:T(8,128)(2,1)S(1)}, u32[]{:S(2)}, u32[]{:S(2)}) collective-permute-start(bf16[2,2,2,2,24,768]{5,4,3,2,1,0:T(8,128)(2,1)S(1)} %dynamic-slice_bitcast_fusion.2), channel_id=1, source_target_pairs={{0,1},{1,0},{2,3},{3,2},{4,5},{5,4},{6,7},{7,6},{8,9},{9,8},{10,11... | collective-permute-start | bytes 1769480 | tf_op jit(solution)/shard_map/ppermute | solution.py:508
  211.7 16.4 %collective-permute-start.5 = (bf16[256,768]{1,0:T(8,128)(2,1)S(1)}, bf16[256,768]{1,0:T(8,128)(2,1)S(1)}, u32[]{:S(2)}, u32[]{:S(2)}) collective-permute-start(bf16[256,768]{1,0:T(8,128)(2,1)S(1)} %copy-done.10), channel_id=1, source_target_pairs={{0,3},{1,2},{2,1},{3,0},{4,7},{5,6},{6,5},{7,4},{8,11},{9,10},{10,... | collective-permute-start | bytes 1179656 | tf_op jit(solution)/shard_map/ppermute | solution.py:356
  220.5 16.0 %collective-permute-start.2 = (bf16[256,768]{1,0:T(8,128)(2,1)S(1)}, bf16[256,768]{1,0:T(8,128)(2,1)S(1)}, u32[]{:S(2)}, u32[]{:S(2)}) collective-permute-start(bf16[256,768]{1,0:T(8,128)(2,1)S(1)} %copy-done.14), channel_id=1, source_target_pairs={{0,3},{1,2},{2,1},{3,0},{4,7},{5,6},{6,5},{7,4},{8,11},{9,10},{10,... | collective-permute-start | bytes 1179656 | tf_op jit(solution)/shard_map/ppermute | solution.py:356
  228.0 10.6 %collective-permute-start.21 = (bf16[2,2,2,2,24,768]{5,4,3,2,1,0:T(8,128)(2,1)S(1)}, bf16[2,2,2,2,24,768]{5,4,3,2,1,0:T(8,128)(2,1)S(1)}, u32[]{:S(2)}, u32[]{:S(2)}) collective-permute-start(bf16[2,2,2,2,24,768]{5,4,3,2,1,0:T(8,128)(2,1)S(1)} %copy-done.7), channel_id=1, source_target_pairs={{0,1},{1,0},{2,3},{3,2},{4,5},{5,4},{6,7},{7,6},{8,9},{9,8},{10,11... | collective-permute-start | bytes 1769480 | tf_op jit(solution)/shard_map/ppermute | solution.py:508
  240.4 13.9 %collective-permute-start.22 = (bf16[2,2,2,24,768]{4,3,2,1,0:T(8,128)(2,1)S(1)}, bf16[2,2,2,24,768]{4,3,2,1,0:T(8,128)(2,1)S(1)}, u32[]{:S(2)}, u32[]{:S(2)}) collective-permute-start(bf16[2,2,2,24,768]{4,3,2,1,0:T(8,128)(2,1)S(1)} %fusion.7), channel_id=1, source_target_pairs={{0,8},{1,9},{2,10},{3,11},{4,12},{5,13},{6,14},{7,15},{8,0},{9,1},... | collective-permute-start | bytes 884744 | tf_op jit(solution)/shard_map/ppermute | solution.py:508
  241.1 20.4 %collective-permute-start.17 = (bf16[2,2,2,24,768]{4,3,2,1,0:T(8,128)(2,1)S(1)}, bf16[2,2,2,24,768]{4,3,2,1,0:T(8,128)(2,1)S(1)}, u32[]{:S(2)}, u32[]{:S(2)}) collective-permute-start(bf16[2,2,2,24,768]{4,3,2,1,0:T(8,128)(2,1)S(1)} %fusion.8), channel_id=1, source_target_pairs={{0,4},{1,5},{2,6},{3,7},{4,0},{5,1},{6,2},{7,3},{8,12},{9,13},{10,... | collective-permute-start | bytes 884744 | tf_op jit(solution)/shard_map/ppermute | solution.py:508
  248.6 14.6 %collective-permute-start.12 = (bf16[2,2,2,24,768]{4,3,2,1,0:T(8,128)(2,1)S(1)}, bf16[2,2,2,24,768]{4,3,2,1,0:T(8,128)(2,1)S(1)}, u32[]{:S(2)}, u32[]{:S(2)}) collective-permute-start(bf16[2,2,2,24,768]{4,3,2,1,0:T(8,128)(2,1)S(1)} %fusion.9), channel_id=1, source_target_pairs={{0,2},{1,3},{2,0},{3,1},{4,6},{5,7},{6,4},{7,5},{8,10},{9,11},{10,... | collective-permute-start | bytes 884744 | tf_op jit(solution)/shard_map/ppermute | solution.py:508
  254.2 13.7 %collective-permute-start.28 = (bf16[2,2,24,768]{3,2,0,1:T(8,128)(2,1)S(1)}, bf16[2,2,24,768]{3,2,0,1:T(8,128)(2,1)S(1)}, u32[]{:S(2)}, u32[]{:S(2)}) collective-permute-start(bf16[2,2,24,768]{3,2,0,1:T(8,128)(2,1)S(1)} %copy.82), channel_id=1, source_target_pairs={{0,16},{1,17},{2,18},{3,19},{4,20},{5,21},{6,22},{7,23},{8,24},{9,... | collective-permute-start | bytes 442376 | tf_op jit(solution)/shard_map/ppermute | solution.py:508
  256.9 13.0 %collective-permute-start.23 = (bf16[2,2,24,768]{3,2,0,1:T(8,128)(2,1)S(1)}, bf16[2,2,24,768]{3,2,0,1:T(8,128)(2,1)S(1)}, u32[]{:S(2)}, u32[]{:S(2)}) collective-permute-start(bf16[2,2,24,768]{3,2,0,1:T(8,128)(2,1)S(1)} %copy.76), channel_id=1, source_target_pairs={{0,16},{1,17},{2,18},{3,19},{4,20},{5,21},{6,22},{7,23},{8,24},{9,... | collective-permute-start | bytes 442376 | tf_op jit(solution)/shard_map/ppermute | solution.py:508
  259.2 40.5 %collective-permute-start.37 = (bf16[2,2,2,96,768]{4,3,2,1,0:T(8,128)(2,1)S(1)}, bf16[2,2,2,96,768]{4,3,2,1,0:T(8,128)(2,1)S(1)}, u32[]{:S(2)}, u32[]{:S(2)}) collective-permute-start(bf16[2,2,2,96,768]{4,3,2,1,0:T(8,128)(2,1)S(1)} %fusion), channel_id=1, source_target_pairs={{0,2},{1,3},{2,0},{3,1},{4,6},{5,7},{6,4},{7,5},{8,10},{9,11},{10,... | collective-permute-start | bytes 3538952 | tf_op jit(solution)/shard_map/ppermute | solution.py:508
  261.5 42.3 %collective-permute-start.32 = (bf16[2,2,2,24,3072]{4,3,2,1,0:T(8,128)(2,1)S(1)}, bf16[2,2,2,24,3072]{4,3,2,1,0:T(8,128)(2,1)S(1)}, u32[]{:S(2)}, u32[]{:S(2)}) collective-permute-start(bf16[2,2,2,24,3072]{4,3,2,1,0:T(8,128)(2,1)S(1)} %fusion.1), channel_id=1, source_target_pairs={{0,4},{1,5},{2,6},{3,7},{4,0},{5,1},{6,2},{7,3},{8,12},{9,13},{10,... | collective-permute-start | bytes 3538952 | tf_op jit(solution)/shard_map/ppermute | solution.py:508
  267.9 23.3 %collective-permute-start.13 = (bf16[2,2,24,768]{3,2,0,1:T(8,128)(2,1)S(1)}, bf16[2,2,24,768]{3,2,0,1:T(8,128)(2,1)S(1)}, u32[]{:S(2)}, u32[]{:S(2)}) collective-permute-start(bf16[2,2,24,768]{3,2,0,1:T(8,128)(2,1)S(1)} %copy.67), channel_id=1, source_target_pairs={{0,4},{1,5},{2,6},{3,7},{4,0},{5,1},{6,2},{7,3},{8,12},{9,13},{10,... | collective-permute-start | bytes 442376 | tf_op jit(solution)/shard_map/ppermute | solution.py:508
  269.9 23.9 %collective-permute-start.29 = (bf16[2,24,768]{2,1,0:T(8,128)(2,1)S(1)}, bf16[2,24,768]{2,1,0:T(8,128)(2,1)S(1)}, u32[]{:S(2)}, u32[]{:S(2)}) collective-permute-start(bf16[2,24,768]{2,1,0:T(8,128)(2,1)S(1)} %fusion.18), channel_id=1, source_target_pairs={{0,2},{1,3},{2,0},{3,1},{4,6},{5,7},{6,4},{7,5},{8,10},{9,11},{10,... | collective-permute-start | bytes 221192 | tf_op jit(solution)/shard_map/ppermute | solution.py:508
  272.6 23.0 %collective-permute-start.24 = (bf16[2,24,768]{2,1,0:T(8,128)(2,1)S(1)}, bf16[2,24,768]{2,1,0:T(8,128)(2,1)S(1)}, u32[]{:S(2)}, u32[]{:S(2)}) collective-permute-start(bf16[2,24,768]{2,1,0:T(8,128)(2,1)S(1)} %fusion.19), channel_id=1, source_target_pairs={{0,2},{1,3},{2,0},{3,1},{4,6},{5,7},{6,4},{7,5},{8,10},{9,11},{10,... | collective-permute-start | bytes 221192 | tf_op jit(solution)/shard_map/ppermute | solution.py:508
  299.8 20.0 %collective-permute-start.15 = (bf16[24,768]{1,0:T(8,128)(2,1)S(1)}, bf16[24,768]{1,0:T(8,128)(2,1)S(1)}, u32[]{:S(2)}, u32[]{:S(2)}) collective-permute-start(bf16[24,768]{1,0:T(8,128)(2,1)S(1)} %fusion.28), channel_id=1, source_target_pairs={{0,16},{1,17},{2,18},{3,19},{4,20},{5,21},{6,22},{7,23},{8,24},{9,... | collective-permute-start | bytes 110600 | tf_op jit(solution)/shard_map/ppermute | solution.py:508
  303.8 10.9 %collective-permute-start.38 = (bf16[2,2,96,768]{3,2,0,1:T(8,128)(2,1)S(1)}, bf16[2,2,96,768]{3,2,0,1:T(8,128)(2,1)S(1)}, u32[]{:S(2)}, u32[]{:S(2)}) collective-permute-start(bf16[2,2,96,768]{3,2,0,1:T(8,128)(2,1)S(1)} %copy.96), channel_id=1, source_target_pairs={{0,4},{1,5},{2,6},{3,7},{4,0},{5,1},{6,2},{7,3},{8,12},{9,13},{10,... | collective-permute-start | bytes 1769480 | tf_op jit(solution)/shard_map/ppermute | solution.py:508
  305.8 12.5 %collective-permute-start.33 = (bf16[2,2,24,3072]{3,2,0,1:T(8,128)(2,1)S(1)}, bf16[2,2,24,3072]{3,2,0,1:T(8,128)(2,1)S(1)}, u32[]{:S(2)}, u32[]{:S(2)}) collective-permute-start(bf16[2,2,24,3072]{3,2,0,1:T(8,128)(2,1)S(1)} %copy.89), channel_id=1, source_target_pairs={{0,2},{1,3},{2,0},{3,1},{4,6},{5,7},{6,4},{7,5},{8,10},{9,11},{10,... | collective-permute-start | bytes 1769480 | tf_op jit(solution)/shard_map/ppermute | solution.py:508
  319.4 10.2 %collective-permute-start.34 = (bf16[2,24,3072]{2,1,0:T(8,128)(2,1)S(1)}, bf16[2,24,3072]{2,1,0:T(8,128)(2,1)S(1)}, u32[]{:S(2)}, u32[]{:S(2)}) collective-permute-start(bf16[2,24,3072]{2,1,0:T(8,128)(2,1)S(1)} %fusion.5), channel_id=1, source_target_pairs={{0,8},{1,9},{2,10},{3,11},{4,12},{5,13},{6,14},{7,15},{8,0},{9,1},... | collective-permute-start | bytes 884744 | tf_op jit(solution)/shard_map/ppermute | solution.py:508
  (35 other events, 359.7 us)

commit v3 on v2

--- a/solution.py
+++ b/solution.py
@@ -37,6 +37,10 @@
     return pl.BlockSpec(shape, lambda *_: (0,) * len(shape))
 
 
+def as_row(ref):
+    return ref[...].astype(F32)[None, :]
+
+
 def center(v):
     mean = jnp.mean(v, axis=-1, keepdims=True)
     cent = v - mean
@@ -51,11 +55,13 @@
     return phi, u * e * INV_SQRT_2PI
 
 
-def attend_kernel(n_blk, live_ref, q_ref, k_ref, v_ref, c_ref, p_ref, il_ref):
+def attend_kernel(n_blk, len_ref, q_ref, k_ref, v_ref, c_ref, p_ref, il_ref):
     seq = q_ref.shape[1]
     tok = seq // n_blk
+    blk = lax.axis_index("blk")
+    length = len_ref[blk]
     s = dot(k_ref[...].T, q_ref[...])
-    live = [live_ref[0, i] > 0 for i in range(n_blk)]
+    live = [(blk ^ i) * tok < length for i in range(n_blk)]
     m = None
     for i in range(n_blk):
         mi = jnp.max(s[i * tok : (i + 1) * tok], axis=0, keepdims=True)
@@ -138,6 +144,7 @@
     for i, load in enumerate(loads):
         load.wait()
         wt[i] = wbuf[i].T
+    cols = jnp.concatenate([as_row(bq), as_row(bv), jnp.zeros((6, width), F32)], axis=0).T
     writes = []
     for s in range(n_blk):
         if s == 0:
@@ -146,11 +153,11 @@
             copies[s].wait_recv()
         sl = slice(s * tok, (s + 1) * tok)
         n, _ = center(xbuf[s].astype(F32))
-        n = (n * gain[...] + bias[...]).astype(BF16).T
+        n = (n * as_row(gain) + as_row(bias)).astype(BF16).T
         nt[:, sl] = n
-        qkv[0, :, sl] = ((dot(wt[0], n) + bq[...]) * scale).astype(BF16)
+        qkv[0, :, sl] = ((dot(wt[0], n) + cols[:, :1]) * scale).astype(BF16)
         qkv[1, :, sl] = dot(wt[1], n).astype(BF16)
-        qkv[2, :, sl] = (dot(wt[2], n) + bv[...]).astype(BF16)
+        qkv[2, :, sl] = (dot(wt[2], n) + cols[:, 1:2]).astype(BF16)
         for i, (src, dst) in enumerate(
             (
                 (xbuf.at[s], xs_any.at[s]),
@@ -169,7 +176,7 @@
         write.wait()
 
 
-def attend_spread_kernel(n_blk, live_ref, q_ref, k_ref, v_ref, g_any, c_ref, p_ref, il_ref, gs_any, send, recv, osem):
+def attend_spread_kernel(n_blk, len_ref, q_ref, k_ref, v_ref, g_any, c_ref, p_ref, il_ref, gs_any, send, recv, osem):
     h = pl.program_id(0)
     dp = lax.axis_index("dp")
     blk = lax.axis_index("blk")
@@ -193,13 +200,170 @@
         for s in range(1, n_blk):
             copy(s).start()
 
-    attend_kernel(n_blk, live_ref, q_ref, k_ref, v_ref, c_ref, p_ref, il_ref)
+    attend_kernel(n_blk, len_ref, q_ref, k_ref, v_ref, c_ref, p_ref, il_ref)
 
     @pl.when(h == pl.num_programs(0) - 1)
     def _():
         own.wait()
         for s in range(1, n_blk):
             copy(s).wait()
+
+
+def regroup(v, share):
+    def slab(c, x, y):
+        at = [(z * 8 + y * 4 + x * 2 + c) * share for z in range(4)]
+        return jnp.concatenate([v[a : a + share] for a in at], axis=0)
+
+    return [[[slab(c, x, y) for y in range(2)] for x in range(2)] for c in range(2)]
+
+
+CXY = [(c, x, y) for c in range(2) for x in range(2) for y in range(2)]
+
+
+class Scatter:
+    def __init__(self, source, cols, share, first, out, bufs, place):
+        self.source, self.cols, self.share, self.out = source, cols, share, out
+        self.b = bufs
+        dp, blk = place
+        self.c, self.x, self.y, self.z = blk & 1, blk >> 1, dp & 1, dp >> 1
+        self.first = first
+        ids = {"x": (dp, blk ^ 2), "y": (dp ^ 1, blk)}
+        self.mp = self.x if first == "x" else self.y
+        self.mq = self.y if first == "x" else self.x
+        self.core_id = (dp, blk ^ 1)
+        self.p_id = ids[first]
+        self.q_id = ids["y" if first == "x" else "x"]
+        self.z_ids = [(((self.z + d) & 3) * 2 + self.y, blk) for d in (1, 2, 3)]
+        self.chunk = share if share % 16 == 0 else 2 * share
+
+    def remote(self, src, dst, i, where):
+        return pltpu.make_async_remote_copy(
+            src_ref=src,
+            dst_ref=dst,
+            send_sem=self.b["send"].at[i],
+            recv_sem=self.b["recv"].at[i],
+            device_id=where,
+            device_id_type=MESH,
+        )
+
+    def part(self, c):
+        if self.cols is None:
+            return self.source.at[c]
+        return self.source.at[c, :, :, :, self.cols]
+
+    def core_copy(self):
+        return self.remote(self.part(1 - self.c), self.b["r0"], 0, self.core_id)
+
+    def load(self):
+        return pltpu.make_async_copy(self.part(self.c), self.b["keep"], self.b["load"])
+
+    def p_copy(self):
+        return self.remote(self.b["t1"], self.b["r1"], 1, self.p_id)
+
+    def q_copy(self):
+        return self.remote(self.b["t2"], self.b["r2"], 2, self.q_id)
+
+    def z_copies(self):
+        return [self.remote(self.b["t3"].at[d], self.b["r3"].at[d], 3 + d, self.z_ids[d]) for d in range(3)]
+
+    def pick(self, ref, a, b, rows):
+        return (ref[a, b, rows] if self.first == "x" else ref[b, a, rows]).astype(F32)
+
+    def base(self, a, b, rows):
+        if "keep" in self.b:
+            own = self.pick(self.b["keep"], a, b, rows)
+        else:
+            own = (
+                self.source[self.c, a, b, rows] if self.first == "x" else self.source[self.c, b, a, rows]
+            ).astype(F32)
+        return own + self.pick(self.b["r0"], a, b, rows)
+
+    def each(self, fn):
+        rows = 4 * self.share
+
+        def step(i, carry):
+            fn(i, pl.ds(pl.multiple_of(i * self.chunk, self.chunk), self.chunk))
+            return carry
+
+        lax.fori_loop(0, rows // self.chunk, step, 0)
+
+    def stage0(self):
+        self.core_copy().start()
+        if "keep" in self.b:
+            self.load().start()
+
+    def stage1(self):
+        if "keep" in self.b:
+            self.load().wait()
+        self.core_copy().wait()
+        for b in range(2):
+
+            def fn(i, rows):
+                self.b["t1"][b, rows] = self.base(1 - self.mp, b, rows).astype(BF16)
+
+            self.each(fn)
+        self.p_copy().start()
+
+    def stage2(self):
+        self.p_copy().wait()
+
+        def fn(i, rows):
+            v = self.base(self.mp, 1 - self.mq, rows) + self.b["r1"][1 - self.mq, rows].astype(F32)
+            self.b["t2"][rows] = v.astype(BF16)
+
+        self.each(fn)
+        self.q_copy().start()
+
+    def stage3(self):
+        self.q_copy().wait()
+        share = self.share
+        per = self.chunk // share
+        f = self.b["f"]
+
+        def fn(i, rows):
+            v = self.base(self.mp, self.mq, rows)
+            v = v + self.b["r1"][self.mq, rows].astype(F32) + self.b["r2"][rows].astype(F32)
+            for k in range(per):
+                f[i * per + k] = v[k * share : (k + 1) * share]
+
+        self.each(fn)
+        pad = self.b["t3"].shape[1] - share
+        for d in range(3):
+            v = f[(self.z + d + 1) & 3]
+            if pad:
+                v = jnp.concatenate([v, jnp.zeros((pad, v.shape[1]), F32)], axis=0)
+            self.b["t3"][d] = v.astype(BF16)
+        for copy in self.z_copies():
+            copy.start()
+
+    def stage4(self):
+        for copy in self.z_copies():
+            copy.wait()
+        v = self.b["f"][self.z]
+        for d in range(3):
+            v = v + self.b["r3"][d].astype(F32)[: self.share]
+        self.out(v)
+
+
+def scatter_scratch(share, cols, in_hbm):
+    rows = 4 * share
+    pad = -(-share // 16) * 16
+    bufs = {
+        "r0": pltpu.VMEM((2, 2, rows, cols), BF16),
+        "t1": pltpu.VMEM((2, rows, cols), BF16),
+        "r1": pltpu.VMEM((2, rows, cols), BF16),
+        "t2": pltpu.VMEM((rows, cols), BF16),
+        "r2": pltpu.VMEM((rows, cols), BF16),
+        "t3": pltpu.VMEM((3, pad, cols), BF16),
+        "r3": pltpu.VMEM((3, pad, cols), BF16),
+        "f": pltpu.VMEM((4, share, cols), F32),
+        "send": pltpu.SemaphoreType.DMA((6,)),
+        "recv": pltpu.SemaphoreType.DMA((6,)),
+    }
+    if in_hbm:
+        bufs["keep"] = pltpu.VMEM((2, 2, rows, cols), BF16)
+        bufs["load"] = pltpu.SemaphoreType.DMA
+    return bufs
 
 
 def ffn_kernel(n_blk, *refs):
@@ -318,6 +482,460 @@
     gv_ref[...] = dot(nt, dv_ref[...], NT).astype(BF16)
     vec_ref[0:1] = dot(ones, dq_ref[...], NT)[:1]
     vec_ref[1:2] = dot(ones, dv_ref[...], NT)[:1]
+
+
+def ffn_host_kernel(names, n_blk, *refs):
+    r = dict(zip(names, refs))
+    i = pl.program_id(0)
+    j = i & 3
+    dp = lax.axis_index("dp")
+    blk = lax.axis_index("blk")
+    core, y = blk & 1, dp & 1
+    mid, acc, n2, n2t, act, gp, gw, r0, t1, r1 = [
+        r[k] for k in ("mid", "acc", "n2", "n2t", "act", "gp", "gw", "r0", "t1", "r1")
+    ]
+    g, win, wout, ct = r["g"], r["win"], r["wout"], r["ct"]
+    seq, width = mid.shape
+    tok = seq // n_blk
+    tile = act.shape[1]
+    share_f = gw.shape[4]
+    rows = [slice(s * tok, (s + 1) * tok) for s in range(n_blk)]
+
+    def core_copy(plane):
+        return pltpu.make_async_remote_copy(
+            src_ref=gw.at[1 - core, :, :, plane],
+            dst_ref=r0.at[:, :, plane],
+            send_sem=r["csend"].at[plane],
+            recv_sem=r["crecv"].at[plane],
+            device_id=(dp, blk ^ 1),
+            device_id_type=MESH,
+        )
+
+    def y_copy():
+        return pltpu.make_async_remote_copy(
+            src_ref=t1, dst_ref=r1, send_sem=r["ysend"], recv_sem=r["yrecv"], device_id=(dp ^ 1, blk), device_id_type=MESH
+        )
+
+    def out_copy(s):
+        src, dst = r["obuf"].at[s], r["output"].at[blk]
+        if s == 0:
+            return pltpu.make_async_copy(src, dst, r["lsem"].at[0])
+        return pltpu.make_async_remote_copy(
+            src_ref=src,
+            dst_ref=dst,
+            send_sem=r["osend"].at[s - 1],
+            recv_sem=r["orecv"].at[s - 1],
+            device_id=(dp, blk ^ s),
+            device_id_type=MESH,
+        )
+
+    @pl.when(i == 0)
+    def _():
+        greet([(dp, blk ^ 1), (dp, blk ^ 2), (dp, blk ^ 3), (dp ^ 1, blk)])
+        bins = as_row(r["bin"])
+        for k in range(4):
+            r["bins"][k] = bins[:, k * tile : (k + 1) * tile]
+        for sl in rows:
+            m = r["x"][sl].astype(F32) + dot(ct[:, sl], r["wo"][...], TN) + as_row(r["bo"])
+            mid[sl] = m
+            acc[sl] = m + as_row(r["bout"])
+            n, _ = center(m)
+            nb = (n * as_row(r["gain"]) + as_row(r["bias"])).astype(BF16)
+            n2[sl] = nb
+            n2t[:, sl] = nb.T
+
+    @pl.when(i < 4)
+    def _():
+        for sl in rows:
+            pre = dot(n2[sl], win[...]) + r["bins"][j]
+            phi, slope = gate(pre)
+            a = (pre * phi).astype(BF16)
+            act[sl] = a
+            gp[j, sl] = (phi + slope).astype(BF16)
+            acc[sl] += dot(a, wout[...])
+        v = dot(act[...], g[...], TN)
+        for c, x, yy in CXY:
+            at = (yy * 4 + x * 2 + c) * share_f
+            gw[c, x, yy, j] = v[at : at + share_f].astype(BF16)
+        core_copy(j).start()
+
+    @pl.when(i == 4)
+    def _():
+        for s in range(n_blk - 1, -1, -1):
+            r["obuf"][s] = acc[rows[s]].astype(BF16)
+            out_copy(s).start()
+            acc[rows[s]] = jnp.zeros((tok, width), F32)
+
+    @pl.when(i >= 4)
+    def _():
+        total = None
+        for sl in rows:
+            d = (dot(g[sl], wout[...], NT) * gp[j, sl].astype(F32)).astype(BF16)
+            act[sl] = d
+            col = jnp.sum(d.astype(F32), axis=0, keepdims=True)
+            total = col if total is None else total + col
+            acc[sl] += dot(d, win[...], NT)
+        r["bing"][j] = total
+        v = regroup(dot(n2t[...], act[...]), width // 32)
+        for c, x, yy in CXY:
+            r["gwin"][c, x, yy] = v[c][x][yy].astype(BF16)
+
+    @pl.when(i == 4)
+    def _():
+        for k in range(4):
+            core_copy(k).wait()
+
+        def step(k, carry):
+            for x in range(2):
+                t1[x, k] = (gw[core, x, 1 - y, k].astype(F32) + r0[x, 1 - y, k].astype(F32)).astype(BF16)
+            return carry
+
+        lax.fori_loop(0, 4, step, 0)
+        y_copy().start()
+
+    @pl.when(i == 7)
+    def _():
+        head = width // H
+        sums = [None] * 4
+        for sl in rows:
+            n, rstd = center(mid[sl])
+            e = acc[sl]
+            gf = g[sl].astype(F32)
+            f = e * as_row(r["gain"])
+            dm = gf + rstd * (
+                f - jnp.mean(f, axis=-1, keepdims=True) - n * jnp.mean(f * n, axis=-1, keepdims=True)
+            )
+            mid[sl] = dm
+            db = dm.astype(BF16)
+            n2[sl] = db
+            for k, term in enumerate((gf, e * n, e, db.astype(F32))):
+                col = jnp.sum(term, axis=0, keepdims=True)
+                sums[k] = col if sums[k] is None else sums[k] + col
+            dc = dot(r["wo"][...], db, NT)
+            for h in range(H):
+                hs = slice(h * head, (h + 1) * head)
+                r["dot"][hs, sl] = (dc[hs] * r["il"][h, :, sl]).astype(BF16)
+        save = pltpu.make_async_copy(mid, r["dmid"], r["lsem"].at[1])
+        save.start()
+        vec = r["vec"]
+        vec[...] = jnp.zeros_like(vec)
+        for k in range(4):
+            vec[4 + k : 5 + k] = sums[k]
+            vec[8 + k : 9 + k] = r["bing"][k]
+        v = regroup(dot(ct[...], n2[...]), width // 32)
+        for c, x, yy in CXY:
+            r["gwo"][c, x, yy] = v[c][x][yy].astype(BF16)
+        y_copy().wait()
+
+        def step(k, carry):
+            for x in range(2):
+                v = gw[core, x, y, k].astype(F32) + r0[x, y, k].astype(F32) + r1[x, k].astype(F32)
+                t1[x, k] = v.astype(BF16)
+            return carry
+
+        lax.fori_loop(0, 4, step, 0)
+        part = pltpu.make_async_copy(t1, r["part"], r["lsem"].at[2])
+        part.start()
+        for s in range(n_blk):
+            out_copy(s).wait()
+        save.wait()
+        part.wait()
+
+
+class Resume:
+    def __init__(self, r, place):
+        dp, blk = place
+        self.r = r
+        self.x, self.y, self.z = blk >> 1, dp & 1, dp >> 1
+        self.ids = [(((self.z + d) & 3) * 2 + self.y, blk) for d in (1, 2, 3)] + [(dp, blk ^ 2)]
+
+    def remote(self, src, dst, i):
+        return pltpu.make_async_remote_copy(
+            src_ref=src,
+            dst_ref=dst,
+            send_sem=self.r["w_send"].at[i],
+            recv_sem=self.r["w_recv"].at[i],
+            device_id=self.ids[i],
+            device_id_type=MESH,
+        )
+
+    def z_copies(self):
+        return [
+            self.remote(self.r["part"].at[:, (self.z + d + 1) & 3], self.r["w_rz"].at[d], d) for d in range(3)
+        ]
+
+    def load(self):
+        return pltpu.make_async_copy(self.r["part"].at[:, self.z], self.r["w_keep"], self.r["lsem"].at[0])
+
+    def x_copy(self):
+        return self.remote(self.r["w_t"], self.r["w_rx"], 3)
+
+    def stage0(self):
+        for copy in self.z_copies():
+            copy.start()
+        self.load().start()
+
+    def stage1(self):
+        self.load().wait()
+        for copy in self.z_copies():
+            copy.wait()
+        for k in range(2):
+            v = self.r["w_keep"][k].astype(F32)
+            for d in range(3):
+                v = v + self.r["w_rz"][d, k].astype(F32)
+            self.r["w_f"][k] = v
+        self.r["w_t"][...] = self.r["w_f"][1 - self.x].astype(BF16)
+        self.x_copy().start()
+
+    def stage2(self):
+        self.x_copy().wait()
+        self.r["s_wout"][...] = self.r["w_f"][self.x] + self.r["w_rx"][...].astype(F32)
+
+
+def finish_kernel(n_big, *refs):
+    src, vec = refs[:n_big], refs[n_big]
+    dst, small = refs[n_big + 1 : 2 * n_big + 1], refs[2 * n_big + 1 :]
+    for a, b in zip(src[:2], dst[:2]):
+        b[...] = a[...]
+
+    @pl.when(pl.program_id(0) == 0)
+    def _():
+        for a, b in zip(src[2:], dst[2:]):
+            b[...] = a[...]
+        me = lax.axis_index("dp") * lax.axis_size("blk") + lax.axis_index("blk")
+        share = small[0].shape[0]
+        wide = small[8].shape[0]
+        width = vec.shape[1]
+        moved = pltpu.roll(vec[:8], lax.rem(width - me * share, width), 1)
+        for i, k in enumerate((0, 1, 2, 3, 7, 5, 6, 4)):
+            small[i][...] = moved[k, :share]
+        each = width // wide
+        lines = vec[8:16]
+        moved = pltpu.roll(lines, lax.rem(width - lax.rem(me, each) * wide, width), 1)
+        row = lax.div(me, each)
+        pick = lax.broadcasted_iota(jnp.int32, moved.shape, 0) == row
+        small[8][...] = jnp.sum(jnp.where(pick, moved, 0.0), axis=0)[:wide]
+
+
+def back_kernel(scale, names, tasks, plan, *refs):
+    r = dict(zip(names, refs))
+    h = pl.program_id(0)
+    dp = lax.axis_index("dp")
+    blk = lax.axis_index("blk")
+    place = (dp, blk)
+    n_blk, tok, width = r["xs"].shape
+    seq = n_blk * tok
+    head = width // H
+    dcat, wcat, gq, vec = r["dcat"], r["wcat"], r["gq"], r["vec"]
+
+    def put(ref, cols):
+        def out(v):
+            if cols is None:
+                ref[...] = v
+            else:
+                ref[:, cols] = v
+
+        return out
+
+    jobs = {}
+    for name, source, index, cols, share, first, out, out_cols in tasks:
+        ref = r[source] if index is None else r[source].at[index]
+        bufs = {k: r[name + "_" + k] for k in SCATTER_KEYS if name + "_" + k in r}
+        if isinstance(out, tuple):
+            outs = [put(r[o], out_cols) for o in out]
+
+            def sink(v, outs=outs):
+                each = v.shape[1] // len(outs)
+                for i, o in enumerate(outs):
+                    o(v[:, i * each : (i + 1) * each])
+
+        else:
+            sink = put(r[out], out_cols)
+        jobs[name] = Scatter(ref, cols, share, first, sink, bufs, place)
+
+    jobs["wout"] = Resume(r, place)
+
+    def spread(src, dst, sems, s):
+        return pltpu.make_async_remote_copy(
+            src_ref=src.at[s],
+            dst_ref=dst.at[blk],
+            send_sem=sems[0].at[s - 1],
+            recv_sem=sems[1].at[s - 1],
+            device_id=(dp, blk ^ s),
+            device_id_type=MESH,
+        )
+
+    def in_copy(s):
+        if s == 0:
+            return pltpu.make_async_copy(r["dx"].at[0], r["input_grad"].at[blk], r["lsem"].at[1])
+        return spread(r["dx"], r["input_grad"], (r["isend"], r["irecv"]), s)
+
+    def loads():
+        pairs = [(r["xs"], r["xbuf"]), (r["dmid"], r["dmbuf"])]
+        pairs += [(r[w], wcat.at[:, i * width : (i + 1) * width]) for i, w in enumerate(("wq", "wk", "wv"))]
+        return [pltpu.make_async_copy(a, b, r["lsem"].at[2 + i]) for i, (a, b) in enumerate(pairs)]
+
+    z, y = dp >> 1, dp & 1
+    vec_ids = [[(dp, blk ^ 1)], [(dp, blk ^ 2)], [(dp ^ 1, blk)]]
+    vec_ids.append([(((z + d) & 3) * 2 + y, blk) for d in (1, 2, 3)])
+
+    def vec_copies(stage):
+        return [
+            pltpu.make_async_remote_copy(
+                src_ref=vec,
+                dst_ref=r["rvec"].at[stage + d],
+                send_sem=r["vsend"].at[stage + d],
+                recv_sem=r["vrecv"].at[stage + d],
+                device_id=where,
+                device_id_type=MESH,
+            )
+            for d, where in enumerate(vec_ids[stage])
+        ]
+
+    def vec_start(stage):
+        for copy in vec_copies(stage):
+            copy.start()
+
+    def vec_end(stage):
+        copies = vec_copies(stage)
+        for copy in copies:
+            copy.wait()
+        for d in range(len(copies)):
+            vec[...] += r["rvec"][stage + d]
+
+    def input_piece(s, sums):
+        sl = slice(s * tok, (s + 1) * tok)
+        e = dot(wcat[...], dcat[:, sl]).T
+        n, rstd = center(r["xbuf"][s].astype(F32))
+        f = e * as_row(r["gain"])
+        dx = r["dmbuf"][sl] + rstd * (
+            f - jnp.mean(f, axis=-1, keepdims=True) - n * jnp.mean(f * n, axis=-1, keepdims=True)
+        )
+        r["dx"][s] = dx.astype(BF16)
+        in_copy(s).start()
+        new = [jnp.sum(t, axis=0, keepdims=True) for t in (e * n, e)]
+        return new if sums is None else [a + b for a, b in zip(sums, new)]
+
+    @pl.when(h == 0)
+    def _():
+        greet(
+            [(dp, blk ^ 1), (dp, blk ^ 2), (dp, blk ^ 3), (dp ^ 1, blk)]
+            + [(((z + d) & 3) * 2 + y, blk) for d in (1, 2, 3)]
+        )
+        for load in loads():
+            load.start()
+        vec[...] = r["vec_in"][...]
+
+    def act(item):
+        kind, what = item
+        getattr(jobs[kind], "stage%d" % what)()
+
+    for at in range(H):
+        if plan.get(at):
+
+            @pl.when(h == at)
+            def _(at=at):
+                for item in plan[at]:
+                    act(item)
+
+    @pl.when(h < H)
+    def _():
+        do = r["do"][...]
+        vh = r["v"][...].T
+        delta = jnp.sum(do.astype(F32) * r["ct"][...].astype(F32), axis=0, keepdims=True)
+        step = seq // 2
+        base = pl.multiple_of(h * head, head)
+        for c in range(2):
+            sl = slice(c * step, (c + 1) * step)
+            dpr = dot(vh, do[:, sl])
+            d = (r["p"][0, :, sl].astype(F32) * (dpr - delta[:, sl])).astype(BF16)
+            r["ds"][:, sl] = d
+            dcat[pl.ds(base, head), sl] = (dot(r["k"][...], d) * scale).astype(BF16)
+        dcat[pl.ds(base + 2 * width, head)] = dot(r["p"][0], do, NT).T.astype(BF16)
+        dcat[pl.ds(base + width, head)] = (dot(r["ds"][...], r["q"][...], NT) * LN2).T.astype(BF16)
+
+    n_group = gq.shape[0]
+    cols = width // n_group
+    for gi in range(n_group):
+
+        @pl.when(h == (gi + 1) * (H // n_group) - 1)
+        def _(gi=gi):
+            nt = r["nt"][...]
+            ones = jnp.ones((8, seq), BF16)
+            for t in range(3):
+                part = dcat[t * width + gi * cols : t * width + (gi + 1) * cols]
+                v = regroup(dot(nt, part, NT), width // 32)
+                for c, x, y in CXY:
+                    gq[gi, c, x, y, :, t * cols : (t + 1) * cols] = v[c][x][y].astype(BF16)
+                if t != 1:
+                    row = 2 if t == 0 else 3
+                    vec[row : row + 1, gi * cols : (gi + 1) * cols] = dot(ones, part, NT)[:1]
+            jobs["q%d" % gi].stage0()
+
+    @pl.when(h == H)
+    def _():
+        sums = None
+        for load in loads():
+            load.wait()
+        for item in plan["tail"]:
+            kind, what = item
+            if kind == "piece":
+                sums = input_piece(what, sums)
+                if what == 0:
+                    vec[0:1] = sums[0]
+                    vec[1:2] = sums[1]
+            elif kind == "vec":
+                if what > 0:
+                    vec_end(what - 1)
+                if what < 4:
+                    vec_start(what)
+            else:
+                act(item)
+        r["vec_out"][...] = vec[...]
+        for s in range(n_blk):
+            in_copy(s).wait()
+
+
+PLAN = {
+    0: [("wout", 0), ("wo", 0), ("a2", 0), ("b2", 0)],
+    1: [("wo", 1)],
+    2: [("a2", 1)],
+    3: [("b2", 1)],
+    5: [("q0", 1), ("wo", 2)],
+    8: [("a2", 2), ("q0", 2)],
+    9: [("q1", 1)],
+    10: [("wout", 1)],
+    11: [("wo", 3)],
+    "tail": [
+        ("piece", 3),
+        ("b2", 2),
+        ("piece", 2),
+        ("q2", 1),
+        ("piece", 1),
+        ("a2", 3),
+        ("q0", 3),
+        ("piece", 0),
+        ("vec", 0),
+        ("q1", 2),
+        ("wout", 2),
+        ("vec", 1),
+        ("b2", 3),
+        ("q2", 2),
+        ("vec", 2),
+        ("wo", 4),
+        ("q1", 3),
+        ("vec", 3),
+        ("q2", 3),
+        ("a2", 4),
+        ("q0", 4),
+        ("vec", 4),
+        ("b2", 4),
+        ("q1", 4),
+        ("q2", 4),
+    ],
+}
+
+SCATTER_KEYS = ("r0", "t1", "r1", "t2", "r2", "t3", "r3", "f", "send", "recv", "keep", "load")
 
 
 def body(
@@ -363,9 +981,7 @@
         return out
 
     row = lambda v: v.astype(F32).reshape(1, -1)
-    column = lambda v: v.astype(F32).reshape(-1, 1)
-
-    live = ((blk ^ jnp.arange(n_blk)) * tok < lengths[blk]).astype(jnp.int32).reshape(1, n_blk)
+
 
     sds = jax.ShapeDtypeStruct
     piece = full((tok, width))
@@ -395,7 +1011,7 @@
         compiler_params=params(collective_id=0, has_side_effects=True),
         cost_estimate=cost(3 * seq * width * width, 14 * seq * width),
         name="qkv",
-    )(inputs, row(ln1_gain), row(ln1_bias), w_query, column(b_query), w_key, w_value, column(b_value))
+    )(inputs, ln1_gain, ln1_bias, w_query, b_query, w_key, w_value, b_value)
 
     per_head = pl.BlockSpec((head, seq), lambda h: (h, 0))
     per_square = pl.BlockSpec((1, seq, seq), lambda h: (h, 0, 0))
@@ -418,7 +1034,199 @@
         compiler_params=params(collective_id=1, has_side_effects=True),
         cost_estimate=cost(8 * seq * seq * width, 2 * H * seq * seq, H * seq * seq),
         name="attend",
-    )(live, qt, kt, vt, out_grad)
+    )(lengths, qt, kt, vt, out_grad)
+
+    if n_dp == 8 and n_blk == 4 and width % 768 == 0 and hidden == 4 * width:
+        share, share_f = width // n_dev, hidden // n_dev
+        tile = hidden // 4
+        once = lambda shape: pl.BlockSpec(shape, lambda i: (0,) * len(shape), pipeline_mode=pl.Buffered(1))
+        vec_rows = 16
+        ins = {
+            "x": (xs.reshape(seq, width), once((seq, width))),
+            "g": (gs.reshape(seq, width), once((seq, width))),
+            "ct": (ct, once((width, seq))),
+            "il": (inv_total, once((H, 1, seq))),
+            "wo": (w_output, once((width, width))),
+            "bo": (b_output, once((width,))),
+            "gain": (ln2_gain, once((width,))),
+            "bias": (ln2_bias, once((width,))),
+            "bout": (b_out, once((width,))),
+            "bin": (b_in, once((hidden,))),
+            "win": (w_in, pl.BlockSpec((width, tile), lambda i: (0, i % 4))),
+            "wout": (w_out, pl.BlockSpec((tile, width), lambda i: (i % 4, 0))),
+        }
+        outs = {
+            "output": (sds((n_seq, tok, width), BF16), anywhere),
+            "dmid": (sds((seq, width), F32), anywhere),
+            "dot": (sds((width, seq), BF16), once((width, seq))),
+            "gwin": (
+                sds((2, 2, 2, 4 * share, hidden), BF16),
+                pl.BlockSpec((2, 2, 2, 4 * share, tile), lambda i: (0, 0, 0, 0, jnp.maximum(i - 4, 0))),
+            ),
+            "gwo": (sds((2, 2, 2, 4 * share, width), BF16), once((2, 2, 2, 4 * share, width))),
+            "part": (sds((2, 4, share_f, width), BF16), anywhere),
+            "vec": (sds((vec_rows, width), F32), once((vec_rows, width))),
+        }
+        scratch = {
+            "mid": pltpu.VMEM((seq, width), F32),
+            "acc": pltpu.VMEM((seq, width), F32),
+            "n2": pltpu.VMEM((seq, width), BF16),
+            "n2t": pltpu.VMEM((width, seq), BF16),
+            "act": pltpu.VMEM((seq, tile), BF16),
+            "gp": pltpu.VMEM((4, seq, tile), BF16),
+            "bins": pltpu.VMEM((4, 1, tile), F32),
+            "bing": pltpu.VMEM((4, 1, tile), F32),
+            "obuf": pltpu.VMEM((n_blk, tok, width), BF16),
+            "gw": pltpu.VMEM((2, 2, 2, 4, share_f, width), BF16),
+            "r0": pltpu.VMEM((2, 2, 4, share_f, width), BF16),
+            "t1": pltpu.VMEM((2, 4, share_f, width), BF16),
+            "r1": pltpu.VMEM((2, 4, share_f, width), BF16),
+            "csend": pltpu.SemaphoreType.DMA((4,)),
+            "crecv": pltpu.SemaphoreType.DMA((4,)),
+            "ysend": pltpu.SemaphoreType.DMA,
+            "yrecv": pltpu.SemaphoreType.DMA,
+            "osend": pltpu.SemaphoreType.DMA((n_blk - 1,)),
+            "orecv": pltpu.SemaphoreType.DMA((n_blk - 1,)),
+            "lsem": pltpu.SemaphoreType.DMA((3,)),
+        }
+        names = tuple(ins) + tuple(outs) + tuple(scratch)
+        ffn = pl.pallas_call(
+            functools.partial(ffn_host_kernel, names, n_blk),
+            grid=(8,),
+            in_specs=[v[1] for v in ins.values()],
+            out_specs=[v[1] for v in outs.values()],
+            out_shape=[v[0] for v in outs.values()],
+            scratch_shapes=list(scratch.values()),
+            compiler_params=pltpu.CompilerParams(
+                vmem_limit_bytes=62 * 2**20, collective_id=3, has_side_effects=True
+            ),
+            name="ffn",
+        )(*[v[0] for v in ins.values()])
+        ffn = dict(zip(outs, ffn))
+        tasks = (
+            ("a2", "gwin", None, slice(0, hidden // 2), share, "y", "s_win", slice(0, hidden // 2)),
+            ("b2", "gwin", None, slice(hidden // 2, hidden), share, "y", "s_win", slice(hidden // 2, hidden)),
+            ("wo", "gwo", None, None, share, "x", "s_wo", None),
+        ) + tuple(
+            (
+                "q%d" % i,
+                "gq",
+                i,
+                None,
+                share,
+                "xxy"[i],
+                ("s_wq", "s_wk", "s_wv"),
+                slice(i * cols, (i + 1) * cols),
+            )
+            for i in range(n_col)
+        )
+        sizes = {"a2": hidden // 2, "b2": hidden // 2, "wo": width}
+        plan = PLAN
+        last = lambda shape: pl.BlockSpec(shape, lambda h: (jnp.minimum(h, H - 1),) + (0,) * (len(shape) - 1))
+        strip_h = last((head, seq))
+        ins = {
+            "p": (probs, last((1, seq, seq))),
+            "q": (qt, strip_h),
+            "k": (kt, strip_h),
+            "v": (vt, strip_h),
+            "do": (ffn["dot"], strip_h),
+            "ct": (ct, strip_h),
+            "nt": (nt, wide),
+            "gain": (ln1_gain, full((width,))),
+            "vec_in": (ffn["vec"], full((vec_rows, width))),
+            "xs": (xs, anywhere),
+            "dmid": (ffn["dmid"], anywhere),
+            "wq": (w_query, anywhere),
+            "wk": (w_key, anywhere),
+            "wv": (w_value, anywhere),
+            "part": (ffn["part"], anywhere),
+            "gwin": (ffn["gwin"], anywhere),
+            "gwo": (ffn["gwo"], anywhere),
+        }
+        outs = {
+            "input_grad": (sds((n_seq, tok, width), BF16), anywhere),
+            "s_wq": (sds((share, width), F32), full((share, width))),
+            "s_wk": (sds((share, width), F32), full((share, width))),
+            "s_wv": (sds((share, width), F32), full((share, width))),
+            "s_wo": (sds((share, width), F32), full((share, width))),
+            "s_win": (sds((share, hidden), F32), full((share, hidden))),
+            "s_wout": (sds((share_f, width), F32), full((share_f, width))),
+            "vec_out": (sds((vec_rows, width), F32), full((vec_rows, width))),
+        }
+        scratch = {
+            "ds": pltpu.VMEM((seq, seq), BF16),
+            "dcat": pltpu.VMEM((3 * width, seq), BF16),
+            "wcat": pltpu.VMEM((width, 3 * width), BF16),
+            "gq": pltpu.VMEM((n_col, 2, 2, 2, 4 * share, 3 * cols), BF16),
+            "vec": pltpu.VMEM((vec_rows, width), F32),
+            "rvec": pltpu.VMEM((6, vec_rows, width), F32),
+            "xbuf": pltpu.VMEM((n_blk, tok, width), BF16),
+            "dmbuf": pltpu.VMEM((seq, width), F32),
+            "dx": pltpu.VMEM((n_blk, tok, width), BF16),
+            "lsem": pltpu.SemaphoreType.DMA((7,)),
+            "vsend": pltpu.SemaphoreType.DMA((6,)),
+            "vrecv": pltpu.SemaphoreType.DMA((6,)),
+            "w_keep": pltpu.VMEM((2, share_f, width), BF16),
+            "w_rz": pltpu.VMEM((3, 2, share_f, width), BF16),
+            "w_f": pltpu.VMEM((2, share_f, width), F32),
+            "w_t": pltpu.VMEM((share_f, width), BF16),
+            "w_rx": pltpu.VMEM((share_f, width), BF16),
+            "w_send": pltpu.SemaphoreType.DMA((4,)),
+            "w_recv": pltpu.SemaphoreType.DMA((4,)),
+            "isend": pltpu.SemaphoreType.DMA((n_blk - 1,)),
+            "irecv": pltpu.SemaphoreType.DMA((n_blk - 1,)),
+        }
+        for name, source, _, _, task_share, _, _, _ in tasks:
+            for k, v in scatter_scratch(task_share, sizes.get(name, width), source != "gq").items():
+                scratch[name + "_" + k] = v
+        names = tuple(ins) + tuple(outs) + tuple(scratch)
+        got = pl.pallas_call(
+            functools.partial(back_kernel, scale, names, tasks, plan),
+            grid=(H + 1,),
+            in_specs=[v[1] for v in ins.values()],
+            out_specs=[v[1] for v in outs.values()],
+            out_shape=[v[0] for v in outs.values()],
+            scratch_shapes=list(scratch.values()),
+            compiler_params=pltpu.CompilerParams(
+                vmem_limit_bytes=60 * 2**20, collective_id=2, has_side_effects=True
+            ),
+            name="back",
+        )(*[v[0] for v in ins.values()])
+        got = dict(zip(outs, got))
+        big = [ffn["output"], got["input_grad"]] + [
+            got[k] for k in ("s_wq", "s_wk", "s_wv", "s_wo", "s_win", "s_wout")
+        ]
+        part = pl.BlockSpec((1, tok, width), lambda i: (i, 0, 0))
+        flat = [sds(v.shape, v.dtype) for v in big]
+        fin = pl.pallas_call(
+            functools.partial(finish_kernel, len(big)),
+            grid=(n_blk,),
+            in_specs=[part] * 2 + [full(v.shape) for v in big[2:]] + [full((vec_rows, width))],
+            out_specs=[part] * 2 + [full(v.shape) for v in big[2:]] + [full((share,))] * 8 + [full((share_f,))],
+            out_shape=flat + [sds((share,), F32)] * 8 + [sds((share_f,), F32)],
+            name="finish",
+        )(*big, got["vec_out"])
+        output, input_grad, s_wq, s_wk, s_wv, s_wo, s_win, s_wout = fin[: len(big)]
+        g1, b1, bq, bv, bo_sum, g2, b2, bout_sum, bin_sum = fin[len(big) :]
+        return (
+            output,
+            input_grad,
+            g1,
+            b1,
+            s_wq,
+            bq,
+            s_wk,
+            s_wv,
+            bv,
+            s_wo,
+            bo_sum,
+            g2,
+            b2,
+            s_win,
+            bin_sum,
+            s_wout,
+            bout_sum,
+        )
 
     n_tile = 4
     tile = hidden // n_tile

time: 342 us -> 209 us (0.61)
  Pallas kernels: 91.7 us -> 208 us
  other arithmetic: 86.8 us -> 0 us
  waiting for transfers between devices: 80.7 us -> 0 us
  starting transfers between devices: 43.8 us -> 0 us
  local copies, waits for them, and re-layouts: 35.8 us -> 0 us
    pallas_call x2 -> x3, Pallas kernels: 38 us -> 154 us  [the longest x1 89 us: body(): pl.pallas_call(functools.partial(back_kernel, scale, names, tasks, plan),...]
    ppermute x41 -> x0, waiting for transfers between devices: 80.7 us -> none  [the longest x35 61 us: scatter(): lax.ppermute(send.astype(wire), ('dp', 'blk'), [(i, i ^ 1 << b) for i in...]
    pallas_call x3 -> x0, other arithmetic: 65.7 us -> none  [the longest x2 56.2 us: body(): pl.pallas_call(functools.partial(ffn_kernel, n_blk), grid=(n_tile,), in_s...]
    ppermute x41 -> x0, starting transfers between devices: 43.8 us -> none  [the longest x35 41.1 us: scatter(): lax.ppermute(send.astype(wire), ('dp', 'blk'), [(i, i ^ 1 << b) for i in...]
    convert_element_type x25 -> x0, other arithmetic: 12.8 us -> none  [the longest x24 11.6 us: scatter(): send.astype(wire)]
    squeeze x7 -> x0, local copies, waits for them, and re-layouts: 10.6 us -> none  [scatter(): other = lax.dynamic_index_in_dim(t, 1 - mine, at, keepdims=False)]
    reshape x8 -> x0, local copies, waits for them, and re-layouts: 8.45 us -> none  [the longest x6 5.26 us: body(): row = lambda v: v.astype(F32).reshape(1, -1)]
    add x11 -> x0, other arithmetic: 7.58 us -> none  [the longest x7 6.95 us: scatter(): total = total + t.astype(F32)]
  transfers between devices with their start and end apart: 41 -> 0, of which waited for: 18 -> 0; matrix products, arithmetic and copies ran while one was open for 14% -> 0% of each run, Pallas kernels for 11% -> 0%
where the time goes in v3:
time: 209 us
  Pallas kernels  208 us (100%)
    pallas_call x1, Pallas kernels, body(): pl.pallas_call(functools.partial(back_kernel, scale, names, tasks, plan),...  89 us
    pallas_call x1, Pallas kernels, body(): pl.pallas_call(functools.partial(ffn_host_kernel, names, n_blk), grid=(8,...  60.5 us
    pallas_call x1, Pallas kernels, body(): pl.pallas_call(functools.partial(qkv_spread_kernel, scale * LOG2E, n_blk)...  26.8 us
    pallas_call x1, Pallas kernels, body(): pl.pallas_call(functools.partial(attend_spread_kernel, n_blk), grid=(H,),...  26.7 us
    pallas_call x1, Pallas kernels, body(): pl.pallas_call(functools.partial(finish_kernel, len(big)), grid=(n_blk,),...  4.94 us

profile of v3, /device:TPU:0, one launch (start us, length us, event | category | flops | bytes accessed | tf_op | source)
XLA Modules:
  0.0 208.8 jit_solution(2708947161177104642)
XLA Ops:
  0.7 26.8 %qkv.1 = (bf16[4,256,768]{2,1,0:T(8,128)(2,1)}, bf16[768,1024]{1,0:T(8,128)(2,1)}, bf16[768,1024]{1,0:T(8,128)(2,1)}, bf16[768,1024]{1,0:T(8,128)(2,1)}, bf16[768,1024]{1,0:T(8,128)(2,1)}) custom-call(bf16[4,256,768]{2,1,0:T(8,128)(2,1)} %x_any.1, bf16[768]{0:T(1024)(128)(2,1)} %refs_7_.3, bf16[768]{0:T(1024)(128)(2,1)} %bias.1, bf16[768,768]{1,0:T(8,128)(2,1)} %refs_11_.3, ...), custom_call_target="tpu_custom_call" | custom-call | flops 3623878656 | bytes 11010048 | tf_op jit(solution)/shard_map/qkv/pallas_call | solution.py:994
  27.5 26.7 %attend.1 = (bf16[768,1024]{1,0:T(8,128)(2,1)}, bf16[12,1024,1024]{2,1,0:T(8,128)(2,1)}, f32[12,1,1024]{2,1,0:T(1,128)}, bf16[4,256,768]{2,1,0:T(8,128)(2,1)}) custom-call(s32[4]{0:T(128)} %len_ref.1, bf16[768,1024]{1,0:T(8,128)(2,1)} %get-tuple-element.59.q_ref.refs_1_, bf16[768,1024]{1,0:T(8,128)(2,1)} %get-tuple-element.60.k_ref.refs_2_, ...), custom_call_target="tpu_custom_call" | custom-call | flops 12884901888 | bytes 25165824 | tf_op jit(solution)/shard_map/attend/pallas_call | solution.py:1018
  54.2 60.5 %ffn.1 = (bf16[4,256,768]{2,1,0:T(8,128)(2,1)}, f32[1024,768]{1,0:T(8,128)}, bf16[768,1024]{1,0:T(8,128)(2,1)}, bf16[2,2,2,96,3072]{4,3,2,1,0:T(8,128)(2,1)}, bf...) custom-call(bf16[1024,768]{1,0:T(8,128)(2,1)} %bitcast.2, ...), custom_call_target="tpu_custom_call" | custom-call | tf_op jit(solution)/shard_map/ffn/pallas_call | solution.py:1093
  114.7 89.0 %back.1 = (bf16[4,256,768]{2,1,0:T(8,128)(2,1)}, f32[24,768]{1,0:T(8,128)}, f32[24,768]{1,0:T(8,128)}, f32[24,768]{1,0:T(8,128)}, f32[24,768]{1,0:T(8,128)}, /*i...) custom-call(bf16[12,1024,1024]{2,1,0:T(8,128)(2,1)} %get-tuple-element.66.refs_0_, ...), custom_call_target="tpu_custom_call" | custom-call | tf_op jit(solution)/shard_map/back/pallas_call | solution.py:1183
  203.7 4.9 %finish.1 = (bf16[4,256,768]{2,1,0:T(8,128)(2,1)}, bf16[4,256,768]{2,1,0:T(8,128)(2,1)}, f32[24,768]{1,0:T(8,128)}, f32[24,768]{1,0:T(8,128)}, f32[24,768]{1,0:T...) custom-call(bf16[4,256,768]{2,1,0:T(8,128)(2,1)} %get-tuple-element., ...), custom_call_target="tpu_custom_call" | custom-call | tf_op jit(solution)/shard_map/finish/pallas_call | solution.py:1201

commit v4 on v3

--- a/solution.py
+++ b/solution.py
@@ -140,16 +140,20 @@
             device_id=(dp, blk ^ s),
             device_id_type=MESH,
         )
-        copies[s].start()
+        if s != 2:
+            copies[s].start()
     for i, load in enumerate(loads):
         load.wait()
         wt[i] = wbuf[i].T
     cols = jnp.concatenate([as_row(bq), as_row(bv), jnp.zeros((6, width), F32)], axis=0).T
     writes = []
-    for s in range(n_blk):
+    for s in (0, 1, 3, 2):
         if s == 0:
             own.wait()
         else:
+            if s == 3:
+                copies[3].wait_send()
+                copies[2].start()
             copies[s].wait_recv()
         sl = slice(s * tok, (s + 1) * tok)
         n, _ = center(xbuf[s].astype(F32))
@@ -170,7 +174,7 @@
             write = pltpu.make_async_copy(src, dst, osem.at[s, i])
             write.start()
             writes.append(write)
-    for s in order:
+    for s in (1, 2):
         copies[s].wait_send()
     for write in writes:
         write.wait()
@@ -327,11 +331,11 @@
                 f[i * per + k] = v[k * share : (k + 1) * share]
 
         self.each(fn)
-        pad = self.b["t3"].shape[1] - share
+        half = f.shape[2] // 2
         for d in range(3):
             v = f[(self.z + d + 1) & 3]
-            if pad:
-                v = jnp.concatenate([v, jnp.zeros((pad, v.shape[1]), F32)], axis=0)
+            if per > 1:
+                v = jnp.concatenate([v[:, :half], v[:, half:]], axis=0)
             self.b["t3"][d] = v.astype(BF16)
         for copy in self.z_copies():
             copy.start()
@@ -341,25 +345,73 @@
             copy.wait()
         v = self.b["f"][self.z]
         for d in range(3):
-            v = v + self.b["r3"][d].astype(F32)[: self.share]
+            w = self.b["r3"][d].astype(F32)
+            if self.chunk > self.share:
+                w = jnp.concatenate([w[: self.share], w[self.share :]], axis=1)
+            v = v + w
         self.out(v)
 
 
-def scatter_scratch(share, cols, in_hbm):
+class ScatterLate(Scatter):
+    def x_copy(self):
+        return self.remote(self.b["f2"].at[1 - self.x], self.b["rx"], 2, self.q_id)
+
+    def stage2(self):
+        self.p_copy().wait()
+        share = self.share
+        per = self.chunk // share
+        f = self.b["f"]
+        for x in range(2):
+
+            def fn(i, rows, x=x):
+                v = self.base(self.mp, x, rows) + self.b["r1"][x, rows].astype(F32)
+                for k in range(per):
+                    f[x, i * per + k] = v[k * share : (k + 1) * share]
+
+            self.each(fn)
+        for d in range(3):
+            at = (self.z + d + 1) & 3
+            self.b["t3"][d] = jnp.concatenate([f[0, at], f[1, at]], axis=0).astype(BF16)
+        for copy in self.z_copies():
+            copy.start()
+
+    def stage3(self):
+        for copy in self.z_copies():
+            copy.wait()
+        for x in range(2):
+            v = self.b["f"][x, self.z]
+            for d in range(3):
+                v = v + self.b["r3"][d].astype(F32)[x * self.share : (x + 1) * self.share]
+            self.b["f2"][x] = v
+        self.x_copy().start()
+
+    def stage4(self):
+        self.x_copy().wait()
+        self.out(self.b["f2"][self.x] + self.b["rx"][...])
+
+
+def scatter_scratch(share, cols, in_hbm, late):
     rows = 4 * share
-    pad = -(-share // 16) * 16
+    slab = (share, cols) if share % 16 == 0 else (2 * share, cols // 2)
     bufs = {
         "r0": pltpu.VMEM((2, 2, rows, cols), BF16),
         "t1": pltpu.VMEM((2, rows, cols), BF16),
         "r1": pltpu.VMEM((2, rows, cols), BF16),
         "t2": pltpu.VMEM((rows, cols), BF16),
         "r2": pltpu.VMEM((rows, cols), BF16),
-        "t3": pltpu.VMEM((3, pad, cols), BF16),
-        "r3": pltpu.VMEM((3, pad, cols), BF16),
+        "t3": pltpu.VMEM((3,) + slab, BF16),
+        "r3": pltpu.VMEM((3,) + slab, BF16),
         "f": pltpu.VMEM((4, share, cols), F32),
         "send": pltpu.SemaphoreType.DMA((6,)),
         "recv": pltpu.SemaphoreType.DMA((6,)),
     }
+    if late:
+        del bufs["t2"], bufs["r2"]
+        bufs["t3"] = pltpu.VMEM((3, 2 * share, cols), BF16)
+        bufs["r3"] = pltpu.VMEM((3, 2 * share, cols), BF16)
+        bufs["f"] = pltpu.VMEM((2, 4, share, cols), F32)
+        bufs["f2"] = pltpu.VMEM((2, share, cols), F32)
+        bufs["rx"] = pltpu.VMEM((share, cols), F32)
     if in_hbm:
         bufs["keep"] = pltpu.VMEM((2, 2, rows, cols), BF16)
         bufs["load"] = pltpu.SemaphoreType.DMA
@@ -511,10 +563,21 @@
             device_id_type=MESH,
         )
 
-    def y_copy():
+    def y_copy(plane):
         return pltpu.make_async_remote_copy(
-            src_ref=t1, dst_ref=r1, send_sem=r["ysend"], recv_sem=r["yrecv"], device_id=(dp ^ 1, blk), device_id_type=MESH
+            src_ref=t1.at[:, plane],
+            dst_ref=r1.at[:, plane],
+            send_sem=r["ysend"].at[plane],
+            recv_sem=r["yrecv"].at[plane],
+            device_id=(dp ^ 1, blk),
+            device_id_type=MESH,
         )
+
+    def y_start(plane):
+        core_copy(plane).wait()
+        for x in range(2):
+            t1[x, plane] = (gw[core, x, 1 - y, plane].astype(F32) + r0[x, 1 - y, plane].astype(F32)).astype(BF16)
+        y_copy(plane).start()
 
     def out_copy(s):
         src, dst = r["obuf"].at[s], r["output"].at[blk]
@@ -553,6 +616,11 @@
             act[sl] = a
             gp[j, sl] = (phi + slope).astype(BF16)
             acc[sl] += dot(a, wout[...])
+
+        @pl.when(i > 0)
+        def _():
+            y_start(j - 1)
+
         v = dot(act[...], g[...], TN)
         for c, x, yy in CXY:
             at = (yy * 4 + x * 2 + c) * share_f
@@ -576,22 +644,14 @@
             total = col if total is None else total + col
             acc[sl] += dot(d, win[...], NT)
         r["bing"][j] = total
+
+        @pl.when(i == 4)
+        def _():
+            y_start(3)
+
         v = regroup(dot(n2t[...], act[...]), width // 32)
         for c, x, yy in CXY:
             r["gwin"][c, x, yy] = v[c][x][yy].astype(BF16)
-
-    @pl.when(i == 4)
-    def _():
-        for k in range(4):
-            core_copy(k).wait()
-
-        def step(k, carry):
-            for x in range(2):
-                t1[x, k] = (gw[core, x, 1 - y, k].astype(F32) + r0[x, 1 - y, k].astype(F32)).astype(BF16)
-            return carry
-
-        lax.fori_loop(0, 4, step, 0)
-        y_copy().start()
 
     @pl.when(i == 7)
     def _():
@@ -618,14 +678,14 @@
         save = pltpu.make_async_copy(mid, r["dmid"], r["lsem"].at[1])
         save.start()
         vec = r["vec"]
-        vec[...] = jnp.zeros_like(vec)
         for k in range(4):
-            vec[4 + k : 5 + k] = sums[k]
-            vec[8 + k : 9 + k] = r["bing"][k]
+            vec[k : k + 1] = sums[k]
+            vec[4 + k : 5 + k] = r["bing"][k]
         v = regroup(dot(ct[...], n2[...]), width // 32)
         for c, x, yy in CXY:
             r["gwo"][c, x, yy] = v[c][x][yy].astype(BF16)
-        y_copy().wait()
+        for k in range(4):
+            y_copy(k).wait()
 
         def step(k, carry):
             for x in range(2):
@@ -693,8 +753,8 @@
 
 
 def finish_kernel(n_big, *refs):
-    src, vec = refs[:n_big], refs[n_big]
-    dst, small = refs[n_big + 1 : 2 * n_big + 1], refs[2 * n_big + 1 :]
+    src, va, vb = refs[:n_big], refs[n_big], refs[n_big + 1]
+    dst, small = refs[n_big + 2 : 2 * n_big + 2], refs[2 * n_big + 2 :]
     for a, b in zip(src[:2], dst[:2]):
         b[...] = a[...]
 
@@ -705,14 +765,18 @@
         me = lax.axis_index("dp") * lax.axis_size("blk") + lax.axis_index("blk")
         share = small[0].shape[0]
         wide = small[8].shape[0]
-        width = vec.shape[1]
-        moved = pltpu.roll(vec[:8], lax.rem(width - me * share, width), 1)
-        for i, k in enumerate((0, 1, 2, 3, 7, 5, 6, 4)):
-            small[i][...] = moved[k, :share]
+        width = va.shape[1]
+        shift = lax.rem(width - me * share, width)
+        moved = pltpu.roll(va[...], shift, 1)
+        for k in range(4):
+            small[k][...] = moved[k, :share]
+        lines = vb[...]
+        moved = pltpu.roll(lines, shift, 1)
+        for i, k in enumerate((3, 1, 2, 0)):
+            small[4 + i][...] = moved[k, :share]
         each = width // wide
-        lines = vec[8:16]
         moved = pltpu.roll(lines, lax.rem(width - lax.rem(me, each) * wide, width), 1)
-        row = lax.div(me, each)
+        row = 4 + lax.div(me, each)
         pick = lax.broadcasted_iota(jnp.int32, moved.shape, 0) == row
         small[8][...] = jnp.sum(jnp.where(pick, moved, 0.0), axis=0)[:wide]
 
@@ -726,7 +790,7 @@
     n_blk, tok, width = r["xs"].shape
     seq = n_blk * tok
     head = width // H
-    dcat, wcat, gq, vec = r["dcat"], r["wcat"], r["gq"], r["vec"]
+    dcat, wcat, gq, vec = r["dcat"], r["wcat"], r["gq"], r["va"]
 
     def put(ref, cols):
         def out(v):
@@ -751,7 +815,8 @@
 
         else:
             sink = put(r[out], out_cols)
-        jobs[name] = Scatter(ref, cols, share, first, sink, bufs, place)
+        kind = ScatterLate if first == "late" else Scatter
+        jobs[name] = kind(ref, cols, share, "y" if first == "late" else first, sink, bufs, place)
 
     jobs["wout"] = Resume(r, place)
 
@@ -776,36 +841,37 @@
         return [pltpu.make_async_copy(a, b, r["lsem"].at[2 + i]) for i, (a, b) in enumerate(pairs)]
 
     z, y = dp >> 1, dp & 1
-    vec_ids = [[(dp, blk ^ 1)], [(dp, blk ^ 2)], [(dp ^ 1, blk)]]
-    vec_ids.append([(((z + d) & 3) * 2 + y, blk) for d in (1, 2, 3)])
-
-    def vec_copies(stage):
+    z_ids = [(((z + d) & 3) * 2 + y, blk) for d in (1, 2, 3)]
+    vec_ids = [z_ids, [(dp ^ 1, blk)], [(dp, blk ^ 1), (dp, blk ^ 2), (dp, blk ^ 3)]]
+
+    def vec_copies(name, stage):
+        at = (0, 3, 4)[stage]
         return [
             pltpu.make_async_remote_copy(
-                src_ref=vec,
-                dst_ref=r["rvec"].at[stage + d],
-                send_sem=r["vsend"].at[stage + d],
-                recv_sem=r["vrecv"].at[stage + d],
+                src_ref=r[name],
+                dst_ref=r[name + "_r"].at[at + d],
+                send_sem=r[name + "_send"].at[at + d],
+                recv_sem=r[name + "_recv"].at[at + d],
                 device_id=where,
                 device_id_type=MESH,
             )
             for d, where in enumerate(vec_ids[stage])
         ]
 
-    def vec_start(stage):
-        for copy in vec_copies(stage):
-            copy.start()
-
-    def vec_end(stage):
-        copies = vec_copies(stage)
-        for copy in copies:
-            copy.wait()
-        for d in range(len(copies)):
-            vec[...] += r["rvec"][stage + d]
+    def vec_step(name, stage):
+        if stage > 0:
+            copies = vec_copies(name, stage - 1)
+            for copy in copies:
+                copy.wait()
+            at = (0, 3, 4)[stage - 1]
+            r[name][...] += sum(r[name + "_r"][at + d] for d in range(len(copies)))
+        if stage < 3:
+            for copy in vec_copies(name, stage):
+                copy.start()
 
     def input_piece(s, sums):
         sl = slice(s * tok, (s + 1) * tok)
-        e = dot(wcat[...], dcat[:, sl]).T
+        e = r["ebuf"][s & 1].T
         n, rstd = center(r["xbuf"][s].astype(F32))
         f = e * as_row(r["gain"])
         dx = r["dmbuf"][sl] + rstd * (
@@ -824,11 +890,15 @@
         )
         for load in loads():
             load.start()
-        vec[...] = r["vec_in"][...]
+        vec[...] = jnp.zeros_like(vec)
+        r["vb"][...] = r["vec_in"][...]
 
     def act(item):
         kind, what = item
-        getattr(jobs[kind], "stage%d" % what)()
+        if kind in ("va", "vb"):
+            vec_step(kind, what)
+        else:
+            getattr(jobs[kind], "stage%d" % what)()
 
     for at in range(H):
         if plan.get(at):
@@ -879,63 +949,65 @@
             load.wait()
         for item in plan["tail"]:
             kind, what = item
-            if kind == "piece":
+            if kind == "mul":
+                r["ebuf"][what & 1] = dot(wcat[...], dcat[:, what * tok : (what + 1) * tok])
+            elif kind == "piece":
                 sums = input_piece(what, sums)
                 if what == 0:
                     vec[0:1] = sums[0]
                     vec[1:2] = sums[1]
-            elif kind == "vec":
-                if what > 0:
-                    vec_end(what - 1)
-                if what < 4:
-                    vec_start(what)
             else:
                 act(item)
-        r["vec_out"][...] = vec[...]
+        r["va_out"][...] = vec[...]
+        r["vb_out"][...] = r["vb"][...]
         for s in range(n_blk):
             in_copy(s).wait()
 
 
 PLAN = {
-    0: [("wout", 0), ("wo", 0), ("a2", 0), ("b2", 0)],
-    1: [("wo", 1)],
-    2: [("a2", 1)],
-    3: [("b2", 1)],
-    5: [("q0", 1), ("wo", 2)],
-    8: [("a2", 2), ("q0", 2)],
+    0: [("wout", 0), ("a2", 0), ("b2", 0), ("wo", 0)],
+    2: [("a2", 1), ("b2", 1)],
+    3: [("wo", 1)],
+    5: [("q0", 1)],
+    7: [("a2", 2), ("b2", 2)],
     9: [("q1", 1)],
-    10: [("wout", 1)],
-    11: [("wo", 3)],
+    10: [("q0", 2), ("wo", 2)],
+    11: [("a2", 3), ("b2", 3), ("wout", 1)],
     "tail": [
+        ("mul", 3),
+        ("mul", 2),
         ("piece", 3),
-        ("b2", 2),
+        ("q2", 1),
+        ("mul", 1),
         ("piece", 2),
-        ("q2", 1),
+        ("mul", 0),
         ("piece", 1),
-        ("a2", 3),
+        ("piece", 0),
+        ("vb", 0),
+        ("va", 0),
+        ("q2", 2),
+        ("q1", 2),
+        ("wo", 3),
         ("q0", 3),
-        ("piece", 0),
-        ("vec", 0),
-        ("q1", 2),
+        ("vb", 1),
+        ("va", 1),
         ("wout", 2),
-        ("vec", 1),
-        ("b2", 3),
-        ("q2", 2),
-        ("vec", 2),
+        ("a2", 4),
+        ("vb", 2),
+        ("va", 2),
+        ("q1", 3),
+        ("b2", 4),
+        ("q2", 3),
+        ("vb", 3),
+        ("va", 3),
         ("wo", 4),
-        ("q1", 3),
-        ("vec", 3),
-        ("q2", 3),
-        ("a2", 4),
         ("q0", 4),
-        ("vec", 4),
-        ("b2", 4),
         ("q1", 4),
         ("q2", 4),
     ],
 }
 
-SCATTER_KEYS = ("r0", "t1", "r1", "t2", "r2", "t3", "r3", "f", "send", "recv", "keep", "load")
+SCATTER_KEYS = ("f2", "rx", "r0", "t1", "r1", "t2", "r2", "t3", "r3", "f", "send", "recv", "keep", "load")
 
 
 def body(
@@ -1040,7 +1112,7 @@
         share, share_f = width // n_dev, hidden // n_dev
         tile = hidden // 4
         once = lambda shape: pl.BlockSpec(shape, lambda i: (0,) * len(shape), pipeline_mode=pl.Buffered(1))
-        vec_rows = 16
+        vec_rows = 8
         ins = {
             "x": (xs.reshape(seq, width), once((seq, width))),
             "g": (gs.reshape(seq, width), once((seq, width))),
@@ -1083,8 +1155,8 @@
             "r1": pltpu.VMEM((2, 4, share_f, width), BF16),
             "csend": pltpu.SemaphoreType.DMA((4,)),
             "crecv": pltpu.SemaphoreType.DMA((4,)),
-            "ysend": pltpu.SemaphoreType.DMA,
-            "yrecv": pltpu.SemaphoreType.DMA,
+            "ysend": pltpu.SemaphoreType.DMA((4,)),
+            "yrecv": pltpu.SemaphoreType.DMA((4,)),
             "osend": pltpu.SemaphoreType.DMA((n_blk - 1,)),
             "orecv": pltpu.SemaphoreType.DMA((n_blk - 1,)),
             "lsem": pltpu.SemaphoreType.DMA((3,)),
@@ -1104,7 +1176,7 @@
         )(*[v[0] for v in ins.values()])
         ffn = dict(zip(outs, ffn))
         tasks = (
-            ("a2", "gwin", None, slice(0, hidden // 2), share, "y", "s_win", slice(0, hidden // 2)),
+            ("a2", "gwin", None, slice(0, hidden // 2), share, "x", "s_win", slice(0, hidden // 2)),
             ("b2", "gwin", None, slice(hidden // 2, hidden), share, "y", "s_win", slice(hidden // 2, hidden)),
             ("wo", "gwo", None, None, share, "x", "s_wo", None),
         ) + tuple(
@@ -1114,7 +1186,7 @@
                 i,
                 None,
                 share,
-                "xxy"[i],
+                ("y", "x", "late")[i],
                 ("s_wq", "s_wk", "s_wv"),
                 slice(i * cols, (i + 1) * cols),
             )
@@ -1151,21 +1223,27 @@
             "s_wo": (sds((share, width), F32), full((share, width))),
             "s_win": (sds((share, hidden), F32), full((share, hidden))),
             "s_wout": (sds((share_f, width), F32), full((share_f, width))),
-            "vec_out": (sds((vec_rows, width), F32), full((vec_rows, width))),
+            "va_out": (sds((8, width), F32), full((8, width))),
+            "vb_out": (sds((8, width), F32), full((8, width))),
         }
         scratch = {
             "ds": pltpu.VMEM((seq, seq), BF16),
             "dcat": pltpu.VMEM((3 * width, seq), BF16),
             "wcat": pltpu.VMEM((width, 3 * width), BF16),
             "gq": pltpu.VMEM((n_col, 2, 2, 2, 4 * share, 3 * cols), BF16),
-            "vec": pltpu.VMEM((vec_rows, width), F32),
-            "rvec": pltpu.VMEM((6, vec_rows, width), F32),
+            "va": pltpu.VMEM((8, width), F32),
+            "vb": pltpu.VMEM((8, width), F32),
+            "va_r": pltpu.VMEM((7, 8, width), F32),
+            "vb_r": pltpu.VMEM((7, 8, width), F32),
+            "ebuf": pltpu.VMEM((2, width, tok), F32),
             "xbuf": pltpu.VMEM((n_blk, tok, width), BF16),
             "dmbuf": pltpu.VMEM((seq, width), F32),
             "dx": pltpu.VMEM((n_blk, tok, width), BF16),
             "lsem": pltpu.SemaphoreType.DMA((7,)),
-            "vsend": pltpu.SemaphoreType.DMA((6,)),
-            "vrecv": pltpu.SemaphoreType.DMA((6,)),
+            "va_send": pltpu.SemaphoreType.DMA((7,)),
+            "va_recv": pltpu.SemaphoreType.DMA((7,)),
+            "vb_send": pltpu.SemaphoreType.DMA((7,)),
+            "vb_recv": pltpu.SemaphoreType.DMA((7,)),
             "w_keep": pltpu.VMEM((2, share_f, width), BF16),
             "w_rz": pltpu.VMEM((3, 2, share_f, width), BF16),
             "w_f": pltpu.VMEM((2, share_f, width), F32),
@@ -1176,8 +1254,8 @@
             "isend": pltpu.SemaphoreType.DMA((n_blk - 1,)),
             "irecv": pltpu.SemaphoreType.DMA((n_blk - 1,)),
         }
-        for name, source, _, _, task_share, _, _, _ in tasks:
-            for k, v in scatter_scratch(task_share, sizes.get(name, width), source != "gq").items():
+        for name, source, _, _, task_share, first, _, _ in tasks:
+            for k, v in scatter_scratch(task_share, sizes.get(name, width), source != "gq", first == "late").items():
                 scratch[name + "_" + k] = v
         names = tuple(ins) + tuple(outs) + tuple(scratch)
         got = pl.pallas_call(
@@ -1201,11 +1279,11 @@
         fin = pl.pallas_call(
             functools.partial(finish_kernel, len(big)),
             grid=(n_blk,),
-            in_specs=[part] * 2 + [full(v.shape) for v in big[2:]] + [full((vec_rows, width))],
+            in_specs=[part] * 2 + [full(v.shape) for v in big[2:]] + [full((8, width))] * 2,
             out_specs=[part] * 2 + [full(v.shape) for v in big[2:]] + [full((share,))] * 8 + [full((share_f,))],
             out_shape=flat + [sds((share,), F32)] * 8 + [sds((share_f,), F32)],
             name="finish",
-        )(*big, got["vec_out"])
+        )(*big, got["va_out"], got["vb_out"])
         output, input_grad, s_wq, s_wk, s_wv, s_wo, s_win, s_wout = fin[: len(big)]
         g1, b1, bq, bv, bo_sum, g2, b2, bout_sum, bin_sum = fin[len(big) :]
         return (

time: 209 us -> 184 us (0.88)
  Pallas kernels: 208 us -> 183 us
    pallas_call x1, Pallas kernels: 89 us -> 73.9 us  [body(): pl.pallas_call(functools.partial(back_kernel, scale, names, tasks, plan),...]
    pallas_call x1, Pallas kernels: 60.5 us -> 52 us  [body(): pl.pallas_call(functools.partial(ffn_host_kernel, names, n_blk), grid=(8,...]
where the time goes in v4:
time: 184 us
  Pallas kernels  183 us (99%)
    pallas_call x1, Pallas kernels, body(): pl.pallas_call(functools.partial(back_kernel, scale, names, tasks, plan),...  73.9 us
    pallas_call x1, Pallas kernels, body(): pl.pallas_call(functools.partial(ffn_host_kernel, names, n_blk), grid=(8,...  52 us
    pallas_call x1, Pallas kernels, body(): pl.pallas_call(functools.partial(attend_spread_kernel, n_blk), grid=(H,),...  26.4 us
    pallas_call x1, Pallas kernels, body(): pl.pallas_call(functools.partial(qkv_spread_kernel, scale * LOG2E, n_blk)...  25.8 us
    pallas_call x1, Pallas kernels, body(): pl.pallas_call(functools.partial(finish_kernel, len(big)), grid=(n_blk,),...  4.96 us

profile of v4, /device:TPU:0, one launch (start us, length us, event | category | flops | bytes accessed | tf_op | source)
XLA Modules:
  0.0 183.8 jit_solution(2724393257466536977)
XLA Ops:
  0.7 25.8 %qkv.1 = (bf16[4,256,768]{2,1,0:T(8,128)(2,1)}, bf16[768,1024]{1,0:T(8,128)(2,1)}, bf16[768,1024]{1,0:T(8,128)(2,1)}, bf16[768,1024]{1,0:T(8,128)(2,1)}, bf16[768,1024]{1,0:T(8,128)(2,1)}) custom-call(bf16[4,256,768]{2,1,0:T(8,128)(2,1)} %x_any.1, bf16[768]{0:T(1024)(128)(2,1)} %refs_7_.3, bf16[768]{0:T(1024)(128)(2,1)} %bias.1, bf16[768,768]{1,0:T(8,128)(2,1)} %refs_11_.3, ...), custom_call_target="tpu_custom_call" | custom-call | flops 3623878656 | bytes 11010048 | tf_op jit(solution)/shard_map/qkv/pallas_call | solution.py:1066
  26.4 26.4 %attend.1 = (bf16[768,1024]{1,0:T(8,128)(2,1)}, bf16[12,1024,1024]{2,1,0:T(8,128)(2,1)}, f32[12,1,1024]{2,1,0:T(1,128)}, bf16[4,256,768]{2,1,0:T(8,128)(2,1)}) custom-call(s32[4]{0:T(128)} %len_ref.1, bf16[768,1024]{1,0:T(8,128)(2,1)} %get-tuple-element.60.q_ref.refs_1_, bf16[768,1024]{1,0:T(8,128)(2,1)} %get-tuple-element.61.k_ref.refs_2_, ...), custom_call_target="tpu_custom_call" | custom-call | flops 12884901888 | bytes 25165824 | tf_op jit(solution)/shard_map/attend/pallas_call | solution.py:1090
  52.8 52.0 %ffn.1 = (bf16[4,256,768]{2,1,0:T(8,128)(2,1)}, f32[1024,768]{1,0:T(8,128)}, bf16[768,1024]{1,0:T(8,128)(2,1)}, bf16[2,2,2,96,3072]{4,3,2,1,0:T(8,128)(2,1)}, bf...) custom-call(bf16[1024,768]{1,0:T(8,128)(2,1)} %bitcast.2, ...), custom_call_target="tpu_custom_call" | custom-call | tf_op jit(solution)/shard_map/ffn/pallas_call | solution.py:1165
  104.8 73.9 %back.1 = (bf16[4,256,768]{2,1,0:T(8,128)(2,1)}, f32[24,768]{1,0:T(8,128)}, f32[24,768]{1,0:T(8,128)}, f32[24,768]{1,0:T(8,128)}, f32[24,768]{1,0:T(8,128)}, /*i...) custom-call(bf16[12,1024,1024]{2,1,0:T(8,128)(2,1)} %get-tuple-element.67.refs_0_, ...), custom_call_target="tpu_custom_call" | custom-call | tf_op jit(solution)/shard_map/back/pallas_call | solution.py:1261
  178.7 5.0 %finish.1 = (bf16[4,256,768]{2,1,0:T(8,128)(2,1)}, bf16[4,256,768]{2,1,0:T(8,128)(2,1)}, f32[24,768]{1,0:T(8,128)}, f32[24,768]{1,0:T(8,128)}, f32[24,768]{1,0:T...) custom-call(bf16[4,256,768]{2,1,0:T(8,128)(2,1)} %get-tuple-element., ...), custom_call_target="tpu_custom_call" | custom-call | tf_op jit(solution)/shard_map/finish/pallas_call | solution.py:1279

commit v5 on v4

--- a/solution.py
+++ b/solution.py
@@ -55,30 +55,57 @@
     return phi, u * e * INV_SQRT_2PI
 
 
-def attend_kernel(n_blk, len_ref, q_ref, k_ref, v_ref, c_ref, p_ref, il_ref):
+def attend_kernel(n_blk, len_ref, q_ref, k_ref, v_ref, c_ref, p_ref, il_ref, f_ref):
     seq = q_ref.shape[1]
     tok = seq // n_blk
     blk = lax.axis_index("blk")
     length = len_ref[blk]
-    s = dot(k_ref[...].T, q_ref[...])
     live = [(blk ^ i) * tok < length for i in range(n_blk)]
-    m = None
+    keys, q, v = k_ref[...].T, q_ref[...], v_ref[...]
+    m = jnp.full((1, seq), -1e30, F32)
+    total = summed = None
+    tops = []
+    ahead = dot(keys[:tok], q)
     for i in range(n_blk):
-        mi = jnp.max(s[i * tok : (i + 1) * tok], axis=0, keepdims=True)
-        mi = jnp.where(live[i], mi, -1e30)
-        m = mi if m is None else jnp.maximum(m, mi)
-    total = None
-    ps = []
+        s = ahead
+        if i + 1 < n_blk:
+            ahead = dot(keys[(i + 1) * tok : (i + 2) * tok], q)
+        new = jnp.maximum(m, jnp.where(live[i], jnp.max(s, axis=0, keepdims=True), -1e30))
+        p = jnp.exp2(s - jnp.where(live[i], new, 1e30))
+        part = jnp.sum(p, axis=0, keepdims=True)
+        p = p.astype(BF16)
+        p_ref[0, i * tok : (i + 1) * tok] = p
+        o = dot(v[:, i * tok : (i + 1) * tok], p)
+        if i == 0:
+            summed, total = o, part
+        else:
+            shrink = jnp.exp2(m - new)
+            summed, total = summed * shrink + o, total * shrink + part
+        m = new
+        tops.append(m)
+    inv = 1.0 / total
+    c_ref[...] = (summed * inv).astype(BF16)
+    il_ref[0] = inv
     for i in range(n_blk):
-        p = jnp.exp2(s[i * tok : (i + 1) * tok] - jnp.where(live[i], m, 1e30))
-        li = jnp.sum(p, axis=0, keepdims=True)
-        total = li if total is None else total + li
-        pb = p.astype(BF16)
-        p_ref[0, i * tok : (i + 1) * tok] = pb
-        ps.append(pb)
-    inv = 1.0 / total
-    c_ref[...] = (dot(v_ref[...], jnp.concatenate(ps, axis=0)) * inv).astype(BF16)
-    il_ref[0] = inv
+        f_ref[0, i : i + 1] = jnp.exp2(tops[i] - m)
+
+
+def attend_back_head(scale, n_blk, p_ref, q, k, v, do, ct, f_ref, ds, doi):
+    seq = q.shape[1]
+    tok = seq // n_blk
+    vh = v.T
+    do = do.astype(F32)
+    delta = jnp.sum(do * ct.astype(F32), axis=0, keepdims=True)
+    for i in range(n_blk):
+        sl = slice(i * tok, (i + 1) * tok)
+        f = f_ref[0, i : i + 1]
+        d = (do * f).astype(BF16)
+        doi[i] = d
+        ds[sl] = (p_ref[0, sl].astype(F32) * (dot(vh[sl], d) - delta * f)).astype(BF16)
+    dq = (dot(k, ds[...]) * scale).astype(BF16)
+    dv = [dot(p_ref[0, i * tok : (i + 1) * tok], doi[i], NT).T.astype(BF16) for i in range(n_blk)]
+    dk = (dot(ds[...], q, NT) * LN2).T.astype(BF16)
+    return dq, dk, jnp.concatenate(dv, axis=1)
 
 
 MESH = pl.DeviceIdType.MESH
@@ -180,7 +207,7 @@
         write.wait()
 
 
-def attend_spread_kernel(n_blk, len_ref, q_ref, k_ref, v_ref, g_any, c_ref, p_ref, il_ref, gs_any, send, recv, osem):
+def attend_spread_kernel(n_blk, len_ref, q_ref, k_ref, v_ref, g_any, c_ref, p_ref, il_ref, f_ref, gs_any, send, recv, osem):
     h = pl.program_id(0)
     dp = lax.axis_index("dp")
     blk = lax.axis_index("blk")
@@ -204,7 +231,7 @@
         for s in range(1, n_blk):
             copy(s).start()
 
-    attend_kernel(n_blk, len_ref, q_ref, k_ref, v_ref, c_ref, p_ref, il_ref)
+    attend_kernel(n_blk, len_ref, q_ref, k_ref, v_ref, c_ref, p_ref, il_ref, f_ref)
 
     @pl.when(h == pl.num_programs(0) - 1)
     def _():
@@ -273,6 +300,11 @@
     def pick(self, ref, a, b, rows):
         return (ref[a, b, rows] if self.first == "x" else ref[b, a, rows]).astype(F32)
 
+    def two(self, a, b, rows):
+        own = self.b["keep"] if "keep" in self.b else self.source.at[self.c]
+        a, b = (a, b) if self.first == "x" else (b, a)
+        return own[a, b, rows] + self.b["r0"][a, b, rows]
+
     def base(self, a, b, rows):
         if "keep" in self.b:
             own = self.pick(self.b["keep"], a, b, rows)
@@ -303,7 +335,7 @@
         for b in range(2):
 
             def fn(i, rows):
-                self.b["t1"][b, rows] = self.base(1 - self.mp, b, rows).astype(BF16)
+                self.b["t1"][b, rows] = self.two(1 - self.mp, b, rows)
 
             self.each(fn)
         self.p_copy().start()
@@ -488,20 +520,12 @@
         gwo_ref[...] = dot(ct_ref[...], n2[...]).astype(BF16)
 
 
-def attend_back_kernel(scale, p_ref, q_ref, k_ref, v_ref, do_ref, c_ref, dq_ref, dk_ref, dv_ref, ds):
-    seq = q_ref.shape[1]
-    do = do_ref[...]
-    vh = v_ref[...].T
-    delta = jnp.sum(do.astype(F32) * c_ref[...].astype(F32), axis=0, keepdims=True)
-    step = seq // 2
-    for c in range(2):
-        sl = slice(c * step, (c + 1) * step)
-        dp = dot(vh, do[:, sl])
-        d = (p_ref[0, :, sl].astype(F32) * (dp - delta[:, sl])).astype(BF16)
-        ds[:, sl] = d
-        dq_ref[:, sl] = (dot(k_ref[...], d) * scale).astype(BF16)
-    dv_ref[...] = dot(p_ref[0], do, NT).T.astype(BF16)
-    dk_ref[...] = (dot(ds[...], q_ref[...], NT) * LN2).T.astype(BF16)
+def attend_back_kernel(
+    scale, n_blk, p_ref, q_ref, k_ref, v_ref, do_ref, c_ref, f_ref, dq_ref, dk_ref, dv_ref, ds, doi
+):
+    dq_ref[...], dk_ref[...], dv_ref[...] = attend_back_head(
+        scale, n_blk, p_ref, q_ref[...], k_ref[...], v_ref[...], do_ref[...], c_ref[...], f_ref, ds, doi
+    )
 
 
 def input_kernel(n_blk, x_ref, dmid_ref, gain_ref, dq_ref, dk_ref, dv_ref, wq_ref, wk_ref, wv_ref, *rest):
@@ -576,7 +600,7 @@
     def y_start(plane):
         core_copy(plane).wait()
         for x in range(2):
-            t1[x, plane] = (gw[core, x, 1 - y, plane].astype(F32) + r0[x, 1 - y, plane].astype(F32)).astype(BF16)
+            t1[x, plane] = gw[core, x, 1 - y, plane] + r0[x, 1 - y, plane]
         y_copy(plane).start()
 
     def out_copy(s):
@@ -609,8 +633,11 @@
 
     @pl.when(i < 4)
     def _():
-        for sl in rows:
-            pre = dot(n2[sl], win[...]) + r["bins"][j]
+        ahead = dot(n2[rows[0]], win[...])
+        for s, sl in enumerate(rows):
+            pre = ahead + r["bins"][j]
+            if s + 1 < n_blk:
+                ahead = dot(n2[rows[s + 1]], win[...])
             phi, slope = gate(pre)
             a = (pre * phi).astype(BF16)
             act[sl] = a
@@ -637,8 +664,11 @@
     @pl.when(i >= 4)
     def _():
         total = None
-        for sl in rows:
-            d = (dot(g[sl], wout[...], NT) * gp[j, sl].astype(F32)).astype(BF16)
+        ahead = dot(g[rows[0]], wout[...], NT)
+        for s, sl in enumerate(rows):
+            d = (ahead * gp[j, sl].astype(F32)).astype(BF16)
+            if s + 1 < n_blk:
+                ahead = dot(g[rows[s + 1]], wout[...], NT)
             act[sl] = d
             col = jnp.sum(d.astype(F32), axis=0, keepdims=True)
             total = col if total is None else total + col
@@ -910,19 +940,23 @@
 
     @pl.when(h < H)
     def _():
-        do = r["do"][...]
-        vh = r["v"][...].T
-        delta = jnp.sum(do.astype(F32) * r["ct"][...].astype(F32), axis=0, keepdims=True)
-        step = seq // 2
         base = pl.multiple_of(h * head, head)
-        for c in range(2):
-            sl = slice(c * step, (c + 1) * step)
-            dpr = dot(vh, do[:, sl])
-            d = (r["p"][0, :, sl].astype(F32) * (dpr - delta[:, sl])).astype(BF16)
-            r["ds"][:, sl] = d
-            dcat[pl.ds(base, head), sl] = (dot(r["k"][...], d) * scale).astype(BF16)
-        dcat[pl.ds(base + 2 * width, head)] = dot(r["p"][0], do, NT).T.astype(BF16)
-        dcat[pl.ds(base + width, head)] = (dot(r["ds"][...], r["q"][...], NT) * LN2).T.astype(BF16)
+        dq, dk, dv = attend_back_head(
+            scale,
+            n_blk,
+            r["p"],
+            r["q"][...],
+            r["k"][...],
+            r["v"][...],
+            r["do"][...],
+            r["ct"][...],
+            r["tops"],
+            r["ds"],
+            r["doi"],
+        )
+        dcat[pl.ds(base, head)] = dq
+        dcat[pl.ds(base + width, head)] = dk
+        dcat[pl.ds(base + 2 * width, head)] = dv
 
     n_group = gq.shape[0]
     cols = width // n_group
@@ -1087,15 +1121,17 @@
 
     per_head = pl.BlockSpec((head, seq), lambda h: (h, 0))
     per_square = pl.BlockSpec((1, seq, seq), lambda h: (h, 0, 0))
-    ct, probs, inv_total, gs = pl.pallas_call(
+    per_block = pl.BlockSpec((1, n_blk, seq), lambda h: (h, 0, 0))
+    ct, probs, inv_total, tops, gs = pl.pallas_call(
         functools.partial(attend_spread_kernel, n_blk),
         grid=(H,),
         in_specs=[pl.BlockSpec(memory_space=pltpu.SMEM), per_head, per_head, per_head, anywhere],
-        out_specs=[per_head, per_square, pl.BlockSpec((1, 1, seq), lambda h: (h, 0, 0)), anywhere],
+        out_specs=[per_head, per_square, pl.BlockSpec((1, 1, seq), lambda h: (h, 0, 0)), per_block, anywhere],
         out_shape=[
             sds((width, seq), BF16),
             sds((H, seq, seq), BF16),
             sds((H, 1, seq), F32),
+            sds((H, n_blk, seq), F32),
             sds((n_blk, tok, width), BF16),
         ],
         scratch_shapes=[
@@ -1203,6 +1239,7 @@
             "v": (vt, strip_h),
             "do": (ffn["dot"], strip_h),
             "ct": (ct, strip_h),
+            "tops": (tops, last((1, n_blk, seq))),
             "nt": (nt, wide),
             "gain": (ln1_gain, full((width,))),
             "vec_in": (ffn["vec"], full((vec_rows, width))),
@@ -1228,6 +1265,7 @@
         }
         scratch = {
             "ds": pltpu.VMEM((seq, seq), BF16),
+            "doi": pltpu.VMEM((n_blk, head, seq), BF16),
             "dcat": pltpu.VMEM((3 * width, seq), BF16),
             "wcat": pltpu.VMEM((width, 3 * width), BF16),
             "gq": pltpu.VMEM((n_col, 2, 2, 2, 4 * share, 3 * cols), BF16),
@@ -1404,16 +1442,16 @@
     output = collect(out_pieces)
 
     dqt, dkt, dvt = pl.pallas_call(
-        functools.partial(attend_back_kernel, scale),
+        functools.partial(attend_back_kernel, scale, n_blk),
         grid=(H,),
-        in_specs=[per_square] + [per_head] * 5,
+        in_specs=[per_square] + [per_head] * 5 + [per_block],
         out_specs=[per_head] * 3,
         out_shape=[sds((width, seq), BF16)] * 3,
-        scratch_shapes=[pltpu.VMEM((seq, seq), BF16)],
+        scratch_shapes=[pltpu.VMEM((seq, seq), BF16), pltpu.VMEM((n_blk, head, seq), BF16)],
         compiler_params=params(),
         cost_estimate=cost(10 * seq * seq * width, 2 * H * seq * seq),
         name="attend_back",
-    )(probs, qt, kt, vt, dct, ct)
+    )(probs, qt, kt, vt, dct, ct, tops)
 
     result = pl.pallas_call(
         functools.partial(input_kernel, n_blk),

time: 184 us -> 181 us (0.984)
  Pallas kernels: 183 us -> 180 us
    pallas_call x1, Pallas kernels: 26.4 us -> 24 us  [body(): pl.pallas_call(functools.partial(attend_spread_kernel, n_blk), grid=(H,),...]
where the time goes in v5:
time: 181 us
  Pallas kernels  180 us (99%)
    pallas_call x1, Pallas kernels, body(): pl.pallas_call(functools.partial(back_kernel, scale, names, tasks, plan),...  73.9 us
    pallas_call x1, Pallas kernels, body(): pl.pallas_call(functools.partial(ffn_host_kernel, names, n_blk), grid=(8,...  51.3 us
    pallas_call x1, Pallas kernels, body(): pl.pallas_call(functools.partial(qkv_spread_kernel, scale * LOG2E, n_blk)...  25.8 us
    pallas_call x1, Pallas kernels, body(): pl.pallas_call(functools.partial(attend_spread_kernel, n_blk), grid=(H,),...  24 us
    pallas_call x1, Pallas kernels, body(): pl.pallas_call(functools.partial(finish_kernel, len(big)), grid=(n_blk,),...  4.96 us

profile of v5, /device:TPU:0, one launch (start us, length us, event | category | flops | bytes accessed | tf_op | source)
XLA Modules:
  0.0 180.8 jit_solution(11766103829985810514)
XLA Ops:
  0.7 25.8 %qkv.1 = (bf16[4,256,768]{2,1,0:T(8,128)(2,1)}, bf16[768,1024]{1,0:T(8,128)(2,1)}, bf16[768,1024]{1,0:T(8,128)(2,1)}, bf16[768,1024]{1,0:T(8,128)(2,1)}, bf16[768,1024]{1,0:T(8,128)(2,1)}) custom-call(bf16[4,256,768]{2,1,0:T(8,128)(2,1)} %x_any.1, bf16[768]{0:T(1024)(128)(2,1)} %refs_8_.3, bf16[768]{0:T(1024)(128)(2,1)} %bias.1, bf16[768,768]{1,0:T(8,128)(2,1)} %refs_12_.1, ...), custom_call_target="tpu_custom_call" | custom-call | flops 3623878656 | bytes 11010048 | tf_op jit(solution)/shard_map/qkv/pallas_call | solution.py:1100
  26.4 24.0 %attend.1 = (bf16[768,1024]{1,0:T(8,128)(2,1)}, bf16[12,1024,1024]{2,1,0:T(8,128)(2,1)}, f32[12,1,1024]{2,1,0:T(1,128)}, f32[12,4,1024]{2,1,0:T(4,128)}, bf16[4,256,768]{2,1,0:T(8,128)(2,1)}) custom-call(s32[4]{0:T(128)} %len_ref.1, bf16[768,1024]{1,0:T(8,128)(2,1)} %get-tuple-element.61.q_ref.refs_1_, bf16[768,1024]{1,0:T(8,128)(2,1)} %get-tuple-element.62.k_ref.refs_2_, ...), custom_call_target="tpu_custom_call" | custom-call | flops 12884901888 | bytes 25165824 | tf_op jit(solution)/shard_map/attend/pallas_call | solution.py:1125
  50.5 51.3 %ffn.1 = (bf16[4,256,768]{2,1,0:T(8,128)(2,1)}, f32[1024,768]{1,0:T(8,128)}, bf16[768,1024]{1,0:T(8,128)(2,1)}, bf16[2,2,2,96,3072]{4,3,2,1,0:T(8,128)(2,1)}, bf...) custom-call(bf16[1024,768]{1,0:T(8,128)(2,1)} %bitcast.2, ...), custom_call_target="tpu_custom_call" | custom-call | tf_op jit(solution)/shard_map/ffn/pallas_call | solution.py:1201
  101.8 73.9 %back.1 = (bf16[4,256,768]{2,1,0:T(8,128)(2,1)}, f32[24,768]{1,0:T(8,128)}, f32[24,768]{1,0:T(8,128)}, f32[24,768]{1,0:T(8,128)}, f32[24,768]{1,0:T(8,128)}, /*i...) custom-call(bf16[12,1024,1024]{2,1,0:T(8,128)(2,1)} %get-tuple-element.68.refs_0_, ...), custom_call_target="tpu_custom_call" | custom-call | tf_op jit(solution)/shard_map/back/pallas_call | solution.py:1299
  175.7 5.0 %finish.1 = (bf16[4,256,768]{2,1,0:T(8,128)(2,1)}, bf16[4,256,768]{2,1,0:T(8,128)(2,1)}, f32[24,768]{1,0:T(8,128)}, f32[24,768]{1,0:T(8,128)}, f32[24,768]{1,0:T...) custom-call(bf16[4,256,768]{2,1,0:T(8,128)(2,1)} %get-tuple-element., ...), custom_call_target="tpu_custom_call" | custom-call | tf_op jit(solution)/shard_map/finish/pallas_call | solution.py:1317

commit v6 on v5

--- a/solution.py
+++ b/solution.py
@@ -570,7 +570,8 @@
     mid, acc, n2, n2t, act, gp, gw, r0, t1, r1 = [
         r[k] for k in ("mid", "acc", "n2", "n2t", "act", "gp", "gw", "r0", "t1", "r1")
     ]
-    g, win, wout, ct = r["g"], r["win"], r["wout"], r["ct"]
+    g, win, wout, ct = r["gbuf"], r["win"], r["wout"], r["ct"]
+    g_load = pltpu.make_async_copy(r["g"], g, r["lsem"].at[3])
     seq, width = mid.shape
     tok = seq // n_blk
     tile = act.shape[1]
@@ -618,6 +619,7 @@
 
     @pl.when(i == 0)
     def _():
+        g_load.start()
         greet([(dp, blk ^ 1), (dp, blk ^ 2), (dp, blk ^ 3), (dp ^ 1, blk)])
         bins = as_row(r["bin"])
         for k in range(4):
@@ -647,6 +649,10 @@
         @pl.when(i > 0)
         def _():
             y_start(j - 1)
+
+        @pl.when(i == 0)
+        def _():
+            g_load.wait()
 
         v = dot(act[...], g[...], TN)
         for c, x, yy in CXY:
@@ -865,6 +871,9 @@
             return pltpu.make_async_copy(r["dx"].at[0], r["input_grad"].at[blk], r["lsem"].at[1])
         return spread(r["dx"], r["input_grad"], (r["isend"], r["irecv"]), s)
 
+    def nt_load():
+        return pltpu.make_async_copy(r["nt"], r["ntbuf"], r["lsem"].at[7])
+
     def loads():
         pairs = [(r["xs"], r["xbuf"]), (r["dmid"], r["dmbuf"])]
         pairs += [(r[w], wcat.at[:, i * width : (i + 1) * width]) for i, w in enumerate(("wq", "wk", "wv"))]
@@ -918,6 +927,7 @@
             [(dp, blk ^ 1), (dp, blk ^ 2), (dp, blk ^ 3), (dp ^ 1, blk)]
             + [(((z + d) & 3) * 2 + y, blk) for d in (1, 2, 3)]
         )
+        nt_load().start()
         for load in loads():
             load.start()
         vec[...] = jnp.zeros_like(vec)
@@ -964,7 +974,9 @@
 
         @pl.when(h == (gi + 1) * (H // n_group) - 1)
         def _(gi=gi):
-            nt = r["nt"][...]
+            if gi == 0:
+                nt_load().wait()
+            nt = r["ntbuf"][...]
             ones = jnp.ones((8, seq), BF16)
             for t in range(3):
                 part = dcat[t * width + gi * cols : t * width + (gi + 1) * cols]
@@ -1151,7 +1163,7 @@
         vec_rows = 8
         ins = {
             "x": (xs.reshape(seq, width), once((seq, width))),
-            "g": (gs.reshape(seq, width), once((seq, width))),
+            "g": (gs.reshape(seq, width), anywhere),
             "ct": (ct, once((width, seq))),
             "il": (inv_total, once((H, 1, seq))),
             "wo": (w_output, once((width, width))),
@@ -1176,6 +1188,7 @@
             "vec": (sds((vec_rows, width), F32), once((vec_rows, width))),
         }
         scratch = {
+            "gbuf": pltpu.VMEM((seq, width), BF16),
             "mid": pltpu.VMEM((seq, width), F32),
             "acc": pltpu.VMEM((seq, width), F32),
             "n2": pltpu.VMEM((seq, width), BF16),
@@ -1195,7 +1208,7 @@
             "yrecv": pltpu.SemaphoreType.DMA((4,)),
             "osend": pltpu.SemaphoreType.DMA((n_blk - 1,)),
             "orecv": pltpu.SemaphoreType.DMA((n_blk - 1,)),
-            "lsem": pltpu.SemaphoreType.DMA((3,)),
+            "lsem": pltpu.SemaphoreType.DMA((4,)),
         }
         names = tuple(ins) + tuple(outs) + tuple(scratch)
         ffn = pl.pallas_call(
@@ -1240,7 +1253,7 @@
             "do": (ffn["dot"], strip_h),
             "ct": (ct, strip_h),
             "tops": (tops, last((1, n_blk, seq))),
-            "nt": (nt, wide),
+            "nt": (nt, anywhere),
             "gain": (ln1_gain, full((width,))),
             "vec_in": (ffn["vec"], full((vec_rows, width))),
             "xs": (xs, anywhere),
@@ -1274,10 +1287,11 @@
             "va_r": pltpu.VMEM((7, 8, width), F32),
             "vb_r": pltpu.VMEM((7, 8, width), F32),
             "ebuf": pltpu.VMEM((2, width, tok), F32),
+            "ntbuf": pltpu.VMEM((width, seq), BF16),
             "xbuf": pltpu.VMEM((n_blk, tok, width), BF16),
             "dmbuf": pltpu.VMEM((seq, width), F32),
             "dx": pltpu.VMEM((n_blk, tok, width), BF16),
-            "lsem": pltpu.SemaphoreType.DMA((7,)),
+            "lsem": pltpu.SemaphoreType.DMA((8,)),
             "va_send": pltpu.SemaphoreType.DMA((7,)),
             "va_recv": pltpu.SemaphoreType.DMA((7,)),
             "vb_send": pltpu.SemaphoreType.DMA((7,)),
@@ -1312,11 +1326,11 @@
         big = [ffn["output"], got["input_grad"]] + [
             got[k] for k in ("s_wq", "s_wk", "s_wv", "s_wo", "s_win", "s_wout")
         ]
-        part = pl.BlockSpec((1, tok, width), lambda i: (i, 0, 0))
+        part = pl.BlockSpec((n_blk // 2, tok, width), lambda i: (i, 0, 0))
         flat = [sds(v.shape, v.dtype) for v in big]
         fin = pl.pallas_call(
             functools.partial(finish_kernel, len(big)),
-            grid=(n_blk,),
+            grid=(2,),
             in_specs=[part] * 2 + [full(v.shape) for v in big[2:]] + [full((8, width))] * 2,
             out_specs=[part] * 2 + [full(v.shape) for v in big[2:]] + [full((share,))] * 8 + [full((share_f,))],
             out_shape=flat + [sds((share,), F32)] * 8 + [sds((share_f,), F32)],

time: 181 us -> 179 us (0.989)
  Pallas kernels: 180 us -> 178 us
where the time goes in v6:
time: 179 us
  Pallas kernels  178 us (99%)
    pallas_call x1, Pallas kernels, body(): pl.pallas_call(functools.partial(back_kernel, scale, names, tasks, plan),...  73.6 us
    pallas_call x1, Pallas kernels, body(): pl.pallas_call(functools.partial(ffn_host_kernel, names, n_blk), grid=(8,...  50.8 us
    pallas_call x1, Pallas kernels, body(): pl.pallas_call(functools.partial(qkv_spread_kernel, scale * LOG2E, n_blk)...  25.8 us
    pallas_call x1, Pallas kernels, body(): pl.pallas_call(functools.partial(attend_spread_kernel, n_blk), grid=(H,),...  24 us
    pallas_call x1, Pallas kernels, body(): pl.pallas_call(functools.partial(finish_kernel, len(big)), grid=(2,), in_...  3.91 us

profile of v6, /device:TPU:0, one launch (start us, length us, event | category | flops | bytes accessed | tf_op | source)
XLA Modules:
  0.0 179.0 jit_solution(13870006138471732213)
XLA Ops:
  0.7 25.8 %qkv.1 = (bf16[4,256,768]{2,1,0:T(8,128)(2,1)}, bf16[768,1024]{1,0:T(8,128)(2,1)}, bf16[768,1024]{1,0:T(8,128)(2,1)}, bf16[768,1024]{1,0:T(8,128)(2,1)}, bf16[768,1024]{1,0:T(8,128)(2,1)}) custom-call(bf16[4,256,768]{2,1,0:T(8,128)(2,1)} %x_any.1, bf16[768]{0:T(1024)(128)(2,1)} %refs_8_.3, bf16[768]{0:T(1024)(128)(2,1)} %bias.1, bf16[768,768]{1,0:T(8,128)(2,1)} %refs_12_.1, ...), custom_call_target="tpu_custom_call" | custom-call | flops 3623878656 | bytes 11010048 | tf_op jit(solution)/shard_map/qkv/pallas_call | solution.py:1112
  26.4 24.0 %attend.1 = (bf16[768,1024]{1,0:T(8,128)(2,1)}, bf16[12,1024,1024]{2,1,0:T(8,128)(2,1)}, f32[12,1,1024]{2,1,0:T(1,128)}, f32[12,4,1024]{2,1,0:T(4,128)}, bf16[4,256,768]{2,1,0:T(8,128)(2,1)}) custom-call(s32[4]{0:T(128)} %len_ref.1, bf16[768,1024]{1,0:T(8,128)(2,1)} %get-tuple-element.61.q_ref.refs_1_, bf16[768,1024]{1,0:T(8,128)(2,1)} %get-tuple-element.62.k_ref.refs_2_, ...), custom_call_target="tpu_custom_call" | custom-call | flops 12884901888 | bytes 25165824 | tf_op jit(solution)/shard_map/attend/pallas_call | solution.py:1137
  50.5 50.8 %ffn.1 = (bf16[4,256,768]{2,1,0:T(8,128)(2,1)}, f32[1024,768]{1,0:T(8,128)}, bf16[768,1024]{1,0:T(8,128)(2,1)}, bf16[2,2,2,96,3072]{4,3,2,1,0:T(8,128)(2,1)}, bf...) custom-call(bf16[1024,768]{1,0:T(8,128)(2,1)} %bitcast.2, ...), custom_call_target="tpu_custom_call" | custom-call | tf_op jit(solution)/shard_map/ffn/pallas_call | solution.py:1214
  101.3 73.6 %back.1 = (bf16[4,256,768]{2,1,0:T(8,128)(2,1)}, f32[24,768]{1,0:T(8,128)}, f32[24,768]{1,0:T(8,128)}, f32[24,768]{1,0:T(8,128)}, f32[24,768]{1,0:T(8,128)}, /*i...) custom-call(bf16[12,1024,1024]{2,1,0:T(8,128)(2,1)} %get-tuple-element.68.refs_0_, ...), custom_call_target="tpu_custom_call" | custom-call | tf_op jit(solution)/shard_map/back/pallas_call | solution.py:1313
  175.0 3.9 %finish.1 = (bf16[4,256,768]{2,1,0:T(8,128)(2,1)}, bf16[4,256,768]{2,1,0:T(8,128)(2,1)}, f32[24,768]{1,0:T(8,128)}, f32[24,768]{1,0:T(8,128)}, f32[24,768]{1,0:T...) custom-call(bf16[4,256,768]{2,1,0:T(8,128)(2,1)} %get-tuple-element., ...), custom_call_target="tpu_custom_call" | custom-call | tf_op jit(solution)/shard_map/finish/pallas_call | solution.py:1331

commit v7 on v6

--- a/solution.py
+++ b/solution.py
@@ -231,7 +231,21 @@
         for s in range(1, n_blk):
             copy(s).start()
 
-    attend_kernel(n_blk, len_ref, q_ref, k_ref, v_ref, c_ref, p_ref, il_ref, f_ref)
+    pack = p_ref.shape[0]
+    head = q_ref.shape[0] // pack
+    for g in range(pack):
+        rows, one = slice(g * head, (g + 1) * head), slice(g, g + 1)
+        attend_kernel(
+            n_blk,
+            len_ref,
+            q_ref.at[rows],
+            k_ref.at[rows],
+            v_ref.at[rows],
+            c_ref.at[rows],
+            p_ref.at[one],
+            il_ref.at[one],
+            f_ref.at[one],
+        )
 
     @pl.when(h == pl.num_programs(0) - 1)
     def _():
@@ -1134,11 +1148,14 @@
     per_head = pl.BlockSpec((head, seq), lambda h: (h, 0))
     per_square = pl.BlockSpec((1, seq, seq), lambda h: (h, 0, 0))
     per_block = pl.BlockSpec((1, n_blk, seq), lambda h: (h, 0, 0))
+    pack = 2
+    heads = lambda *shape: pl.BlockSpec(shape, lambda h: (h,) + (0,) * (len(shape) - 1))
+    strips = heads(pack * head, seq)
     ct, probs, inv_total, tops, gs = pl.pallas_call(
         functools.partial(attend_spread_kernel, n_blk),
-        grid=(H,),
-        in_specs=[pl.BlockSpec(memory_space=pltpu.SMEM), per_head, per_head, per_head, anywhere],
-        out_specs=[per_head, per_square, pl.BlockSpec((1, 1, seq), lambda h: (h, 0, 0)), per_block, anywhere],
+        grid=(H // pack,),
+        in_specs=[pl.BlockSpec(memory_space=pltpu.SMEM), strips, strips, strips, anywhere],
+        out_specs=[strips, heads(pack, seq, seq), heads(pack, 1, seq), heads(pack, n_blk, seq), anywhere],
         out_shape=[
             sds((width, seq), BF16),
             sds((H, seq, seq), BF16),

time: 179 us -> 179 us (level)
  no operation moved by 1% of the time
where the time goes in v7:
time: 179 us
  Pallas kernels  178 us (99%)
    pallas_call x1, Pallas kernels, body(): pl.pallas_call(functools.partial(back_kernel, scale, names, tasks, plan),...  73.8 us
    pallas_call x1, Pallas kernels, body(): pl.pallas_call(functools.partial(ffn_host_kernel, names, n_blk), grid=(8,...  50.8 us
    pallas_call x1, Pallas kernels, body(): pl.pallas_call(functools.partial(qkv_spread_kernel, scale * LOG2E, n_blk)...  25.8 us
    pallas_call x1, Pallas kernels, body(): pl.pallas_call(functools.partial(attend_spread_kernel, n_blk), grid=(H //...  23.5 us
    pallas_call x1, Pallas kernels, body(): pl.pallas_call(functools.partial(finish_kernel, len(big)), grid=(2,), in_...  3.91 us

profile of v7, /device:TPU:0, one launch (start us, length us, event | category | flops | bytes accessed | tf_op | source)
XLA Modules:
  0.0 178.7 jit_solution(16357230192788523946)
XLA Ops:
  0.7 25.8 %qkv.1 = (bf16[4,256,768]{2,1,0:T(8,128)(2,1)}, bf16[768,1024]{1,0:T(8,128)(2,1)}, bf16[768,1024]{1,0:T(8,128)(2,1)}, bf16[768,1024]{1,0:T(8,128)(2,1)}, bf16[768,1024]{1,0:T(8,128)(2,1)}) custom-call(bf16[4,256,768]{2,1,0:T(8,128)(2,1)} %x_any.1, bf16[768]{0:T(1024)(128)(2,1)} %refs_8_.3, bf16[768]{0:T(1024)(128)(2,1)} %bias.1, bf16[768,768]{1,0:T(8,128)(2,1)} %refs_12_.1, ...), custom_call_target="tpu_custom_call" | custom-call | flops 3623878656 | bytes 11010048 | tf_op jit(solution)/shard_map/qkv/pallas_call | solution.py:1126
  26.4 23.5 %attend.1 = (bf16[768,1024]{1,0:T(8,128)(2,1)}, bf16[12,1024,1024]{2,1,0:T(8,128)(2,1)}, f32[12,1,1024]{2,1,0:T(1,128)}, f32[12,4,1024]{2,1,0:T(4,128)}, bf16[4,256,768]{2,1,0:T(8,128)(2,1)}) custom-call(s32[4]{0:T(128)} %len_ref.1, bf16[768,1024]{1,0:T(8,128)(2,1)} %get-tuple-element.61.q_ref.refs_1_, bf16[768,1024]{1,0:T(8,128)(2,1)} %get-tuple-element.62.k_ref.refs_2_, ...), custom_call_target="tpu_custom_call" | custom-call | flops 12884901888 | bytes 25165824 | tf_op jit(solution)/shard_map/attend/pallas_call | solution.py:1154
  49.9 50.8 %ffn.1 = (bf16[4,256,768]{2,1,0:T(8,128)(2,1)}, f32[1024,768]{1,0:T(8,128)}, bf16[768,1024]{1,0:T(8,128)(2,1)}, bf16[2,2,2,96,3072]{4,3,2,1,0:T(8,128)(2,1)}, bf...) custom-call(bf16[1024,768]{1,0:T(8,128)(2,1)} %bitcast.2, ...), custom_call_target="tpu_custom_call" | custom-call | tf_op jit(solution)/shard_map/ffn/pallas_call | solution.py:1231
  100.8 73.8 %back.1 = (bf16[4,256,768]{2,1,0:T(8,128)(2,1)}, f32[24,768]{1,0:T(8,128)}, f32[24,768]{1,0:T(8,128)}, f32[24,768]{1,0:T(8,128)}, f32[24,768]{1,0:T(8,128)}, /*i...) custom-call(bf16[12,1024,1024]{2,1,0:T(8,128)(2,1)} %get-tuple-element.68.refs_0_, ...), custom_call_target="tpu_custom_call" | custom-call | tf_op jit(solution)/shard_map/back/pallas_call | solution.py:1330
  174.6 3.9 %finish.1 = (bf16[4,256,768]{2,1,0:T(8,128)(2,1)}, bf16[4,256,768]{2,1,0:T(8,128)(2,1)}, f32[24,768]{1,0:T(8,128)}, f32[24,768]{1,0:T(8,128)}, f32[24,768]{1,0:T...) custom-call(bf16[4,256,768]{2,1,0:T(8,128)(2,1)} %get-tuple-element., ...), custom_call_target="tpu_custom_call" | custom-call | tf_op jit(solution)/shard_map/finish/pallas_call | solution.py:1348
